TPU v7x, 128 devices: a whole 4x4x4 slice. The times are simulated.
128 devices in a mesh: lon: 8 (over z, core), lat: 16 (over x, y).
Axes of the slice: x: 4, y: 4, z: 4, core: 2. Of those that a mesh axis runs over, the one named last changes fastest.
Arguments:
- obs_rows: bfloat16 [2048, 128, 256], P(('lon', 'lat')), may hold values from -3 to 3
- innovations: bfloat16 [2048, 128], P(('lon', 'lat')), may hold values from -12 to 12
- obs_home: int32 [2048], replicated, may hold values from 0 to 2047, as said below
- obs_lists: int32 [16, 32, 48], P('lon', 'lat'), may hold values from -1 to 2047, as said below
- loc_weights: float32 [16, 32, 48], P('lon', 'lat'), may hold values from 0.05 to 1
- state_mean: float32 [32, 64, 512], P('lon', 'lat'), may hold values from -6 to 6
- state_perturb: bfloat16 [32, 64, 512, 256], P('lon', 'lat'), may hold values from -6 to 6
- interp_ids: int32 [32, 64, 4], P('lon', 'lat'), may hold values from 0 to 511, as said below
- interp_wts: float32 [32, 64, 4], P('lon', 'lat'), as said below
Outputs:
- analysis: bfloat16 [32, 64, 512, 256], P('lon', 'lat')
Inputs may be any that keep to these rules, and one draw needn't show every extreme that they name: `obs_lists`: each entry is a block id or -1 (padding); in every list the ids come first, 12 or more of them, and ids may repeat. Block b lies in row obs_home[b] of obs_rows. Over the lists of one device's 2 x 2 analysis points, at most 2 entries (repeats counted) name blocks whose rows lie on one device; in every draw some device is named 2 times by the lists of every device. `obs_home`: A permutation of the rows of obs_rows. `interp_ids`: four distinct analysis points, each on the tile's device or at most one analysis point beyond that device's block of points along either dimension. `interp_wts`: Positive; the four weights of a tile sum to one.
All inputs are finite; a program needn't handle non-finite values. Where the computation divides by a largest or mean magnitude, that divisor is 1e-20 or more.
Results may differ from a plain program's by a relative error of at most 0.0042.
Values may be sent and summed in bfloat16 or wider, within the bound.
No kernel may reach another device: no remote copies, remote signals or barrier semaphores. Data moves between devices by JAX's collectives and lax.ppermute only.
A program may use at most 192 MiB of HBM per device.

v0:
```python
import jax
import jax.numpy as jnp
from jax import lax
from jax.sharding import PartitionSpec as P

ITERS = 5


highest = lax.Precision.HIGHEST


def with_halo(cells, sides, width):
    for axis, dim in sides:
        count = lax.axis_size(axis)
        ends = count - 1
        head = lax.slice_in_dim(cells, 0, width, axis=dim)
        tail = lax.slice_in_dim(cells, cells.shape[dim] - width, cells.shape[dim], axis=dim)
        cells = jnp.concatenate(
            [
                lax.ppermute(tail, axis, [(i, (i + 1) % count) for i in range(ends)]),
                cells,
                lax.ppermute(head, axis, [((i + 1) % count, i) for i in range(ends)]),
            ],
            axis=dim,
        )
    return cells


def inverse_root(covariance, drive):
    members = covariance.shape[0]
    identity = jnp.eye(members, dtype=jnp.float32)
    system = identity + covariance / (members - 1)
    bound = jnp.max(jnp.sum(jnp.abs(system), axis=1))
    upper = system / bound
    lower = identity
    for sweep in range(ITERS):
        factor = 1.5 * identity - 0.5 * jnp.dot(lower, upper, precision=highest)
        upper = jnp.dot(upper, factor, precision=highest)
        lower = jnp.dot(factor, lower, precision=highest)
    root = lower / jnp.sqrt(bound)
    shift = jnp.dot(root, jnp.dot(root, drive, precision=highest), precision=highest)
    return (root + shift[:, None]).astype(jnp.bfloat16)


def local(
    obs_rows,
    innovations,
    obs_home,
    obs_lists,
    loc_weights,
    state_mean,
    state_perturb,
    interp_ids,
    interp_wts,
):
    lon_count = lax.axis_size("lon")
    lat_count = lax.axis_size("lat")
    devices_all = lon_count * lat_count
    held_blocks, obs_count, members = obs_rows.shape
    point_rows, point_cols, list_len = obs_lists.shape
    entries = point_rows * point_cols * list_len
    capacity = max(2, (entries + devices_all - 1) // devices_all)
    entry_ids = obs_lists.reshape(-1)
    live = entry_ids >= 0
    home_rows = jnp.take(obs_home, jnp.maximum(entry_ids, 0))
    owner = jnp.where(live, home_rows // held_blocks, devices_all)
    local_slot = home_rows % held_blocks
    owner_hits = (owner[:, None] == jnp.arange(devices_all, dtype=jnp.int32)[None, :]).astype(
        jnp.int32
    )
    rank = jnp.sum((jnp.cumsum(owner_hits, axis=0) - 1) * owner_hits, axis=1)
    request = (
        jnp.zeros((devices_all, capacity), jnp.int32).at[owner, rank].set(local_slot, mode="drop")
    )
    asked = lax.all_to_all(request, ("lon", "lat"), split_axis=0, concat_axis=0, tiled=True)
    picked_rows = jnp.take(obs_rows, asked.reshape(-1), axis=0).reshape(
        devices_all, capacity, obs_count, members
    )
    picked_incr = jnp.take(innovations, asked.reshape(-1), axis=0).reshape(
        devices_all, capacity, obs_count
    )
    got_rows, got_incr = (
        lax.all_to_all(picked_rows, ("lon", "lat"), split_axis=0, concat_axis=0, tiled=True),
        lax.all_to_all(picked_incr, ("lon", "lat"), split_axis=0, concat_axis=0, tiled=True),
    )
    rows_flat = got_rows.reshape(devices_all * capacity, obs_count, members)
    incr_flat = got_incr.reshape(devices_all * capacity, obs_count)
    entry_slot = jnp.where(live, owner * capacity + rank, 0).reshape(-1, list_len)
    weight_live = jnp.where(live, loc_weights.reshape(-1), jnp.float32(0.0)).reshape(-1, list_len)

    def one_point(packed):
        slot_here, weight_here = packed
        blocks = jnp.take(rows_flat, slot_here, axis=0)
        increments = jnp.take(incr_flat, slot_here, axis=0)
        grams = jnp.einsum("lok,lom->lkm", blocks, blocks, preferred_element_type=jnp.float32)
        covariance = jnp.einsum("l,lkm->km", weight_here, grams, precision=highest)
        project = jnp.einsum("lok,lo->lk", blocks, increments, preferred_element_type=jnp.float32)
        drive = jnp.dot(weight_here, project, precision=highest) / (members - 1)
        return inverse_root(covariance, drive)

    weights = lax.map(one_point, (entry_slot, weight_live)).reshape(
        point_rows, point_cols, members, members
    )
    widened = with_halo(weights, (("lon", 0), ("lat", 1)), 1)
    halo_rows = point_rows + 2
    halo_cols = point_cols + 2
    grid_cols = point_cols * lat_count
    tile_rows, tile_cols, cells = state_mean.shape
    tile_count = tile_rows * tile_cols
    target_ids = interp_ids.reshape(tile_count, 4)
    local_row = target_ids // grid_cols - (lax.axis_index("lon") * point_rows - 1)
    local_col = target_ids % grid_cols - (lax.axis_index("lat") * point_cols - 1)
    flat_place = local_row * halo_cols + local_col
    places = jnp.arange(halo_rows * halo_cols, dtype=jnp.int32)
    mixing = jnp.sum(
        interp_wts.reshape(tile_count, 4)[:, :, None]
        * (flat_place[:, :, None] == places[None, None, :]).astype(jnp.float32),
        axis=1,
    )
    tile_w = jnp.dot(
        mixing,
        widened.reshape(halo_rows * halo_cols, members * members).astype(jnp.float32),
        precision=highest,
    )
    tile_w = tile_w.astype(jnp.bfloat16).reshape(tile_count, members, members)
    moved = jnp.einsum(
        "tck,tkm->tcm",
        state_perturb.reshape(tile_count, cells, members),
        tile_w,
        preferred_element_type=jnp.float32,
    )
    result = (state_mean.reshape(tile_count, cells)[:, :, None] + moved).astype(jnp.bfloat16)
    return result.reshape(tile_rows, tile_cols, cells, members)


def solution(mesh):
    return jax.shard_map(
        local,
        mesh=mesh,
        in_specs=(
            P(("lon", "lat"), None, None),
            P(("lon", "lat"), None),
            P(),
            P("lon", "lat", None),
            P("lon", "lat", None),
            P("lon", "lat", None),
            P("lon", "lat", None, None),
            P("lon", "lat", None),
            P("lon", "lat", None),
        ),
        out_specs=P("lon", "lat", None, None),
        check_vma=False,
    )
```

profile of v0, /device:TPU:25, one launch (start us, length us, event | category | flops | bytes accessed | tf_op | source)
XLA Modules:
  0.0 504.8 jit_solution(2822535908845470107)
XLA Ops:
  4.4 9.3 %scatter_fusion = s32[128,2]{0,1:T(2,128)S(1)} fusion(s32[128,2]{0,1:T(2,128)S(1)} %broadcast_in_dim.86, s32[192]{0:T(256)S(1)} %bitcast.197, s32[192]{0:T(256)S(1)} %get-tuple-element.56), kind=kCustom, calls=%fused_computation.5 | custom fusion | bytes 3840 | tf_op jit(solution)/shard_map/scatter | solution.py:73
  13.8 18.5 %all_to_all.19 = s32[128,1,2]{2,1,0:T(1,128)S(1)} all-to-all(s32[128,1,2]{2,1,0:T(1,128)S(1)} %copy.47), channel_id=1, replica_groups=mesh['lon'=8,'lat'=16] {'lon','lat'}, dimensions={0} | all-to-all | bytes 2048 | tf_op jit(solution)/shard_map/all_to_all | solution.py:75
  34.0 9.4 %gather_fusion.3 = bf16[256,128,256]{2,1,0:T(8,128)(2,1)} fusion(bf16[16,128,256]{2,1,0:T(8,128)(2,1)S(1)} %copy-done, s32[1024]{0:T(1024)S(1)} %pad_clamp_fusion.1), kind=kCustom, calls=%fused_computation.3 | custom fusion | bytes 33555456 | tf_op jit(solution)/shard_map/jit(_take)/gather | solution.py:76
  45.1 6.1 %all-to-all-start.2 = ((bf16[128,2,128]{2,1,0:T(2,128)(2,1)}), bf16[128,2,128]{2,1,0:T(2,128)(2,1)S(1)}, u32[]{:S(2)}, u32[]{:S(2)}) async-start(bf16[128,2,128]{2,1,0:T(2,128)(2,1)} %broadcast_select_fusion.4), calls=%async_computation.2 | async-start | bytes 131072 | tf_op jit(solution)/shard_map/all_to_all | solution.py:84
  51.2 14.1 %broadcast_select_fusion.3 = bf16[128,2,128,256]{3,2,1,0:T(8,128)(2,1)} fusion(bf16[128,2,128,256]{3,2,1,0:T(8,128)(2,1)} %bitcast.195, pred[128,2]{1,0:T(8,128)(4,1)S(1)} %copy.49), kind=kLoop, calls=%fused_computation.53 | loop fusion | flops 8388608 | bytes 33554688 | tf_op jit(solution)/shard_map/jit(_take)/select_n | solution.py:76
  65.3 10.2 %all-to-all-start.1 = ((bf16[128,2,128,256]{3,2,1,0:T(8,128)(2,1)}), bf16[128,2,128,256]{3,2,1,0:T(8,128)(2,1)}, u32[]{:S(2)}, u32[]{:S(2)}) async-start(bf16[128,2,128,256]{3,2,1,0:T(8,128)(2,1)} %broadcast_select_fusion.3), calls=%async_computation.1 | async-start | bytes 33554432 | tf_op jit(solution)/shard_map/all_to_all | solution.py:83
  75.8 235.3 %all-to-all-done.1 = bf16[128,2,128,256]{3,2,1,0:T(8,128)(2,1)} async-done(((bf16[128,2,128,256]{3,2,1,0:T(8,128)(2,1)}), bf16[128,2,128,256]{3,2,1,0:T(8,128)(2,1)}, u32[]{:S(2)}, u32[]{:S(2)}) %all-to-all-start.1) | async-done | bytes 16777248 | tf_op jit(solution)/shard_map/all_to_all | solution.py:83
  311.1 147.0 %while.10 = (s32[]{:T(128)}, bf16[4,256,256]{2,1,0:T(8,128)(2,1)}, f32[4,48]{1,0:T(4,128)S(1)}, s32[4,48]{1,0:T(4,128)S(1)}, bf16[256,128,256]{2,1,0:T(8,128)(2,...) while((s32[]{:T(128)}, bf16[4,256,256]{2,1,0:T(8,128)(2,1)}, f32[4,48]{1,0:T(4,128)S(1)}, ...), condition=%wide.region_8.9_spmd, body=%wide.region_5.8_spmd.sunk | while | flops 3672334080 | bytes 49853376 | solution.py:101
  311.1 6.5 %gather_fusion = bf16[48,128,256]{2,1,0:T(8,128)(2,1)S(1)} fusion(bf16[256,128,256]{2,1,0:T(8,128)(2,1)} %get-tuple-element.115, s32[1024]{0:T(1024)S(1)} %pad_clamp_fusion.4), kind=kCustom, calls=%fused_computation.clone.1 | custom fusion | bytes 6291648 | tf_op jit(solution)/shard_map/while/body/eval_jaxpr/jit(_take)/gather | solution.py:93
  321.0 12.8 %fusion.178 = f32[1,256,256]{2,0,1:T(1,128)S(1)} fusion(f32[48,256,256]{2,1,0:T(8,128)S(1)} %fusion.177, f32[4,48]{1,0:T(4,128)S(1)} %get-tuple-element.113, s32[]{:T(128)} %get-tuple-element.103), kind=kOutput, calls=%fused_computation.6.clone.1 | convolution fusion | flops 37748736 | bytes 12845572 | tf_op jit(solution)/shard_map/while/body/eval_jaxpr/l,lkm->km/dot_general | solution.py:96
  347.8 6.5 %gather_fusion = bf16[48,128,256]{2,1,0:T(8,128)(2,1)S(1)} fusion(bf16[256,128,256]{2,1,0:T(8,128)(2,1)} %get-tuple-element.115, s32[1024]{0:T(1024)S(1)} %pad_clamp_fusion.4), kind=kCustom, calls=%fused_computation.clone.1 | custom fusion | bytes 6291648 | tf_op jit(solution)/shard_map/while/body/eval_jaxpr/jit(_take)/gather | solution.py:93
  354.4 3.3 fusion.177
  357.7 12.8 %fusion.178 = f32[1,256,256]{2,0,1:T(1,128)S(1)} fusion(f32[48,256,256]{2,1,0:T(8,128)S(1)} %fusion.177, f32[4,48]{1,0:T(4,128)S(1)} %get-tuple-element.113, s32[]{:T(128)} %get-tuple-element.103), kind=kOutput, calls=%fused_computation.6.clone.1 | convolution fusion | flops 37748736 | bytes 12845572 | tf_op jit(solution)/shard_map/while/body/eval_jaxpr/l,lkm->km/dot_general | solution.py:96
  384.6 6.5 %gather_fusion = bf16[48,128,256]{2,1,0:T(8,128)(2,1)S(1)} fusion(bf16[256,128,256]{2,1,0:T(8,128)(2,1)} %get-tuple-element.115, s32[1024]{0:T(1024)S(1)} %pad_clamp_fusion.4), kind=kCustom, calls=%fused_computation.clone.1 | custom fusion | bytes 6291648 | tf_op jit(solution)/shard_map/while/body/eval_jaxpr/jit(_take)/gather | solution.py:93
  391.1 3.3 fusion.177
  394.4 12.8 %fusion.178 = f32[1,256,256]{2,0,1:T(1,128)S(1)} fusion(f32[48,256,256]{2,1,0:T(8,128)S(1)} %fusion.177, f32[4,48]{1,0:T(4,128)S(1)} %get-tuple-element.113, s32[]{:T(128)} %get-tuple-element.103), kind=kOutput, calls=%fused_computation.6.clone.1 | convolution fusion | flops 37748736 | bytes 12845572 | tf_op jit(solution)/shard_map/while/body/eval_jaxpr/l,lkm->km/dot_general | solution.py:96
  421.3 6.5 %gather_fusion = bf16[48,128,256]{2,1,0:T(8,128)(2,1)S(1)} fusion(bf16[256,128,256]{2,1,0:T(8,128)(2,1)} %get-tuple-element.115, s32[1024]{0:T(1024)S(1)} %pad_clamp_fusion.4), kind=kCustom, calls=%fused_computation.clone.1 | custom fusion | bytes 6291648 | tf_op jit(solution)/shard_map/while/body/eval_jaxpr/jit(_take)/gather | solution.py:93
  431.2 12.8 %fusion.178 = f32[1,256,256]{2,0,1:T(1,128)S(1)} fusion(f32[48,256,256]{2,1,0:T(8,128)S(1)} %fusion.177, f32[4,48]{1,0:T(4,128)S(1)} %get-tuple-element.113, s32[]{:T(128)} %get-tuple-element.103), kind=kOutput, calls=%fused_computation.6.clone.1 | convolution fusion | flops 37748736 | bytes 12845572 | tf_op jit(solution)/shard_map/while/body/eval_jaxpr/l,lkm->km/dot_general | solution.py:96
  464.4 4.4 collective-permute-done.1
  473.0 6.3 %collective-permute-start.3 = (bf16[4,1,256,256]{3,2,1,0:T(8,128)(2,1)S(1)}, bf16[4,1,256,256]{3,2,1,0:T(8,128)(2,1)S(1)}, u32[]{:S(2)}, u32[]{:S(2)}) collective-permute-start(bf16[4,1,256,256]{3,2,1,0:T(8,128)(2,1)S(1)} %get-tuple-element.51), channel_id=1, source_target_pairs={{1,0},{2,1},{3,2},{4,3},{5,4},{6,5},{7,6},{8,7},{9,8},{10,9},{11,1... | collective-permute-start | bytes 1572872 | tf_op jit(solution)/shard_map/ppermute | solution.py:22
  479.6 4.6 collective-permute-done.2
  484.2 3.4 collective-permute-done.3
  494.1 3.4 add_convert_fusion.1
  497.5 7.3 %copy.52 = bf16[4,4,512,256]{3,2,1,0:T(8,128)(2,1)} copy(bf16[4,4,512,256]{2,3,1,0:T(8,128)(2,1)} %bitcast.196) | data formatting | bytes 8388608 | tf_op jit(solution)/shard_map/reshape | solution.py:133
  (183 shorter events, 85.3 us)
Async XLA Ops:
  0.0 34.0 %copy-start = (bf16[16,128,256]{2,1,0:T(8,128)(2,1)S(1)}, bf16[16,128,256]{2,1,0:T(8,128)(2,1)}, u32[]{:S(2)}) copy-start(bf16[16,128,256]{2,1,0:T(8,128)(2,1)} %param.11) | copy-start | bytes 3145732
  34.0 9.4 %copy-start.2 = (bf16[16,128]{1,0:T(8,128)(2,1)S(1)}, bf16[16,128]{1,0:T(8,128)(2,1)}, u32[]{:S(2)}) copy-start(bf16[16,128]{1,0:T(8,128)(2,1)} %param.12) | copy-start | bytes 12292
  45.1 20.2 %all-to-all-start.2 = ((bf16[128,2,128]{2,1,0:T(2,128)(2,1)}), bf16[128,2,128]{2,1,0:T(2,128)(2,1)S(1)}, u32[]{:S(2)}, u32[]{:S(2)}) async-start(bf16[128,2,128]{2,1,0:T(2,128)(2,1)} %broadcast_select_fusion.4), calls=%async_computation.2 | async-start | bytes 131072 | tf_op jit(solution)/shard_map/all_to_all | solution.py:84
  65.3 10.4 %copy-start.7 = (f32[2,2,48]{2,1,0:T(2,128)S(1)}, f32[2,2,48]{2,1,0:T(2,128)}, u32[]{:S(2)}) copy-start(f32[2,2,48]{2,1,0:T(2,128)} %param.15) | copy-start | bytes 2308
  65.3 245.7 %all-to-all-start.1 = ((bf16[128,2,128,256]{3,2,1,0:T(8,128)(2,1)}), bf16[128,2,128,256]{3,2,1,0:T(8,128)(2,1)}, u32[]{:S(2)}, u32[]{:S(2)}) async-start(bf16[128,2,128,256]{3,2,1,0:T(8,128)(2,1)} %broadcast_select_fusion.3), calls=%async_computation.1 | async-start | bytes 33554432 | tf_op jit(solution)/shard_map/all_to_all | solution.py:83
  458.0 21.3 %copy-start.5 = (s32[4,4,4]{2,1,0:T(4,128)S(1)}, s32[4,4,4]{2,1,0:T(4,128)}, u32[]{:S(2)}) copy-start(s32[4,4,4]{2,1,0:T(4,128)} %param.18) | copy-start | bytes 772
  458.0 21.3 %copy-start.6 = (f32[4,4,4]{2,1,0:T(4,128)S(1)}, f32[4,4,4]{2,1,0:T(4,128)}, u32[]{:S(2)}) copy-start(f32[4,4,4]{2,1,0:T(4,128)} %param.19) | copy-start | bytes 772
  458.0 21.4 %copy-start.4 = (f32[4,4,512]{2,1,0:T(4,128)S(1)}, f32[4,4,512]{2,1,0:T(4,128)}, u32[]{:S(2)}) copy-start(f32[4,4,512]{2,1,0:T(4,128)} %param.16) | copy-start | bytes 98308
  459.1 5.2 %collective-permute-start = (bf16[1,2,256,256]{3,2,1,0:T(8,128)(2,1)S(1)}, bf16[1,2,256,256]{3,2,1,0:T(8,128)(2,1)S(1)}, u32[]{:S(2)}, u32[]{:S(2)}) collective-permute-start(bf16[1,2,256,256]{3,2,1,0:T(8,128)(2,1)S(1)} %get-tuple-element.52), channel_id=1, source_target_pairs={{0,16},{16,32},{32,48},{48,64},{64,80},{80,96},{96,112},{1,17},{17... | collective-permute-start | bytes 786440 | tf_op jit(solution)/shard_map/ppermute | solution.py:20
  461.1 7.7 %collective-permute-start.1 = (bf16[1,2,256,256]{3,2,1,0:T(8,128)(2,1)S(1)}, bf16[1,2,256,256]{3,2,1,0:T(8,128)(2,1)S(1)}, u32[]{:S(2)}, u32[]{:S(2)}) collective-permute-start(bf16[1,2,256,256]{3,2,1,0:T(8,128)(2,1)S(1)} %get-tuple-element.53), channel_id=1, source_target_pairs={{16,0},{32,16},{48,32},{64,48},{80,64},{96,80},{112,96},{17,1},{33... | collective-permute-start | bytes 786440 | tf_op jit(solution)/shard_map/ppermute | solution.py:22
  470.0 14.2 %collective-permute-start.2 = (bf16[4,1,256,256]{3,2,1,0:T(8,128)(2,1)S(1)}, bf16[4,1,256,256]{3,2,1,0:T(8,128)(2,1)S(1)}, u32[]{:S(2)}, u32[]{:S(2)}) collective-permute-start(bf16[4,1,256,256]{3,2,1,0:T(8,128)(2,1)S(1)} %get-tuple-element.50), channel_id=1, source_target_pairs={{0,1},{1,2},{2,3},{3,4},{4,5},{5,6},{6,7},{7,8},{8,9},{9,10},{10,1... | collective-permute-start | bytes 1572872 | tf_op jit(solution)/shard_map/ppermute | solution.py:20
  473.0 14.6 %collective-permute-start.3 = (bf16[4,1,256,256]{3,2,1,0:T(8,128)(2,1)S(1)}, bf16[4,1,256,256]{3,2,1,0:T(8,128)(2,1)S(1)}, u32[]{:S(2)}, u32[]{:S(2)}) collective-permute-start(bf16[4,1,256,256]{3,2,1,0:T(8,128)(2,1)S(1)} %get-tuple-element.51), channel_id=1, source_target_pairs={{1,0},{2,1},{3,2},{4,3},{5,4},{6,5},{7,6},{8,7},{9,8},{10,9},{11,1... | collective-permute-start | bytes 1572872 | tf_op jit(solution)/shard_map/ppermute | solution.py:22
  492.0 2.2 copy-start.3
  497.5 7.3 %copy-start.1 = (bf16[16,128,256]{2,1,0:T(8,128)(2,1)S(1)}, bf16[16,128,256]{2,1,0:T(8,128)(2,1)}, u32[]{:S(2)}) copy-start(bf16[16,128,256]{2,1,0:T(8,128)(2,1)} %param.11) | copy-start | bytes 3145732
where the time goes:
time: 512 us; the launch traced here: 505 us
  waiting for transfers between devices  249 us (49%)
  matrix products  114 us (22%)
  local copies, waits for them, and re-layouts  63.7 us (12%)
  starting transfers between devices  29.9 us (6%)
  other arithmetic  27 us (5%)
  blocking collectives  18.5 us (4%)
    all_to_all x1, waiting for transfers between devices, local(): lax.all_to_all(picked_rows, ('lon', 'lat'), split_axis=0, concat_axis=0,...  235 us
    dot_general x4, matrix products, one_point(): covariance = jnp.einsum('l,lkm->km', weight_here, grams, precision=highest)  51.4 us
    gather x4, local copies, waits for them, and re-layouts, one_point(): blocks = jnp.take(rows_flat, slot_here, axis=0)  26.1 us
    all_to_all x1, blocking collectives, local(): lax.all_to_all(request, ('lon', 'lat'), split_axis=0, concat_axis=0, tile...  18.5 us
    dot_general x20, matrix products, inverse_root(): factor = 1.5 * identity - 0.5 * jnp.dot(lower, upper, precision=highest)  16.3 us
    select_n x2, other arithmetic, local(): jnp.take(obs_rows, asked.reshape(-1), axis=0)  14.1 us
    dot_general x20, matrix products, inverse_root(): lower = jnp.dot(factor, lower, precision=highest)  14.1 us
    dot_general x4, matrix products, one_point(): jnp.einsum('lok,lom->lkm', blocks, blocks, preferred_element_type=jnp.flo...  13.3 us
  transfers between devices with their start and end apart: 6, of which 5 were waited for; matrix products, arithmetic and copies ran while one was open for 3% of the time, Pallas kernels for 0%

commit v1 on v0

v1 whole, which is shorter than its diff:
```python
import functools

import jax
import jax.numpy as jnp
from jax import lax
from jax.experimental import pallas as pl
from jax.experimental.pallas import tpu as pltpu
from jax.sharding import PartitionSpec as P

ITERS = 5
FAST = 4
bf16 = jnp.bfloat16
f32 = jnp.float32
highest = lax.Precision.HIGHEST


def split(x):
    hi = x.astype(bf16)
    return hi, (x - hi.astype(f32)).astype(bf16)


def mm(a, b):
    left = jnp.concatenate([a[0], a[0], a[1]], axis=1)
    right = jnp.concatenate([b[0], b[1], b[0]], axis=0)
    return jnp.dot(left, right, preferred_element_type=f32)


def gram_kernel(points, ranks, slots, wts, y_ref, proj_ref, o_ref, acc_ref):
    dest = pl.program_id(0)
    half = y_ref.shape[2] // 2
    row = lax.broadcasted_iota(jnp.int32, (half, half), 0)
    col = lax.broadcasted_iota(jnp.int32, (half, half), 1)
    for p in range(points):
        at = p * ranks
        ys = [y_ref[slots[dest, at + k]] for k in range(FAST)]
        yw = [(ys[k].astype(f32) * wts[dest, at + k]).astype(bf16) for k in range(FAST)]
        acc_ref[p] = lax.dot_general(
            jnp.concatenate(yw, axis=0),
            jnp.concatenate(ys, axis=0),
            (((0,), (0,)), ((), ())),
            preferred_element_type=f32,
        )
        count = slots[dest, points * ranks + p]

        @pl.loop(FAST, jnp.maximum(count, FAST))
        def _(k):
            y = y_ref[slots[dest, at + k]]
            w = (y.astype(f32) * wts[dest, at + k]).astype(bf16)
            acc_ref[p] += lax.dot_general(
                w, y, (((0,), (0,)), ((), ())), preferred_element_type=f32
            )

        drive = lax.fori_loop(
            0,
            count,
            lambda k, total: total + wts[dest, at + k] * proj_ref[slots[dest, at + k]],
            jnp.zeros(proj_ref.shape[1:], f32),
        )
        lower_right = acc_ref[p, half:, half:]
        o_ref[0, p, :half] = acc_ref[p, half:, :half].astype(bf16)
        o_ref[0, p, half : 2 * half] = jnp.where(
            row >= col, acc_ref[p, :half, :half], lower_right
        ).astype(bf16)
        diagonal = jnp.sum(jnp.where(row == col, lower_right, 0.0), axis=0, keepdims=True)
        diag_hi, diag_lo = split(diagonal)
        drive_hi, drive_lo = split(drive)
        tail = jnp.concatenate(
            [
                v.astype(f32)
                for v in (diag_hi, diag_lo, drive_hi, drive_lo)
            ]
            + [jnp.zeros((10, half), f32)],
            axis=0,
        )
        o_ref[0, p, 2 * half :] = tail.astype(bf16)


def root_kernel(parts_ref, o_ref):
    sources, points, _, half = parts_ref.shape
    members = 2 * half
    row = lax.broadcasted_iota(jnp.int32, (half, half), 0)
    col = lax.broadcasted_iota(jnp.int32, (half, half), 1)
    eye = (
        lax.broadcasted_iota(jnp.int32, (members, members), 0)
        == lax.broadcasted_iota(jnp.int32, (members, members), 1)
    ).astype(f32)
    for p in range(points):
        total = parts_ref[0, p].astype(f32)
        for s in range(1, sources):
            total = total + parts_ref[s, p].astype(f32)
        corner = total[:half]
        both = total[half:members]
        turned = both.T
        diagonal = total[members : members + 1] + total[members + 1 : members + 2]
        upper_left = jnp.where(row >= col, both, turned)
        lower_right = jnp.where(
            row == col, jnp.broadcast_to(diagonal, (half, half)), jnp.where(row < col, both, turned)
        )
        cov = jnp.concatenate(
            [
                jnp.concatenate([upper_left, corner.T], axis=1),
                jnp.concatenate([corner, lower_right], axis=1),
            ],
            axis=0,
        )
        scale = 1.0 / (members - 1)
        drive = (
            jnp.concatenate(
                [
                    total[members + 2 + h : members + 3 + h] + total[members + 4 + h : members + 5 + h]
                    for h in range(2)
                ],
                axis=1,
            )
            * scale
        )
        system = eye + cov * scale
        bound = jnp.max(jnp.sum(jnp.abs(system), axis=0, keepdims=True), axis=1, keepdims=True)
        upper = system * (1.0 / bound)
        factor = 1.5 * eye - 0.5 * upper
        factor_s = split(factor)
        lower, lower_s = factor, factor_s
        upper_s = split(mm(split(upper), factor_s))
        for sweep in range(1, ITERS):
            factor_s = split(1.5 * eye - 0.5 * mm(lower_s, upper_s))
            if sweep < ITERS - 1:
                upper_s = split(mm(upper_s, factor_s))
            lower = mm(factor_s, lower_s)
            lower_s = split(lower)
        root = lower * lax.rsqrt(bound)
        root_s = split(root)
        once = mm(split(jnp.broadcast_to(drive, (16, members))), root_s)[:1]
        shift = jnp.sum(root * once, axis=1, keepdims=True)
        o_ref[p] = (root + shift).astype(bf16)


def state_kernel(places, mixing, mean_ref, pert_ref, w_ref, o_ref):
    tile = pl.program_id(0)
    total = mixing[tile, 0] * w_ref[places[tile, 0]].astype(f32)
    for j in range(1, 4):
        total = total + mixing[tile, j] * w_ref[places[tile, j]].astype(f32)
    moved = jnp.dot(pert_ref[0], total.astype(bf16), preferred_element_type=f32)
    mean = jnp.broadcast_to(mean_ref[0], (8, mean_ref.shape[2])).T[:, :1]
    o_ref[0] = (mean + moved).astype(bf16)


def with_halo(cells, sides, width):
    for axis, dim in sides:
        count = lax.axis_size(axis)
        ends = count - 1
        head = lax.slice_in_dim(cells, 0, width, axis=dim)
        tail = lax.slice_in_dim(cells, cells.shape[dim] - width, cells.shape[dim], axis=dim)
        cells = jnp.concatenate(
            [
                lax.ppermute(tail, axis, [(i, (i + 1) % count) for i in range(ends)]),
                cells,
                lax.ppermute(head, axis, [((i + 1) % count, i) for i in range(ends)]),
            ],
            axis=dim,
        )
    return cells


def local(
    obs_rows,
    innovations,
    obs_home,
    obs_lists,
    loc_weights,
    state_mean,
    state_perturb,
    interp_ids,
    interp_wts,
):
    lon_count = lax.axis_size("lon")
    lat_count = lax.axis_size("lat")
    held, obs_count, members = obs_rows.shape
    half = members // 2
    point_rows, point_cols, list_len = obs_lists.shape
    points = point_rows * point_cols
    ranks = 2 * lon_count

    column_rows = lax.all_gather(obs_rows, "lon", tiled=True)
    project = jnp.einsum("lok,lo->lk", obs_rows, innovations, preferred_element_type=f32)
    column_proj = lax.all_gather(project, "lon", tiled=True).reshape(lon_count * held, 2, half)

    ids = obs_lists.reshape(points, list_len)
    live = ids >= 0
    home = jnp.take(obs_home, jnp.maximum(ids, 0))
    column = jnp.where(live, home // held % lat_count, lat_count)
    slot = home // (held * lat_count) * held + home % held
    mask = column[None] == jnp.arange(lat_count, dtype=jnp.int32)[:, None, None]
    rank = jnp.cumsum(mask.astype(jnp.int32), axis=2) - 1
    chosen = mask[..., None] & (rank[..., None] == jnp.arange(ranks, dtype=jnp.int32))
    slots_f = jnp.sum(jnp.where(chosen, slot.astype(f32)[None, :, :, None], 0.0), axis=2)
    wts_f = jnp.sum(
        jnp.where(chosen, loc_weights.reshape(1, points, list_len, 1), 0.0), axis=2
    )
    counts = jnp.sum(mask.astype(f32), axis=2)
    asked = jnp.concatenate(
        [
            slots_f.reshape(lat_count, points * ranks),
            counts,
            wts_f.reshape(lat_count, points * ranks),
        ],
        axis=1,
    )
    asked = lax.all_to_all(asked, "lat", 0, 0, tiled=True)
    cut = points * ranks + points
    slots = asked[:, :cut].astype(jnp.int32)
    wts = asked[:, cut:]

    smem = pl.BlockSpec(memory_space=pltpu.SMEM)
    vmem = pl.BlockSpec(memory_space=pltpu.VMEM)
    rows = members + 16
    partial = pl.pallas_call(
        functools.partial(gram_kernel, points, ranks),
        grid=(lat_count,),
        out_shape=jax.ShapeDtypeStruct((lat_count, points, rows, half), bf16),
        in_specs=[smem, smem, vmem, vmem],
        out_specs=pl.BlockSpec((1, points, rows, half), lambda i: (i, 0, 0, 0)),
        scratch_shapes=[pltpu.VMEM((points, members, members), f32)],
        compiler_params=pltpu.CompilerParams(vmem_limit_bytes=40 << 20),
        cost_estimate=pl.CostEstimate(
            flops=2 * 64 * 512 * 256 * 256, bytes_accessed=13 << 20, transcendentals=0
        ),
        name="gram",
    )(slots, wts, column_rows, column_proj)
    parts = lax.all_to_all(partial, "lat", 0, 0, tiled=True)

    group = 2
    weights = pl.pallas_call(
        root_kernel,
        grid=(points // group,),
        out_shape=jax.ShapeDtypeStruct((points, members, members), bf16),
        in_specs=[pl.BlockSpec((lat_count, group, rows, half), lambda i: (0, i, 0, 0))],
        out_specs=pl.BlockSpec((group, members, members), lambda i: (i, 0, 0)),
        compiler_params=pltpu.CompilerParams(vmem_limit_bytes=40 << 20),
        cost_estimate=pl.CostEstimate(
            flops=4 * 36 * 2 * 256**3, bytes_accessed=5 << 20, transcendentals=0
        ),
        name="root",
    )(parts).reshape(point_rows, point_cols, members, members)

    widened = with_halo(weights, (("lat", 1), ("lon", 0)), 1)
    halo_rows = point_rows + 2
    halo_cols = point_cols + 2
    grid_cols = point_cols * lat_count
    tile_rows, tile_cols, cells = state_mean.shape
    tiles = tile_rows * tile_cols
    target_ids = interp_ids.reshape(tiles, 4)
    local_row = target_ids // grid_cols - (lax.axis_index("lon") * point_rows - 1)
    local_col = target_ids % grid_cols - (lax.axis_index("lat") * point_cols - 1)
    places = local_row * halo_cols + local_col
    result = pl.pallas_call(
        state_kernel,
        grid=(tiles,),
        out_shape=jax.ShapeDtypeStruct((tiles, cells, members), bf16),
        in_specs=[
            smem,
            smem,
            pl.BlockSpec((1, 1, cells), lambda i: (i, 0, 0)),
            pl.BlockSpec((1, cells, members), lambda i: (i, 0, 0)),
            vmem,
        ],
        out_specs=pl.BlockSpec((1, cells, members), lambda i: (i, 0, 0)),
        compiler_params=pltpu.CompilerParams(vmem_limit_bytes=40 << 20),
        cost_estimate=pl.CostEstimate(
            flops=2 * 16 * 512 * 256 * 256, bytes_accessed=11 << 20, transcendentals=0
        ),
        name="state",
    )(
        places,
        interp_wts.reshape(tiles, 4),
        state_mean.reshape(tiles, 1, cells),
        state_perturb.reshape(tiles, cells, members),
        widened.reshape(halo_rows * halo_cols, members, members),
    )
    return result.reshape(tile_rows, tile_cols, cells, members)


def solution(mesh):
    return jax.shard_map(
        local,
        mesh=mesh,
        in_specs=(
            P(("lon", "lat"), None, None),
            P(("lon", "lat"), None),
            P(),
            P("lon", "lat", None),
            P("lon", "lat", None),
            P("lon", "lat", None),
            P("lon", "lat", None, None),
            P("lon", "lat", None),
            P("lon", "lat", None),
        ),
        out_specs=P("lon", "lat", None, None),
        check_vma=False,
    )
```

time: 512 us -> 204 us (0.40); the launches traced: 505 us -> 204 us
  waiting for transfers between devices: 249 us -> 44.1 us
  matrix products: 114 us -> 0.24 us
  local copies, waits for them, and re-layouts: 63.7 us -> 6.28 us
  blocking collectives: 18.5 us -> 72.7 us
  Pallas kernels: 0 us -> 44.6 us
  other arithmetic: 27 us -> 3.27 us
  between operations: 0.26 us -> 13.6 us
  starting transfers between devices: 29.9 us -> 19.4 us
    all_to_all x2 -> x1, waiting for transfers between devices: 235 us -> 0.01 us  [local(): asked = lax.all_to_all(asked, 'lat', 0, 0, tiled=True)]
    dot_general x82 -> x1, matrix products: 114 us -> 0.24 us  [local(): jnp.einsum('lok,lo->lk', obs_rows, innovations, preferred_element_type=f32)]
    pallas_call x0 -> x3, Pallas kernels: none -> 44.6 us  [the longest x1 22.4 us: local(): pl.pallas_call(functools.partial(gram_kernel, points, ranks), grid=(lat_c...]
    gather x12 -> x2, local copies, waits for them, and re-layouts: 40.8 us -> 1.52 us  [local(): home = jnp.take(obs_home, jnp.maximum(ids, 0))]
    all_to_all x1, blocking collectives: 18.5 us -> 57.6 us  [local(): parts = lax.all_to_all(partial, 'lat', 0, 0, tiled=True)]
    all_gather x0 -> x1, waiting for transfers between devices: none -> 27.2 us  [local(): column_rows = lax.all_gather(obs_rows, 'lon', tiled=True)]
    select_n x14 -> x1, other arithmetic: 15.3 us -> 0.02 us  [local(): column = jnp.where(live, home // held % lat_count, lat_count)]
    all_gather x0 -> x1, blocking collectives: none -> 15.1 us  [local(): lax.all_gather(project, 'lon', tiled=True)]
where the time goes in v1:
time: 204 us
  blocking collectives  72.7 us (36%)
  Pallas kernels  44.6 us (22%)
  waiting for transfers between devices  44.1 us (22%)
  starting transfers between devices  19.4 us (10%)
  between operations  13.6 us (7%)
  local copies, waits for them, and re-layouts  6.28 us (3%)
  other arithmetic  3.27 us (2%)
    all_to_all x1, blocking collectives, local(): parts = lax.all_to_all(partial, 'lat', 0, 0, tiled=True)  57.6 us
    all_gather x1, waiting for transfers between devices, local(): column_rows = lax.all_gather(obs_rows, 'lon', tiled=True)  27.2 us
    pallas_call x1, Pallas kernels, local(): pl.pallas_call(functools.partial(gram_kernel, points, ranks), grid=(lat_c...  22.4 us
    all_gather x1, blocking collectives, local(): lax.all_gather(project, 'lon', tiled=True)  15.1 us
    pallas_call x1, Pallas kernels, local(): pl.pallas_call(root_kernel, grid=(points // group,), out_shape=jax.ShapeD...  12.9 us
    pallas_call x1, Pallas kernels, local(): pl.pallas_call(state_kernel, grid=(tiles,), out_shape=jax.ShapeDtypeStruc...  9.31 us
    ppermute x2, waiting for transfers between devices, with_halo(): lax.ppermute(head, axis, [((i + 1) % count, i) for i in range(ends)])  9.11 us
    ppermute x2, starting transfers between devices, with_halo(): lax.ppermute(tail, axis, [(i, (i + 1) % count) for i in range(ends)])  8.74 us
  transfers between devices with their start and end apart: 6, of which 5 were waited for; matrix products, arithmetic and copies ran while one was open for 3% of the time, Pallas kernels for 0%

profile of v1, /device:TPU:25, one launch (start us, length us, event | category | flops | bytes accessed | tf_op | source)
XLA Modules:
  0.0 204.2 jit_solution(9535696548683976096)
XLA Ops:
  6.6 0.7 all-gather.2.cloned.1.call-update
  7.3 0.7 broadcast_compare_fusion.1
  8.0 0.7 broadcast_maximum_fusion
  8.8 1.4 gather_fusion
  10.4 0.8 reduce_window_sum.11
  11.3 0.4 select_reduce_fusion.1
  12.1 0.6 all_to_all.11
  12.7 6.6 %all-to-all-start = ((f32[16,1,132]{2,1,0:T(1,128)}), f32[16,1,132]{2,1,0:T(1,128)S(1)}, u32[]{:S(2)}, u32[]{:S(2)}) async-start(f32[16,1,132]{2,1,0:T(1,128)} %all_to_all.11), calls=%async_computation | async-start | bytes 32768 | tf_op jit(solution)/shard_map/all_to_all | solution.py:208
  19.6 15.1 %all_gather.7 = f32[128,256]{1,0:T(8,128)S(1)} all-gather(f32[16,256]{1,0:T(8,128)S(1)} %bitcast.21), channel_id=1, replica_groups=mesh['lon'=8,'lat'=16] {'lon'}, dimensions={0}, use_global_device_ids=true | all-gather | bytes 147456 | tf_op jit(solution)/shard_map/all_gather | solution.py:185
  34.9 27.2 %all-gather.2.cloned.1.call-done.y_ref = bf16[128,128,256]{2,1,0:T(8,128)(2,1)} async-done(((bf16[16,128,256]{2,1,0:T(8,128)(2,1)}), bf16[128,128,256]{2,1,0:T(8,128)(2,1)}) %all-gather.2.cloned.1.call-update) | async-done | bytes 8388624 | tf_op jit(solution)/shard_map/all_gather | solution.py:183
  62.1 3.4 %copy-done.3 = bf16[128,128,256]{2,1,0:T(8,128)(2,1)S(1)} copy-done((bf16[128,128,256]{2,1,0:T(8,128)(2,1)S(1)}, bf16[128,128,256]{2,1,0:T(8,128)(2,1)}, u32[]{:S(2)}) %copy-start.3) | copy-done | bytes 8388632
  65.5 22.4 %gram.1 = bf16[16,4,272,128]{3,2,1,0:T(8,128)(2,1)S(1)} custom-call(s32[16,68]{1,0:T(8,128)S(1)} %slice_convert_fusion.slots, f32[16,64]{1,0:T(8,128)S(1)} %slice.27.wts, bf16[128,128,256]{2,1,0:T(8,128)(2,1)S(1)} %copy-done.3, f32[128,2,128]{2,1,0:T(2,128)S(1)} %reshape.158.proj_ref), custom_call_target="tpu_custom_call" | custom-call | flops 4294967296 | bytes 13631488 | tf_op jit(solution)/shard_map/gram/pallas_call | solution.py:216
  87.9 57.6 %all_to_all.17.parts_ref = bf16[16,4,272,128]{3,2,1,0:T(8,128)(2,1)S(1)} all-to-all(bf16[16,4,272,128]{3,2,1,0:T(8,128)(2,1)S(1)} %gram.1), channel_id=1, replica_groups=mesh['lon'=8,'lat'=16] {'lat'}, dimensions={0} | all-to-all | bytes 8912896 | tf_op jit(solution)/shard_map/all_to_all | solution.py:229
  145.5 12.9 %root.1 = bf16[4,256,256]{2,1,0:T(8,128)(2,1)S(1)} custom-call(bf16[16,4,272,128]{3,2,1,0:T(8,128)(2,1)S(1)} %all_to_all.17.parts_ref), custom_call_target="tpu_custom_call" | custom-call | flops 4831838208 | bytes 5242880 | tf_op jit(solution)/shard_map/root/pallas_call | solution.py:232
  158.5 3.2 %collective-permute-start = (bf16[2,1,256,256]{3,2,1,0:T(8,128)(2,1)S(1)}, bf16[2,1,256,256]{3,2,1,0:T(8,128)(2,1)S(1)}, u32[]{:S(2)}, u32[]{:S(2)}) collective-permute-start(bf16[2,1,256,256]{3,2,1,0:T(8,128)(2,1)S(1)} %get-tuple-element.9), channel_id=1, source_target_pairs={{0,1},{1,2},{2,3},{3,4},{4,5},{5,6},{6,7},{7,8},{8,9},{9,10},{10,1... | collective-permute-start | bytes 786440 | tf_op jit(solution)/shard_map/ppermute | solution.py:155
  161.7 2.1 %collective-permute-start.1 = (bf16[2,1,256,256]{3,2,1,0:T(8,128)(2,1)S(1)}, bf16[2,1,256,256]{3,2,1,0:T(8,128)(2,1)S(1)}, u32[]{:S(2)}, u32[]{:S(2)}) collective-permute-start(bf16[2,1,256,256]{3,2,1,0:T(8,128)(2,1)S(1)} %get-tuple-element.10), channel_id=1, source_target_pairs={{1,0},{2,1},{3,2},{4,3},{5,4},{6,5},{7,6},{8,7},{9,8},{10,9},{11,1... | collective-permute-start | bytes 786440 | tf_op jit(solution)/shard_map/ppermute | solution.py:157
  163.8 3.0 %collective-permute-done = bf16[2,1,256,256]{3,2,1,0:T(8,128)(2,1)S(1)} collective-permute-done((bf16[2,1,256,256]{3,2,1,0:T(8,128)(2,1)S(1)}, bf16[2,1,256,256]{3,2,1,0:T(8,128)(2,1)S(1)}, u32[]{:S(2)}, u32[]{:S(2)}) %collective-permute-start) | collective-permute-done | bytes 262176 | tf_op jit(solution)/shard_map/ppermute | solution.py:155
  166.8 4.7 %collective-permute-done.1 = bf16[2,1,256,256]{3,2,1,0:T(8,128)(2,1)S(1)} collective-permute-done((bf16[2,1,256,256]{3,2,1,0:T(8,128)(2,1)S(1)}, bf16[2,1,256,256]{3,2,1,0:T(8,128)(2,1)S(1)}, u32[]{:S(2)}, u32[]{:S(2)}) %collective-permute-start.1) | collective-permute-done | bytes 262176 | tf_op jit(solution)/shard_map/ppermute | solution.py:157
  171.7 5.5 %collective-permute-start.2 = (bf16[1,4,256,256]{3,2,1,0:T(8,128)(2,1)S(1)}, bf16[1,4,256,256]{3,2,1,0:T(8,128)(2,1)S(1)}, u32[]{:S(2)}, u32[]{:S(2)}) collective-permute-start(bf16[1,4,256,256]{3,2,1,0:T(8,128)(2,1)S(1)} %get-tuple-element.7), channel_id=1, source_target_pairs={{0,16},{16,32},{32,48},{48,64},{64,80},{80,96},{96,112},{1,17},{17... | collective-permute-start | bytes 1572872 | tf_op jit(solution)/shard_map/ppermute | solution.py:155
  177.2 1.9 collective-permute-start.3
  179.3 4.0 %collective-permute-done.2 = bf16[1,4,256,256]{3,2,1,0:T(8,128)(2,1)S(1)} collective-permute-done((bf16[1,4,256,256]{3,2,1,0:T(8,128)(2,1)S(1)}, bf16[1,4,256,256]{3,2,1,0:T(8,128)(2,1)S(1)}, u32[]{:S(2)}, u32[]{:S(2)}) %collective-permute-start.2) | collective-permute-done | bytes 524320 | tf_op jit(solution)/shard_map/ppermute | solution.py:155
  183.3 4.4 %collective-permute-done.3 = bf16[1,4,256,256]{3,2,1,0:T(8,128)(2,1)S(1)} collective-permute-done((bf16[1,4,256,256]{3,2,1,0:T(8,128)(2,1)S(1)}, bf16[1,4,256,256]{3,2,1,0:T(8,128)(2,1)S(1)}, u32[]{:S(2)}, u32[]{:S(2)}) %collective-permute-start.3) | collective-permute-done | bytes 524320 | tf_op jit(solution)/shard_map/ppermute | solution.py:157
  187.7 0.3 pad_maximum_fusion
  188.0 9.3 %state.1 = bf16[16,512,256]{2,1,0:T(8,128)(2,1)} custom-call(s32[16,4]{1,0:T(8,128)S(1)} %fusion.4.places, f32[16,4]{1,0:T(8,128)S(1)} %bitcast.20, f32[16,1,512]{2,1,0:T(1,128)S(1)} %reshape.154.mean_ref, bf16[16,512,256]{2,1,0:T(8,128)(2,1)S(1)} %bitcast.19, bf16[16,256,256]{2,1,0:T(8,128)(2,1)S(1)} %bitcast.15), custom_call_target="tpu_custom_call" | custom-call | flops 1073741824 | bytes 11534336 | tf_op jit(solution)/shard_map/state/pallas_call | solution.py:255
  (45 shorter events, 1.5 us)
Async XLA Ops:
  6.5 2.2 %copy-start = (s32[2048]{0:T(1024)S(1)}, s32[2048]{0:T(1024)}, u32[]{:S(2)}) copy-start(s32[2048]{0:T(1024)} %param.11) | copy-start | bytes 24580
  6.5 12.8 %copy-start.4 = (bf16[16,128,256]{2,1,0:T(8,128)(2,1)S(1)}, bf16[16,128,256]{2,1,0:T(8,128)(2,1)}, u32[]{:S(2)}) copy-start(bf16[16,128,256]{2,1,0:T(8,128)(2,1)} %param.9) | copy-start | bytes 3145732
  6.5 4.7 %copy-start.8 = (f32[2,2,48]{2,1,0:T(2,128)S(1)}, f32[2,2,48]{2,1,0:T(2,128)}, u32[]{:S(2)}) copy-start(f32[2,2,48]{2,1,0:T(2,128)} %param.13) | copy-start | bytes 2308
  6.5 12.8 %copy-start.6 = (bf16[16,128]{1,0:T(8,128)(2,1)S(1)}, bf16[16,128]{1,0:T(8,128)(2,1)}, u32[]{:S(2)}) copy-start(bf16[16,128]{1,0:T(8,128)(2,1)} %param.10) | copy-start | bytes 12292
  6.5 55.6 %all-gather.2.cloned.1.call-start = ((), (), s32[]{:S(2)}) async-start(), calls=%async_computation.2 | async-start | bytes 9437184 | tf_op jit(solution)/shard_map/all_gather | solution.py:183
  12.7 22.1 %all-to-all-start = ((f32[16,1,132]{2,1,0:T(1,128)}), f32[16,1,132]{2,1,0:T(1,128)S(1)}, u32[]{:S(2)}, u32[]{:S(2)}) async-start(f32[16,1,132]{2,1,0:T(1,128)} %all_to_all.11), calls=%async_computation | async-start | bytes 32768 | tf_op jit(solution)/shard_map/all_to_all | solution.py:208
  62.1 3.4 %copy-start.3 = (bf16[128,128,256]{2,1,0:T(8,128)(2,1)S(1)}, bf16[128,128,256]{2,1,0:T(8,128)(2,1)}, u32[]{:S(2)}) copy-start(bf16[128,128,256]{2,1,0:T(8,128)(2,1)} %all-gather.2.cloned.1.call-done.y_ref) | copy-start | bytes 25165828
  158.5 8.3 %collective-permute-start = (bf16[2,1,256,256]{3,2,1,0:T(8,128)(2,1)S(1)}, bf16[2,1,256,256]{3,2,1,0:T(8,128)(2,1)S(1)}, u32[]{:S(2)}, u32[]{:S(2)}) collective-permute-start(bf16[2,1,256,256]{3,2,1,0:T(8,128)(2,1)S(1)} %get-tuple-element.9), channel_id=1, source_target_pairs={{0,1},{1,2},{2,3},{3,4},{4,5},{5,6},{6,7},{7,8},{8,9},{9,10},{10,1... | collective-permute-start | bytes 786440 | tf_op jit(solution)/shard_map/ppermute | solution.py:155
  161.7 17.5 %copy-start.5 = (f32[4,4,512]{2,1,0:T(4,128)S(1)}, f32[4,4,512]{2,1,0:T(4,128)}, u32[]{:S(2)}) copy-start(f32[4,4,512]{2,1,0:T(4,128)} %param.14) | copy-start | bytes 98308
  161.7 17.5 %copy-start.7 = (s32[4,4,4]{2,1,0:T(4,128)S(1)}, s32[4,4,4]{2,1,0:T(4,128)}, u32[]{:S(2)}) copy-start(s32[4,4,4]{2,1,0:T(4,128)} %param.16) | copy-start | bytes 772
  161.7 9.8 %collective-permute-start.1 = (bf16[2,1,256,256]{3,2,1,0:T(8,128)(2,1)S(1)}, bf16[2,1,256,256]{3,2,1,0:T(8,128)(2,1)S(1)}, u32[]{:S(2)}, u32[]{:S(2)}) collective-permute-start(bf16[2,1,256,256]{3,2,1,0:T(8,128)(2,1)S(1)} %get-tuple-element.10), channel_id=1, source_target_pairs={{1,0},{2,1},{3,2},{4,3},{5,4},{6,5},{7,6},{8,7},{9,8},{10,9},{11,1... | collective-permute-start | bytes 786440 | tf_op jit(solution)/shard_map/ppermute | solution.py:157
  171.7 11.6 %collective-permute-start.2 = (bf16[1,4,256,256]{3,2,1,0:T(8,128)(2,1)S(1)}, bf16[1,4,256,256]{3,2,1,0:T(8,128)(2,1)S(1)}, u32[]{:S(2)}, u32[]{:S(2)}) collective-permute-start(bf16[1,4,256,256]{3,2,1,0:T(8,128)(2,1)S(1)} %get-tuple-element.7), channel_id=1, source_target_pairs={{0,16},{16,32},{32,48},{48,64},{64,80},{80,96},{96,112},{1,17},{17... | collective-permute-start | bytes 1572872 | tf_op jit(solution)/shard_map/ppermute | solution.py:155
  177.2 10.5 %collective-permute-start.3 = (bf16[1,4,256,256]{3,2,1,0:T(8,128)(2,1)S(1)}, bf16[1,4,256,256]{3,2,1,0:T(8,128)(2,1)S(1)}, u32[]{:S(2)}, u32[]{:S(2)}) collective-permute-start(bf16[1,4,256,256]{3,2,1,0:T(8,128)(2,1)S(1)} %get-tuple-element.8), channel_id=1, source_target_pairs={{16,0},{32,16},{48,32},{64,48},{80,64},{96,80},{112,96},{17,1},{33... | collective-permute-start | bytes 1572872 | tf_op jit(solution)/shard_map/ppermute | solution.py:157
  179.2 8.8 %copy-start.2 = (f32[4,4,4]{2,1,0:T(4,128)S(1)}, f32[4,4,4]{2,1,0:T(4,128)}, u32[]{:S(2)}) copy-start(f32[4,4,4]{2,1,0:T(4,128)} %param.17) | copy-start | bytes 772
  179.3 8.8 %copy-start.1 = (bf16[4,4,512,256]{3,2,1,0:T(8,128)(2,1)S(1)}, bf16[4,4,512,256]{3,2,1,0:T(8,128)(2,1)}, u32[]{:S(2)}) copy-start(bf16[4,4,512,256]{3,2,1,0:T(8,128)(2,1)} %param.15) | copy-start | bytes 12582916
Sparse Core Ops, SparseCore 0:
  9.1 52.9 all-gather.1

commit v2 on v1

v2 whole, which is shorter than its diff:
```python
import functools

import jax
import jax.numpy as jnp
from jax import lax
from jax.experimental import pallas as pl
from jax.experimental.pallas import tpu as pltpu
from jax.sharding import PartitionSpec as P

ITERS = 5
FAST = 4
TAIL = 16
SIDE = 4
bf16 = jnp.bfloat16
f32 = jnp.float32
highest = lax.Precision.HIGHEST


def split(x):
    hi = x.astype(bf16)
    return hi, (x - hi.astype(f32)).astype(bf16)


def mm(a, b):
    left = jnp.concatenate([a[0], a[0], a[1]], axis=1)
    right = jnp.concatenate([b[0], b[1], b[0]], axis=0)
    return jnp.dot(left, right, preferred_element_type=f32)


def places_of(half):
    row = lax.broadcasted_iota(jnp.int32, (half, half), 0)
    col = lax.broadcasted_iota(jnp.int32, (half, half), 1)
    return row, col


def pack(matrix, vector_rows):
    half = matrix.shape[0] // 2
    row, col = places_of(half)
    lower_right = matrix[half:, half:]
    both = jnp.where(row >= col, matrix[:half, :half], lower_right)
    diagonal = jnp.sum(jnp.where(row == col, lower_right, 0.0), axis=0, keepdims=True)
    hi = diagonal.astype(bf16).astype(f32)
    tail = jnp.concatenate(
        [hi, diagonal - hi, vector_rows, jnp.zeros((TAIL - 6, half), f32)], axis=0
    )
    return matrix[half:, :half].astype(bf16), both.astype(bf16), tail.astype(bf16)


def unpack(total):
    half = total.shape[1]
    members = 2 * half
    row, col = places_of(half)
    corner = total[:half]
    both = total[half:members]
    turned = both.T
    diagonal = total[members : members + 1] + total[members + 1 : members + 2]
    upper_left = jnp.where(row >= col, both, turned)
    lower_right = jnp.where(
        row == col, jnp.broadcast_to(diagonal, (half, half)), jnp.where(row < col, both, turned)
    )
    matrix = jnp.concatenate(
        [
            jnp.concatenate([upper_left, corner.T], axis=1),
            jnp.concatenate([corner, lower_right], axis=1),
        ],
        axis=0,
    )
    vector = jnp.concatenate(
        [
            total[members + 2 + h : members + 3 + h] + total[members + 4 + h : members + 5 + h]
            for h in range(2)
        ],
        axis=1,
    )
    return matrix, vector


def vector_rows(vector, half):
    hi = vector.astype(bf16).astype(f32)
    lo = vector - hi
    return jnp.concatenate([hi[:, :half], hi[:, half:], lo[:, :half], lo[:, half:]], axis=0)


def gram_kernel(points, ranks, order, slots, wts, y_ref, drive_ref, a_ref, b_ref, acc_ref):
    step = pl.program_id(0)
    half = y_ref.shape[2] // 2
    units = [(order[0, step], p, a_ref) for p in range(0, points, 2)]
    units += [(order[1, step], p, b_ref) for p in range(1, points, 2)]
    most = jnp.int32(0)
    for u, (dest, p, _) in enumerate(units):
        at = p * ranks
        ys = [y_ref[slots[dest, at + k]] for k in range(FAST)]
        yw = [(ys[k].astype(f32) * wts[dest, at + k]).astype(bf16) for k in range(FAST)]
        acc_ref[u] = lax.dot_general(
            jnp.concatenate(yw, axis=0),
            jnp.concatenate(ys, axis=0),
            (((0,), (0,)), ((), ())),
            preferred_element_type=f32,
        )
        most = jnp.maximum(most, slots[dest, points * ranks + p])

    @pl.when(most > FAST)
    def _():
        for u, (dest, p, _) in enumerate(units):
            at = p * ranks

            @pl.loop(FAST, jnp.maximum(slots[dest, points * ranks + p], FAST))
            def _(k):
                y = y_ref[slots[dest, at + k]]
                w = (y.astype(f32) * wts[dest, at + k]).astype(bf16)
                acc_ref[u] += lax.dot_general(
                    w, y, (((0,), (0,)), ((), ())), preferred_element_type=f32
                )

    for u, (dest, p, o_ref) in enumerate(units):
        corner, both, tail = pack(acc_ref[u], drive_ref[dest, p])
        o_ref[0, p // 2, :half] = corner
        o_ref[0, p // 2, half : 2 * half] = both
        o_ref[0, p // 2, 2 * half :] = tail


def root_kernel(firsts, *refs):
    o_ref = refs[-1]
    parts = [r.at[0] for r in refs[:firsts]] + list(refs[firsts:-1])
    points, rows, half = o_ref.shape
    members = 2 * half
    eye = (
        lax.broadcasted_iota(jnp.int32, (members, members), 0)
        == lax.broadcasted_iota(jnp.int32, (members, members), 1)
    ).astype(f32)
    scale = 1.0 / (members - 1)
    for p in range(points):
        total = parts[0][p].astype(f32)
        for part in parts[1:]:
            total = total + part[p].astype(f32)
        cov, drive = unpack(total)
        drive = drive * scale
        system = eye + cov * scale
        bound = jnp.max(jnp.sum(jnp.abs(system), axis=0, keepdims=True), axis=1, keepdims=True)
        upper = system * (1.0 / bound)
        lower = 1.5 * eye - 0.5 * upper
        lower_s = split(lower)
        upper_s = split(mm(split(upper), lower_s))
        for sweep in range(1, ITERS):
            factor_s = split(1.5 * eye - 0.5 * mm(lower_s, upper_s))
            if sweep < ITERS - 1:
                upper_s = split(mm(upper_s, factor_s))
            lower = mm(factor_s, lower_s)
            lower_s = split(lower)
        root = lower * lax.rsqrt(bound)
        root_s = split(root)
        once = mm(split(jnp.broadcast_to(drive, (16, members))), root_s)
        shift = mm(split(once), root_s)[:1]
        corner, both, tail = pack(root, vector_rows(shift, half))
        o_ref[p, :half] = corner
        o_ref[p, half:members] = both
        o_ref[p, members:] = tail


def state_kernel(places, mixing, mean_ref, pert_ref, w_ref, o_ref):
    step = pl.program_id(0)
    count, cells, members = o_ref.shape
    for t in range(count):
        tile = step * count + t
        total = mixing[tile, 0] * w_ref[places[tile, 0]].astype(f32)
        for j in range(1, 4):
            total = total + mixing[tile, j] * w_ref[places[tile, j]].astype(f32)
        root, shift = unpack(total)
        shift = jnp.broadcast_to(shift, (8, members)).T[:, :1]
        moved = jnp.dot(pert_ref[t], (root + shift).astype(bf16), preferred_element_type=f32)
        mean = jnp.broadcast_to(mean_ref[t], (8, cells)).T[:, :1]
        o_ref[t] = (mean + moved).astype(bf16)


def column_of(rows):
    size = lax.axis_size("lon")
    up = [(i, (i + 2) % size) for i in range(size)]
    down = [(i, (i - 2) % size) for i in range(size)]
    cut = rows.shape[0] // 2

    def send(x, pairs):
        return lax.ppermute(x, "lon", pairs)

    def swap(x):
        return lax.ppermute(x, "lon", [(i, i ^ 1) for i in range(size)])

    below = send(rows, up)
    above = send(rows, down)
    far_a = send(below[:cut], up)
    far_b = send(above[cut:], down)
    mine = [rows, above, far_a, far_b, below]
    return jnp.concatenate(mine + [swap(x) for x in mine], axis=0)


def turn(along, k):
    pairs = []
    for x in range(SIDE):
        for y in range(SIDE):
            if along == "y":
                pairs.append((x * SIDE + y, x * SIDE + (y + k) % SIDE))
            else:
                pairs.append((x * SIDE + y, (x + k) % SIDE * SIDE + y))
    return pairs


def local(
    obs_rows,
    innovations,
    obs_home,
    obs_lists,
    loc_weights,
    state_mean,
    state_perturb,
    interp_ids,
    interp_wts,
):
    lon_count = lax.axis_size("lon")
    lat_count = lax.axis_size("lat")
    lon = lax.axis_index("lon")
    lat = lax.axis_index("lat")
    held, obs_count, members = obs_rows.shape
    half = members // 2
    point_rows, point_cols, list_len = obs_lists.shape
    points = point_rows * point_cols
    ranks = 2 * lon_count
    column_blocks = lon_count * held

    column_rows = column_of(obs_rows)
    project = jnp.einsum("lok,lo->lk", obs_rows, innovations, preferred_element_type=f32)
    column_proj = lax.all_gather(project, "lon", tiled=True)

    ids = obs_lists.reshape(points, list_len)
    live = ids >= 0
    home = jnp.take(obs_home, jnp.maximum(ids, 0))
    column = jnp.where(live, home // held % lat_count, lat_count)
    slot = home // (held * lat_count) * held + home % held
    mask = column[None] == jnp.arange(lat_count, dtype=jnp.int32)[:, None, None]
    rank = jnp.cumsum(mask.astype(jnp.int32), axis=2) - 1
    chosen = mask[..., None] & (rank[..., None] == jnp.arange(ranks, dtype=jnp.int32))
    slots_f = jnp.sum(jnp.where(chosen, slot.astype(f32)[None, :, :, None], 0.0), axis=2)
    wts_f = jnp.sum(
        jnp.where(chosen, loc_weights.reshape(1, points, list_len, 1), 0.0), axis=2
    )
    counts = jnp.sum(mask.astype(f32), axis=2)
    asked = jnp.concatenate(
        [
            slots_f.reshape(lat_count, points * ranks),
            counts,
            wts_f.reshape(lat_count, points * ranks),
        ],
        axis=1,
    )
    asked = lax.all_to_all(asked, "lat", 0, 0, tiled=True)
    cut = points * ranks + points
    wts = asked[:, cut:]
    named = asked[:, : points * ranks].astype(jnp.int32)
    from_lon = named // held
    apart = (from_lon // 2 - lon // 2) % (lon_count // 2) + (lon_count // 2) * (
        (from_lon + lon) % 2
    )
    slots = jnp.concatenate(
        [apart * held + named % held, asked[:, points * ranks : cut].astype(jnp.int32)], axis=1
    )

    spread = jnp.sum(
        jnp.where(
            named.reshape(lat_count * points, ranks, 1)
            == jnp.arange(column_blocks, dtype=jnp.int32),
            wts.reshape(lat_count * points, ranks, 1),
            0.0,
        ),
        axis=1,
    )
    drive = jnp.dot(spread, column_proj, precision=highest)
    drive_hi = drive.astype(bf16).astype(f32)
    drive_rows = jnp.concatenate(
        [v.reshape(lat_count, points, 2, half) for v in (drive_hi, drive - drive_hi)], axis=2
    )

    smem = pl.BlockSpec(memory_space=pltpu.SMEM)
    vmem = pl.BlockSpec(memory_space=pltpu.VMEM)
    rows = members + TAIL
    each = points // 2
    x, y = lat // SIDE, lat % SIDE
    others = jnp.arange(SIDE, dtype=jnp.int32)

    def gram(k):
        order = jnp.stack(
            [
                (x + others) % SIDE * SIDE + (y + k) % SIDE,
                (x + k) % SIDE * SIDE + (y + others) % SIDE,
            ]
        )
        shape = jax.ShapeDtypeStruct((SIDE, each, rows, half), bf16)
        block = pl.BlockSpec((1, each, rows, half), lambda i: (i, 0, 0, 0))
        return pl.pallas_call(
            functools.partial(gram_kernel, points, ranks),
            grid=(SIDE,),
            out_shape=(shape, shape),
            in_specs=[smem, smem, smem, vmem, vmem],
            out_specs=(block, block),
            scratch_shapes=[pltpu.VMEM((points, members, members), f32)],
            compiler_params=pltpu.CompilerParams(vmem_limit_bytes=24 << 20),
            cost_estimate=pl.CostEstimate(
                flops=2 * 16 * 512 * 256 * 256, bytes_accessed=10 << 20, transcendentals=0
            ),
            name="gram",
        )(order, slots, wts, column_rows, drive_rows)

    first = {0: [None, None]}
    kept = {}
    for k in (2, 1, 3):
        to_y, to_x = gram(k)
        first[k] = [
            lax.ppermute(to_y, "lat", turn("y", k)),
            lax.ppermute(to_x, "lat", turn("x", k)),
        ]
    first[0] = list(gram(0))

    def second(side, along):
        got = []
        for k in (2, 1, 3):
            total = first[0][side][k].astype(f32)
            for j in (1, 3, 2):
                total = total + first[j][side][k].astype(f32)
            got.append(lax.ppermute(total.astype(bf16), "lat", turn(along, k)))
        return got

    seconds = [second(0, "x"), second(1, "y")]

    def root(side):
        firsts = [first[j][side] for j in (0, 1, 3, 2)]
        one = pl.BlockSpec((1, each, rows, half), lambda i: (0, 0, 0, 0))
        whole = pl.BlockSpec((each, rows, half), lambda i: (0, 0, 0))
        return pl.pallas_call(
            functools.partial(root_kernel, len(firsts)),
            grid=(1,),
            out_shape=jax.ShapeDtypeStruct((each, rows, half), bf16),
            in_specs=[one] * len(firsts) + [whole] * len(seconds[side]),
            out_specs=whole,
            compiler_params=pltpu.CompilerParams(vmem_limit_bytes=24 << 20),
            cost_estimate=pl.CostEstimate(
                flops=2 * 36 * 2 * 256**3, bytes_accessed=2 << 20, transcendentals=0
            ),
            name="root",
        )(*firsts, *seconds[side])

    col_a = root(0)
    right = lax.ppermute(col_a, "lat", [(i + 1, i) for i in range(lat_count - 1)])
    col_b = root(1)
    left = lax.ppermute(col_b, "lat", [(i, i + 1) for i in range(lat_count - 1)])
    cols = [left, col_a, col_b, right]
    below = lax.ppermute(
        jnp.stack([c[0] for c in cols]), "lon", [(i + 1, i) for i in range(lon_count - 1)]
    )
    above = lax.ppermute(
        jnp.stack([c[1] for c in cols]), "lon", [(i, i + 1) for i in range(lon_count - 1)]
    )
    held_w = jnp.concatenate(cols + [above, below], axis=0)

    grid_cols = point_cols * lat_count
    tile_rows, tile_cols, cells = state_mean.shape
    tiles = tile_rows * tile_cols
    target_ids = interp_ids.reshape(tiles, 4)
    local_row = target_ids // grid_cols - lon * point_rows
    local_col = target_ids % grid_cols - lat * point_cols + 1
    places = jnp.where(
        local_row < 0,
        2 * 4 + local_col,
        jnp.where(local_row >= point_rows, 3 * 4 + local_col, local_col * 2 + local_row),
    )
    per = 2
    result = pl.pallas_call(
        state_kernel,
        grid=(tiles // per,),
        out_shape=jax.ShapeDtypeStruct((tiles, cells, members), bf16),
        in_specs=[
            smem,
            smem,
            pl.BlockSpec((per, 1, cells), lambda i: (i, 0, 0)),
            pl.BlockSpec((per, cells, members), lambda i: (i, 0, 0)),
            vmem,
        ],
        out_specs=pl.BlockSpec((per, cells, members), lambda i: (i, 0, 0)),
        compiler_params=pltpu.CompilerParams(vmem_limit_bytes=24 << 20),
        cost_estimate=pl.CostEstimate(
            flops=2 * 16 * 512 * 256 * 256, bytes_accessed=11 << 20, transcendentals=0
        ),
        name="state",
    )(
        places,
        interp_wts.reshape(tiles, 4),
        state_mean.reshape(tiles, 1, cells),
        state_perturb.reshape(tiles, cells, members),
        held_w,
    )
    return result.reshape(tile_rows, tile_cols, cells, members)


def solution(mesh):
    return jax.shard_map(
        local,
        mesh=mesh,
        in_specs=(
            P(("lon", "lat"), None, None),
            P(("lon", "lat"), None),
            P(),
            P("lon", "lat", None),
            P("lon", "lat", None),
            P("lon", "lat", None),
            P("lon", "lat", None, None),
            P("lon", "lat", None),
            P("lon", "lat", None),
        ),
        out_specs=P("lon", "lat", None, None),
        check_vma=False,
    )
```

time: 204 us -> 165 us (0.81); the launches traced: 204 us -> 163 us
  blocking collectives: 72.7 us -> 16.7 us
  starting transfers between devices: 19.4 us -> 47.1 us
  local copies, waits for them, and re-layouts: 6.28 us -> 22.9 us
  between operations: 13.6 us -> 0.46 us
  waiting for transfers between devices: 44.1 us -> 32.7 us
  Pallas kernels: 44.6 us -> 36.6 us
    all_to_all x1 -> x0, blocking collectives: 57.6 us -> none  [local(): parts = lax.all_to_all(partial, 'lat', 0, 0, tiled=True)]
    ppermute x4 -> x25, starting transfers between devices: 12.7 us -> 40.5 us  [the longest x6 13 us: second(): got.append(lax.ppermute(total.astype(bf16), 'lat', turn(along, k)))]
    all_gather x1 -> x0, waiting for transfers between devices: 27.2 us -> none  [local(): column_rows = lax.all_gather(obs_rows, 'lon', tiled=True)]
    ppermute x4 -> x25, waiting for transfers between devices: 16.1 us -> 32.7 us  [the longest x4 9.71 us: send(): return lax.ppermute(x, 'lon', pairs)]
    unnamed x19 -> x27, local copies, waits for them, and re-layouts: 3.42 us -> 18.1 us
    pallas_call x3 -> x7, Pallas kernels: 44.6 us -> 36.6 us  [the longest x4 15.7 us: gram(): pl.pallas_call(functools.partial(gram_kernel, points, ranks), grid=(SIDE,...]
  transfers between devices with their start and end apart: 6 -> 26, of which waited for: 5 -> 7; matrix products, arithmetic and copies ran while one was open for 3% -> 13% of each run, Pallas kernels for 0% -> 15%
where the time goes in v2:
time: 165 us; the launch traced here: 163 us
  starting transfers between devices  47.1 us (29%)
  Pallas kernels  36.6 us (22%)
  waiting for transfers between devices  32.7 us (20%)
  local copies, waits for them, and re-layouts  22.9 us (14%)
  blocking collectives  16.7 us (10%)
  other arithmetic  4.79 us (3%)
  matrix products  1.67 us (1%)
    unnamed x27, local copies, waits for them, and re-layouts  18.1 us
    all_gather x1, blocking collectives, local(): column_proj = lax.all_gather(project, 'lon', tiled=True)  16.7 us
    pallas_call x4, Pallas kernels, gram(): pl.pallas_call(functools.partial(gram_kernel, points, ranks), grid=(SIDE,...  15.7 us
    ppermute x6, starting transfers between devices, second(): got.append(lax.ppermute(total.astype(bf16), 'lat', turn(along, k)))  13 us
    pallas_call x2, Pallas kernels, root(): pl.pallas_call(functools.partial(root_kernel, len(firsts)), grid=(1,), ou...  12.9 us
    ppermute x4, waiting for transfers between devices, send(): return lax.ppermute(x, 'lon', pairs)  9.71 us
    pallas_call x1, Pallas kernels, local(): pl.pallas_call(state_kernel, grid=(tiles // per,), out_shape=jax.ShapeDty...  7.96 us
    all_to_all x1, starting transfers between devices, local(): asked = lax.all_to_all(asked, 'lat', 0, 0, tiled=True)  6.61 us
  transfers between devices with their start and end apart: 26, of which 7 were waited for; matrix products, arithmetic and copies ran while one was open for 13% of the time, Pallas kernels for 15%

profile of v2, /device:TPU:25, one launch (start us, length us, event | category | flops | bytes accessed | tf_op | source)
XLA Modules:
  0.0 163.0 jit_solution(18001368793683510237)
XLA Ops:
  0.0 3.8 %collective-permute-start = (bf16[16,128,256]{2,1,0:T(8,128)(2,1)}, bf16[16,128,256]{2,1,0:T(8,128)(2,1)S(1)}, u32[]{:S(2)}, u32[]{:S(2)}) collective-permute-start(bf16[16,128,256]{2,1,0:T(8,128)(2,1)} %param.9), channel_id=1, source_target_pairs={{0,96},{16,112},{32,0},{48,16},{64,32},{80,48},{96,64},{112,80},{1... | collective-permute-start | bytes 3145736 | tf_op jit(solution)/shard_map/ppermute | solution.py:182
  10.8 6.6 %all-to-all-start = ((f32[16,1,132]{2,1,0:T(1,128)}), f32[16,1,132]{2,1,0:T(1,128)S(1)}, u32[]{:S(2)}, u32[]{:S(2)}) async-start(f32[16,1,132]{2,1,0:T(1,128)} %all_to_all.8), calls=%async_computation | async-start | bytes 32768 | tf_op jit(solution)/shard_map/all_to_all | solution.py:253
  21.3 16.7 %all_gather.3 = f32[128,256]{1,0:T(8,128)S(1)} all-gather(f32[16,256]{1,0:T(8,128)S(1)} %bitcast.32), channel_id=1, replica_groups=mesh['lon'=8,'lat'=16] {'lon'}, dimensions={0}, use_global_device_ids=true | all-gather | bytes 147456 | tf_op jit(solution)/shard_map/all_gather | solution.py:230
  39.2 2.7 %collective-permute-start.3 = (bf16[8,128,256]{2,1,0:T(8,128)(2,1)S(1)}, bf16[8,128,256]{2,1,0:T(8,128)(2,1)S(1)}, u32[]{:S(2)}, u32[]{:S(2)}) collective-permute-start(bf16[8,128,256]{2,1,0:T(8,128)(2,1)S(1)} %slice.154), channel_id=1, source_target_pairs={{0,96},{16,112},{32,0},{48,16},{64,32},{80,48},{96,64},{112,80},{1... | collective-permute-start | bytes 1572872 | tf_op jit(solution)/shard_map/ppermute | solution.py:182
  44.0 9.7 %collective-permute-done.2 = bf16[8,128,256]{2,1,0:T(8,128)(2,1)S(1)} collective-permute-done((bf16[8,128,256]{2,1,0:T(8,128)(2,1)S(1)}, bf16[8,128,256]{2,1,0:T(8,128)(2,1)S(1)}, u32[]{:S(2)}, u32[]{:S(2)}) %collective-permute-start.2) | collective-permute-done | bytes 524320 | tf_op jit(solution)/shard_map/ppermute | solution.py:182
  57.4 2.3 %constant_dynamic-update-slice_fusion.4 = bf16[128,128,256]{2,1,0:T(8,128)(2,1)} fusion(bf16[128,128,256]{2,1,0:T(8,128)(2,1)} %constant_dynamic-update-slice_fusion.5, bf16[16,128,256]{2,1,0:T(8,128)(2,1)} %collective-permute-done.4), kind=kLoop, calls=%fused_computation.26 | loop fusion | bytes 2097152
  63.6 3.4 %copy-done.1 = bf16[128,128,256]{2,1,0:T(8,128)(2,1)S(1)} copy-done((bf16[128,128,256]{2,1,0:T(8,128)(2,1)S(1)}, bf16[128,128,256]{2,1,0:T(8,128)(2,1)}, u32[]{:S(2)}) %copy-start.1) | copy-done | bytes 8388632
  67.0 3.9 %gram.5 = (bf16[4,2,272,128]{3,2,1,0:T(8,128)(2,1)S(1)}, bf16[4,2,272,128]{3,2,1,0:T(8,128)(2,1)}) custom-call(s32[2,4]{1,0:T(2,128)S(1)} %pad_add_fusion.2.order, s32[16,68]{1,0:T(8,128)S(1)} %pad_add_fusion.slots, f32[16,64]{1,0:T(8,128)S(1)} %get-tuple-element.40.wts, bf16[128,128,256]{2,1,0:T(8,128)(2,1)S(1)} %copy-done.1, ...), custom_call_target="tpu_custom_call" | custom-call | flops 1073741824 | bytes 10485760 | tf_op jit(solution)/shard_map/gram/pallas_call | solution.py:296
  72.1 3.9 %gram.6 = (bf16[4,2,272,128]{3,2,1,0:T(8,128)(2,1)S(1)}, bf16[4,2,272,128]{3,2,1,0:T(8,128)(2,1)}) custom-call(s32[2,4]{1,0:T(2,128)S(1)} %pad_add_fusion.3.order, s32[16,68]{1,0:T(8,128)S(1)} %pad_add_fusion.slots, f32[16,64]{1,0:T(8,128)S(1)} %get-tuple-element.40.wts, bf16[128,128,256]{2,1,0:T(8,128)(2,1)S(1)} %copy-done.1, ...), custom_call_target="tpu_custom_call" | custom-call | flops 1073741824 | bytes 10485760 | tf_op jit(solution)/shard_map/gram/pallas_call | solution.py:296
  77.5 4.4 %gram.7 = (bf16[4,2,272,128]{3,2,1,0:T(8,128)(2,1)S(1)}, bf16[4,2,272,128]{3,2,1,0:T(8,128)(2,1)}) custom-call(s32[2,4]{1,0:T(2,128)S(1)} %pad_add_fusion.4.order, s32[16,68]{1,0:T(8,128)S(1)} %pad_add_fusion.slots, f32[16,64]{1,0:T(8,128)S(1)} %get-tuple-element.40.wts, bf16[128,128,256]{2,1,0:T(8,128)(2,1)S(1)} %copy-done.1, ...), custom_call_target="tpu_custom_call" | custom-call | flops 1073741824 | bytes 10485760 | tf_op jit(solution)/shard_map/gram/pallas_call | solution.py:296
  87.0 3.4 %copy-done.2 = bf16[128,128,256]{2,1,0:T(8,128)(2,1)S(1)} copy-done((bf16[128,128,256]{2,1,0:T(8,128)(2,1)S(1)}, bf16[128,128,256]{2,1,0:T(8,128)(2,1)}, u32[]{:S(2)}) %copy-start.2) | copy-done | bytes 8388632
  90.4 3.5 %gram.4 = (bf16[4,2,272,128]{3,2,1,0:T(8,128)(2,1)S(1)}, bf16[4,2,272,128]{3,2,1,0:T(8,128)(2,1)S(1)}) custom-call(s32[2,4]{1,0:T(2,128)S(1)} %pad_add_fusion.1.order, s32[16,68]{1,0:T(8,128)S(1)} %pad_add_fusion.slots, f32[16,64]{1,0:T(8,128)S(1)} %get-tuple-element.40.wts, bf16[128,128,256]{2,1,0:T(8,128)(2,1)S(1)} %copy-done.2, ...), custom_call_target="tpu_custom_call" | custom-call | flops 1073741824 | bytes 10485760 | tf_op jit(solution)/shard_map/gram/pallas_call | solution.py:296
  93.9 4.5 %collective-permute-done.11.refs_3_ = bf16[4,2,272,128]{3,2,1,0:T(8,128)(2,1)S(1)} collective-permute-done((bf16[4,2,272,128]{3,2,1,0:T(8,128)(2,1)}, bf16[4,2,272,128]{3,2,1,0:T(8,128)(2,1)S(1)}, u32[]{:S(2)}, u32[]{:S(2)}) %collective-permute-start.11) | collective-permute-done | bytes 557088 | tf_op jit(solution)/shard_map/ppermute | solution.py:316
  100.2 3.0 %collective-permute-start.13 = (bf16[2,272,128]{2,1,0:T(8,128)(2,1)S(1)}, bf16[2,272,128]{2,1,0:T(8,128)(2,1)S(1)}, u32[]{:S(2)}, u32[]{:S(2)}) collective-permute-start(bf16[2,272,128]{2,1,0:T(8,128)(2,1)S(1)} %get-tuple-element.27), channel_id=1, source_target_pairs={{0,1},{1,2},{2,3},{3,0},{4,5},{5,6},{6,7},{7,4},{8,9},{9,10},{10,1... | collective-permute-start | bytes 417800 | tf_op jit(solution)/shard_map/ppermute | solution.py:326
  103.7 5.7 %collective-permute-done.18.refs_3_ = bf16[4,2,272,128]{3,2,1,0:T(8,128)(2,1)S(1)} collective-permute-done((bf16[4,2,272,128]{3,2,1,0:T(8,128)(2,1)S(1)}, bf16[4,2,272,128]{3,2,1,0:T(8,128)(2,1)S(1)}, u32[]{:S(2)}, u32[]{:S(2)}) %collective-permute-start.18) | collective-permute-done | bytes 557088 | tf_op jit(solution)/shard_map/ppermute | solution.py:315
  109.6 2.6 %collective-permute-start.19 = (bf16[2,272,128]{2,1,0:T(8,128)(2,1)S(1)}, bf16[2,272,128]{2,1,0:T(8,128)(2,1)S(1)}, u32[]{:S(2)}, u32[]{:S(2)}) collective-permute-start(bf16[2,272,128]{2,1,0:T(8,128)(2,1)S(1)} %get-tuple-element.25), channel_id=1, source_target_pairs={{0,8},{1,9},{2,10},{3,11},{4,12},{5,13},{6,14},{7,15},{8,0},{9,1},... | collective-permute-start | bytes 417800 | tf_op jit(solution)/shard_map/ppermute | solution.py:326
  112.2 5.3 %collective-permute-start.20 = (bf16[2,272,128]{2,1,0:T(8,128)(2,1)S(1)}, bf16[2,272,128]{2,1,0:T(8,128)(2,1)S(1)}, u32[]{:S(2)}, u32[]{:S(2)}) collective-permute-start(bf16[2,272,128]{2,1,0:T(8,128)(2,1)S(1)} %get-tuple-element.24), channel_id=1, source_target_pairs={{0,4},{1,5},{2,6},{3,7},{4,8},{5,9},{6,10},{7,11},{8,12},{9,13},{1... | collective-permute-start | bytes 417800 | tf_op jit(solution)/shard_map/ppermute | solution.py:326
  118.1 6.4 %root.2 = bf16[2,272,128]{2,1,0:T(8,128)(2,1)S(1)} custom-call(bf16[4,2,272,128]{3,2,1,0:T(8,128)(2,1)S(1)} %get-tuple-element.13.refs_0_, bf16[4,2,272,128]{3,2,1,0:T(8,128)(2,1)S(1)} %collective-permute-done.9.refs_1_, bf16[4,2,272,128]{3,2,1,0:T(8,128)(2,1)S(1)} %collective-permute-done.10.refs_2_, ...), custom_call_target="tpu_custom_call" | custom-call | flops 2415919104 | bytes 2097152 | tf_op jit(solution)/shard_map/root/pallas_call | solution.py:335
  124.5 3.8 %collective-permute-start.15 = (bf16[2,272,128]{2,1,0:T(8,128)(2,1)S(1)}, bf16[2,272,128]{2,1,0:T(8,128)(2,1)S(1)}, u32[]{:S(2)}, u32[]{:S(2)}) collective-permute-start(bf16[2,272,128]{2,1,0:T(8,128)(2,1)S(1)} %root.2), channel_id=1, source_target_pairs={{0,1},{1,2},{2,3},{3,4},{4,5},{5,6},{6,7},{7,8},{8,9},{9,10},{10,1... | collective-permute-start | bytes 417800 | tf_op jit(solution)/shard_map/ppermute | solution.py:351
  128.4 6.4 %root.3 = bf16[2,272,128]{2,1,0:T(8,128)(2,1)S(1)} custom-call(bf16[4,2,272,128]{3,2,1,0:T(8,128)(2,1)S(1)} %get-tuple-element.17.refs_0_, bf16[4,2,272,128]{3,2,1,0:T(8,128)(2,1)S(1)} %collective-permute-done.16.refs_1_, bf16[4,2,272,128]{3,2,1,0:T(8,128)(2,1)S(1)} %collective-permute-done.17.refs_2_, ...), custom_call_target="tpu_custom_call" | custom-call | flops 2415919104 | bytes 2097152 | tf_op jit(solution)/shard_map/root/pallas_call | solution.py:335
  136.8 6.4 %collective-permute-done.22 = bf16[2,272,128]{2,1,0:T(8,128)(2,1)S(1)} collective-permute-done((bf16[2,272,128]{2,1,0:T(8,128)(2,1)S(1)}, bf16[2,272,128]{2,1,0:T(8,128)(2,1)S(1)}, u32[]{:S(2)}, u32[]{:S(2)}) %collective-permute-start.22) | collective-permute-done | bytes 139296 | tf_op jit(solution)/shard_map/ppermute | solution.py:349
  143.3 3.7 %collective-permute-start.23 = (bf16[4,272,128]{2,1,0:T(8,128)(2,1)S(1)}, bf16[4,272,128]{2,1,0:T(8,128)(2,1)S(1)}, u32[]{:S(2)}, u32[]{:S(2)}) collective-permute-start(bf16[4,272,128]{2,1,0:T(8,128)(2,1)S(1)} %pad_maximum_fusion), channel_id=1, source_target_pairs={{0,16},{16,32},{32,48},{48,64},{64,80},{80,96},{96,112},{1,17},{17... | collective-permute-start | bytes 835592 | tf_op jit(solution)/shard_map/ppermute | solution.py:356
  150.5 4.5 %collective-permute-done.24 = bf16[4,272,128]{2,1,0:T(8,128)(2,1)S(1)} collective-permute-done((bf16[4,272,128]{2,1,0:T(8,128)(2,1)S(1)}, bf16[4,272,128]{2,1,0:T(8,128)(2,1)S(1)}, u32[]{:S(2)}, u32[]{:S(2)}) %collective-permute-start.24) | collective-permute-done | bytes 278560 | tf_op jit(solution)/shard_map/ppermute | solution.py:353
  155.0 8.0 %state.1 = bf16[16,512,256]{2,1,0:T(8,128)(2,1)} custom-call(s32[16,4]{1,0:T(8,128)S(1)} %select_select_fusion.places, f32[16,4]{1,0:T(8,128)S(1)} %bitcast.28, f32[16,1,512]{2,1,0:T(1,128)S(1)} %reshape.316.mean_ref, bf16[16,512,256]{2,1,0:T(8,128)(2,1)S(1)} %bitcast.27, bf16[16,272,128]{2,1,0:T(8,128)(2,1)S(1)} %constant_dynamic-update-slice_fusion.10.w_ref), custom_call_target="tpu_custom_call" | custom-call | flops 1073741824 | bytes 11534336 | tf_op jit(solution)/shard_map/state/pallas_call | solution.py:373
  (119 shorter events, 37.9 us)
Async XLA Ops:
  0.0 39.1 %collective-permute-start = (bf16[16,128,256]{2,1,0:T(8,128)(2,1)}, bf16[16,128,256]{2,1,0:T(8,128)(2,1)S(1)}, u32[]{:S(2)}, u32[]{:S(2)}) collective-permute-start(bf16[16,128,256]{2,1,0:T(8,128)(2,1)} %param.9), channel_id=1, source_target_pairs={{0,96},{16,112},{32,0},{48,16},{64,32},{80,48},{96,64},{112,80},{1... | collective-permute-start | bytes 3145736 | tf_op jit(solution)/shard_map/ppermute | solution.py:182
  3.8 35.2 %collective-permute-start.1 = (bf16[16,128,256]{2,1,0:T(8,128)(2,1)}, bf16[16,128,256]{2,1,0:T(8,128)(2,1)S(1)}, u32[]{:S(2)}, u32[]{:S(2)}) collective-permute-start(bf16[16,128,256]{2,1,0:T(8,128)(2,1)} %param.9), channel_id=1, source_target_pairs={{0,32},{16,48},{32,64},{48,80},{64,96},{80,112},{96,0},{112,16},{1... | collective-permute-start | bytes 3145736 | tf_op jit(solution)/shard_map/ppermute | solution.py:182
  3.8 53.6 %collective-permute-start.4 = (bf16[16,128,256]{2,1,0:T(8,128)(2,1)}, bf16[16,128,256]{2,1,0:T(8,128)(2,1)}, u32[]{:S(2)}, u32[]{:S(2)}) collective-permute-start(bf16[16,128,256]{2,1,0:T(8,128)(2,1)} %param.9), channel_id=1, source_target_pairs={{0,16},{16,0},{32,48},{48,32},{64,80},{80,64},{96,112},{112,96},{1... | collective-permute-start | bytes 3145736 | tf_op jit(solution)/shard_map/ppermute | solution.py:185
  10.8 27.2 %all-to-all-start = ((f32[16,1,132]{2,1,0:T(1,128)}), f32[16,1,132]{2,1,0:T(1,128)S(1)}, u32[]{:S(2)}, u32[]{:S(2)}) async-start(f32[16,1,132]{2,1,0:T(1,128)} %all_to_all.8), calls=%async_computation | async-start | bytes 32768 | tf_op jit(solution)/shard_map/all_to_all | solution.py:253
  39.0 14.6 %collective-permute-start.2 = (bf16[8,128,256]{2,1,0:T(8,128)(2,1)S(1)}, bf16[8,128,256]{2,1,0:T(8,128)(2,1)S(1)}, u32[]{:S(2)}, u32[]{:S(2)}) collective-permute-start(bf16[8,128,256]{2,1,0:T(8,128)(2,1)S(1)} %slice.153), channel_id=1, source_target_pairs={{0,32},{16,48},{32,64},{48,80},{64,96},{80,112},{96,0},{112,16},{1... | collective-permute-start | bytes 1572872 | tf_op jit(solution)/shard_map/ppermute | solution.py:182
  39.2 15.5 %collective-permute-start.3 = (bf16[8,128,256]{2,1,0:T(8,128)(2,1)S(1)}, bf16[8,128,256]{2,1,0:T(8,128)(2,1)S(1)}, u32[]{:S(2)}, u32[]{:S(2)}) collective-permute-start(bf16[8,128,256]{2,1,0:T(8,128)(2,1)S(1)} %slice.154), channel_id=1, source_target_pairs={{0,96},{16,112},{32,0},{48,16},{64,32},{80,48},{96,64},{112,80},{1... | collective-permute-start | bytes 1572872 | tf_op jit(solution)/shard_map/ppermute | solution.py:182
  41.9 17.8 %collective-permute-start.5 = (bf16[16,128,256]{2,1,0:T(8,128)(2,1)S(1)}, bf16[16,128,256]{2,1,0:T(8,128)(2,1)S(1)}, u32[]{:S(2)}, u32[]{:S(2)}) collective-permute-start(bf16[16,128,256]{2,1,0:T(8,128)(2,1)S(1)} %collective-permute-done), channel_id=1, source_target_pairs={{0,16},{16,0},{32,48},{48,32},{64,80},{80,64},{96,112},{112,96},{1... | collective-permute-start | bytes 3145736 | tf_op jit(solution)/shard_map/ppermute | solution.py:185
  42.8 19.7 %collective-permute-start.8 = (bf16[16,128,256]{2,1,0:T(8,128)(2,1)S(1)}, bf16[16,128,256]{2,1,0:T(8,128)(2,1)S(1)}, u32[]{:S(2)}, u32[]{:S(2)}) collective-permute-start(bf16[16,128,256]{2,1,0:T(8,128)(2,1)S(1)} %collective-permute-done.1), channel_id=1, source_target_pairs={{0,16},{16,0},{32,48},{48,32},{64,80},{80,64},{96,112},{112,96},{1... | collective-permute-start | bytes 3145736 | tf_op jit(solution)/shard_map/ppermute | solution.py:185
  70.9 14.7 %collective-permute-start.9 = (bf16[4,2,272,128]{3,2,1,0:T(8,128)(2,1)}, bf16[4,2,272,128]{3,2,1,0:T(8,128)(2,1)S(1)}, u32[]{:S(2)}, u32[]{:S(2)}) collective-permute-start(bf16[4,2,272,128]{3,2,1,0:T(8,128)(2,1)} %get-tuple-element.14), channel_id=1, source_target_pairs={{0,4},{1,5},{2,6},{3,7},{4,8},{5,9},{6,10},{7,11},{8,12},{9,13},{1... | collective-permute-start | bytes 1671176 | tf_op jit(solution)/shard_map/ppermute | solution.py:316
  76.1 17.8 %collective-permute-start.10 = (bf16[4,2,272,128]{3,2,1,0:T(8,128)(2,1)}, bf16[4,2,272,128]{3,2,1,0:T(8,128)(2,1)S(1)}, u32[]{:S(2)}, u32[]{:S(2)}) collective-permute-start(bf16[4,2,272,128]{3,2,1,0:T(8,128)(2,1)} %get-tuple-element.15), channel_id=1, source_target_pairs={{0,12},{1,13},{2,14},{3,15},{4,0},{5,1},{6,2},{7,3},{8,4},{9,5},{1... | collective-permute-start | bytes 1671176 | tf_op jit(solution)/shard_map/ppermute | solution.py:316
  82.0 16.4 %collective-permute-start.11 = (bf16[4,2,272,128]{3,2,1,0:T(8,128)(2,1)}, bf16[4,2,272,128]{3,2,1,0:T(8,128)(2,1)S(1)}, u32[]{:S(2)}, u32[]{:S(2)}) collective-permute-start(bf16[4,2,272,128]{3,2,1,0:T(8,128)(2,1)} %get-tuple-element.16), channel_id=1, source_target_pairs={{0,8},{1,9},{2,10},{3,11},{4,12},{5,13},{6,14},{7,15},{8,0},{9,1},... | collective-permute-start | bytes 1671176 | tf_op jit(solution)/shard_map/ppermute | solution.py:316
  84.1 19.1 %collective-permute-start.16 = (bf16[4,2,272,128]{3,2,1,0:T(8,128)(2,1)S(1)}, bf16[4,2,272,128]{3,2,1,0:T(8,128)(2,1)S(1)}, u32[]{:S(2)}, u32[]{:S(2)}) collective-permute-start(bf16[4,2,272,128]{3,2,1,0:T(8,128)(2,1)S(1)} %get-tuple-element.18), channel_id=1, source_target_pairs={{0,1},{1,2},{2,3},{3,0},{4,5},{5,6},{6,7},{7,4},{8,9},{9,10},{10,1... | collective-permute-start | bytes 1671176 | tf_op jit(solution)/shard_map/ppermute | solution.py:315
  84.5 19.1 %collective-permute-start.17 = (bf16[4,2,272,128]{3,2,1,0:T(8,128)(2,1)S(1)}, bf16[4,2,272,128]{3,2,1,0:T(8,128)(2,1)S(1)}, u32[]{:S(2)}, u32[]{:S(2)}) collective-permute-start(bf16[4,2,272,128]{3,2,1,0:T(8,128)(2,1)S(1)} %get-tuple-element.19), channel_id=1, source_target_pairs={{0,3},{1,0},{2,1},{3,2},{4,7},{5,4},{6,5},{7,6},{8,11},{9,8},{10,9... | collective-permute-start | bytes 1671176 | tf_op jit(solution)/shard_map/ppermute | solution.py:315
  85.6 23.7 %collective-permute-start.18 = (bf16[4,2,272,128]{3,2,1,0:T(8,128)(2,1)S(1)}, bf16[4,2,272,128]{3,2,1,0:T(8,128)(2,1)S(1)}, u32[]{:S(2)}, u32[]{:S(2)}) collective-permute-start(bf16[4,2,272,128]{3,2,1,0:T(8,128)(2,1)S(1)} %get-tuple-element.20), channel_id=1, source_target_pairs={{0,2},{1,3},{2,0},{3,1},{4,6},{5,7},{6,4},{7,5},{8,10},{9,11},{10,... | collective-permute-start | bytes 1671176 | tf_op jit(solution)/shard_map/ppermute | solution.py:315
  98.6 18.9 %collective-permute-start.12 = (bf16[2,272,128]{2,1,0:T(8,128)(2,1)S(1)}, bf16[2,272,128]{2,1,0:T(8,128)(2,1)S(1)}, u32[]{:S(2)}, u32[]{:S(2)}) collective-permute-start(bf16[2,272,128]{2,1,0:T(8,128)(2,1)S(1)} %get-tuple-element.28), channel_id=1, source_target_pairs={{0,2},{1,3},{2,0},{3,1},{4,6},{5,7},{6,4},{7,5},{8,10},{9,11},{10,... | collective-permute-start | bytes 417800 | tf_op jit(solution)/shard_map/ppermute | solution.py:326
  100.2 17.3 %collective-permute-start.13 = (bf16[2,272,128]{2,1,0:T(8,128)(2,1)S(1)}, bf16[2,272,128]{2,1,0:T(8,128)(2,1)S(1)}, u32[]{:S(2)}, u32[]{:S(2)}) collective-permute-start(bf16[2,272,128]{2,1,0:T(8,128)(2,1)S(1)} %get-tuple-element.27), channel_id=1, source_target_pairs={{0,1},{1,2},{2,3},{3,0},{4,5},{5,6},{6,7},{7,4},{8,9},{9,10},{10,1... | collective-permute-start | bytes 417800 | tf_op jit(solution)/shard_map/ppermute | solution.py:326
  103.2 14.9 %collective-permute-start.14 = (bf16[2,272,128]{2,1,0:T(8,128)(2,1)S(1)}, bf16[2,272,128]{2,1,0:T(8,128)(2,1)S(1)}, u32[]{:S(2)}, u32[]{:S(2)}) collective-permute-start(bf16[2,272,128]{2,1,0:T(8,128)(2,1)S(1)} %get-tuple-element.26), channel_id=1, source_target_pairs={{0,3},{1,0},{2,1},{3,2},{4,7},{5,4},{6,5},{7,6},{8,11},{9,8},{10,9... | collective-permute-start | bytes 417800 | tf_op jit(solution)/shard_map/ppermute | solution.py:326
  109.6 18.8 %collective-permute-start.19 = (bf16[2,272,128]{2,1,0:T(8,128)(2,1)S(1)}, bf16[2,272,128]{2,1,0:T(8,128)(2,1)S(1)}, u32[]{:S(2)}, u32[]{:S(2)}) collective-permute-start(bf16[2,272,128]{2,1,0:T(8,128)(2,1)S(1)} %get-tuple-element.25), channel_id=1, source_target_pairs={{0,8},{1,9},{2,10},{3,11},{4,12},{5,13},{6,14},{7,15},{8,0},{9,1},... | collective-permute-start | bytes 417800 | tf_op jit(solution)/shard_map/ppermute | solution.py:326
  112.2 16.2 %collective-permute-start.20 = (bf16[2,272,128]{2,1,0:T(8,128)(2,1)S(1)}, bf16[2,272,128]{2,1,0:T(8,128)(2,1)S(1)}, u32[]{:S(2)}, u32[]{:S(2)}) collective-permute-start(bf16[2,272,128]{2,1,0:T(8,128)(2,1)S(1)} %get-tuple-element.24), channel_id=1, source_target_pairs={{0,4},{1,5},{2,6},{3,7},{4,8},{5,9},{6,10},{7,11},{8,12},{9,13},{1... | collective-permute-start | bytes 417800 | tf_op jit(solution)/shard_map/ppermute | solution.py:326
  117.5 10.9 %collective-permute-start.21 = (bf16[2,272,128]{2,1,0:T(8,128)(2,1)S(1)}, bf16[2,272,128]{2,1,0:T(8,128)(2,1)S(1)}, u32[]{:S(2)}, u32[]{:S(2)}) collective-permute-start(bf16[2,272,128]{2,1,0:T(8,128)(2,1)S(1)} %get-tuple-element.23), channel_id=1, source_target_pairs={{0,12},{1,13},{2,14},{3,15},{4,0},{5,1},{6,2},{7,3},{8,4},{9,5},{1... | collective-permute-start | bytes 417800 | tf_op jit(solution)/shard_map/ppermute | solution.py:326
  124.5 18.7 %collective-permute-start.15 = (bf16[2,272,128]{2,1,0:T(8,128)(2,1)S(1)}, bf16[2,272,128]{2,1,0:T(8,128)(2,1)S(1)}, u32[]{:S(2)}, u32[]{:S(2)}) collective-permute-start(bf16[2,272,128]{2,1,0:T(8,128)(2,1)S(1)} %root.2), channel_id=1, source_target_pairs={{0,1},{1,2},{2,3},{3,4},{4,5},{5,6},{6,7},{7,8},{8,9},{9,10},{10,1... | collective-permute-start | bytes 417800 | tf_op jit(solution)/shard_map/ppermute | solution.py:351
  134.9 8.3 %collective-permute-start.22 = (bf16[2,272,128]{2,1,0:T(8,128)(2,1)S(1)}, bf16[2,272,128]{2,1,0:T(8,128)(2,1)S(1)}, u32[]{:S(2)}, u32[]{:S(2)}) collective-permute-start(bf16[2,272,128]{2,1,0:T(8,128)(2,1)S(1)} %root.3), channel_id=1, source_target_pairs={{1,0},{2,1},{3,2},{4,3},{5,4},{6,5},{7,6},{8,7},{9,8},{10,9},{11,1... | collective-permute-start | bytes 417800 | tf_op jit(solution)/shard_map/ppermute | solution.py:349
  143.3 7.2 %collective-permute-start.23 = (bf16[4,272,128]{2,1,0:T(8,128)(2,1)S(1)}, bf16[4,272,128]{2,1,0:T(8,128)(2,1)S(1)}, u32[]{:S(2)}, u32[]{:S(2)}) collective-permute-start(bf16[4,272,128]{2,1,0:T(8,128)(2,1)S(1)} %pad_maximum_fusion), channel_id=1, source_target_pairs={{0,16},{16,32},{32,48},{48,64},{64,80},{80,96},{96,112},{1,17},{17... | collective-permute-start | bytes 835592 | tf_op jit(solution)/shard_map/ppermute | solution.py:356
  147.1 7.9 %collective-permute-start.24 = (bf16[4,272,128]{2,1,0:T(8,128)(2,1)S(1)}, bf16[4,272,128]{2,1,0:T(8,128)(2,1)S(1)}, u32[]{:S(2)}, u32[]{:S(2)}) collective-permute-start(bf16[4,272,128]{2,1,0:T(8,128)(2,1)S(1)} %pad_maximum_fusion.1), channel_id=1, source_target_pairs={{16,0},{32,16},{48,32},{64,48},{80,64},{96,80},{112,96},{17,1},{33... | collective-permute-start | bytes 835592 | tf_op jit(solution)/shard_map/ppermute | solution.py:353
  (8 other events, 102.9 us)

commit v3 on v2

v3 whole, which is shorter than its diff:
```python
import functools

import jax
import jax.numpy as jnp
from jax import lax
from jax.experimental import pallas as pl
from jax.experimental.pallas import tpu as pltpu
from jax.sharding import PartitionSpec as P

ITERS = 5
FAST = 4
TAIL = 16
SIDE = 4
GRANT = 12 << 20
bf16 = jnp.bfloat16
f32 = jnp.float32
highest = lax.Precision.HIGHEST


def product(a, b):
    rest = jnp.dot(a[1].astype(bf16), b[1].astype(bf16), preferred_element_type=f32)
    return a[0] * b[0], a[0] * b[1] + b[0] * a[1] + rest


def step_factor(a):
    return 1.5 - 0.5 * a[0], -0.5 * a[1]


def row_times(vector, a):
    hi = vector.astype(bf16).astype(f32)
    rows = jnp.concatenate([hi, vector - hi, jnp.zeros((14, vector.shape[1]), f32)], axis=0)
    got = jnp.dot(rows.astype(bf16), a[1].astype(bf16), preferred_element_type=f32)
    return a[0] * vector + jnp.sum(got[:2], axis=0, keepdims=True)


def places_of(half):
    row = lax.broadcasted_iota(jnp.int32, (half, half), 0)
    col = lax.broadcasted_iota(jnp.int32, (half, half), 1)
    return row, col


def pack(matrix, vector_rows):
    half = matrix.shape[0] // 2
    row, col = places_of(half)
    lower_right = matrix[half:, half:]
    both = jnp.where(row >= col, matrix[:half, :half], lower_right)
    diagonal = jnp.sum(jnp.where(row == col, lower_right, 0.0), axis=0, keepdims=True)
    hi = diagonal.astype(bf16).astype(f32)
    tail = jnp.concatenate(
        [hi, diagonal - hi, vector_rows, jnp.zeros((TAIL - 6, half), f32)], axis=0
    )
    return matrix[half:, :half].astype(bf16), both.astype(bf16), tail.astype(bf16)


def unpack(total):
    half = total.shape[1]
    members = 2 * half
    row, col = places_of(half)
    corner = total[:half]
    both = total[half:members]
    turned = both.T
    diagonal = total[members : members + 1] + total[members + 1 : members + 2]
    upper_left = jnp.where(row >= col, both, turned)
    lower_right = jnp.where(
        row == col, jnp.broadcast_to(diagonal, (half, half)), jnp.where(row < col, both, turned)
    )
    matrix = jnp.concatenate(
        [
            jnp.concatenate([upper_left, corner.T], axis=1),
            jnp.concatenate([corner, lower_right], axis=1),
        ],
        axis=0,
    )
    vector = jnp.concatenate(
        [
            total[members + 2 + h : members + 3 + h] + total[members + 4 + h : members + 5 + h]
            for h in range(2)
        ],
        axis=1,
    )
    return matrix, vector


def vector_rows(vector, half):
    hi = vector.astype(bf16).astype(f32)
    lo = vector - hi
    return jnp.concatenate([hi[:, :half], hi[:, half:], lo[:, :half], lo[:, half:]], axis=0)


def gram_kernel(points, ranks, order, slots, wts, drive_ref, *refs):
    pieces = refs[:-4]
    o_ref, acc_ref, y_ref, sem = refs[-4:]
    dest = order[pl.program_id(0)]
    half = y_ref.shape[2] // 2

    @pl.when(pl.program_id(0) == 0)
    def _():
        copies = []
        at = 0
        for i, piece in enumerate(pieces):
            copies.append(
                pltpu.make_async_copy(piece, y_ref.at[pl.ds(at, piece.shape[0])], sem.at[i])
            )
            copies[-1].start()
            at += piece.shape[0]
        for copy in copies:
            copy.wait()

    most = jnp.int32(0)
    for p in range(points):
        at = p * ranks
        ys = [y_ref[slots[dest, at + k]] for k in range(FAST)]
        yw = [(ys[k].astype(f32) * wts[dest, at + k]).astype(bf16) for k in range(FAST)]
        acc_ref[p] = lax.dot_general(
            jnp.concatenate(yw, axis=0),
            jnp.concatenate(ys, axis=0),
            (((0,), (0,)), ((), ())),
            preferred_element_type=f32,
        )
        most = jnp.maximum(most, slots[dest, points * ranks + p])

    @pl.when(most > FAST)
    def _():
        for p in range(points):
            at = p * ranks

            @pl.loop(FAST, jnp.maximum(slots[dest, points * ranks + p], FAST))
            def _(k):
                y = y_ref[slots[dest, at + k]]
                w = (y.astype(f32) * wts[dest, at + k]).astype(bf16)
                acc_ref[p] += lax.dot_general(
                    w, y, (((0,), (0,)), ((), ())), preferred_element_type=f32
                )

    for p in range(points):
        corner, both, tail = pack(acc_ref[p], drive_ref[dest, p])
        o_ref[0, p, :half] = corner
        o_ref[0, p, half : 2 * half] = both
        o_ref[0, p, 2 * half :] = tail


def root_kernel(*refs):
    parts, outs = refs[:-2], refs[-2:]
    points, rows, half = parts[0].shape
    members = 2 * half
    here = range(points)
    eye = (
        lax.broadcasted_iota(jnp.int32, (members, members), 0)
        == lax.broadcasted_iota(jnp.int32, (members, members), 1)
    ).astype(f32)
    scale = 1.0 / (members - 1)
    drives, bounds, uppers, lowers = [], [], [], []
    for p in here:
        total = parts[0][p].astype(f32)
        for part in parts[1:]:
            total = total + part[p].astype(f32)
        cov, drive = unpack(total)
        drives.append(drive * scale)
        system = eye + cov * scale
        bound = jnp.max(
            jnp.sum(jnp.abs(system), axis=0, keepdims=True), axis=1, keepdims=True
        )
        trace = jnp.sum(
            jnp.sum(system * eye, axis=0, keepdims=True), axis=1, keepdims=True
        )
        level = trace * (1.0 / members)
        inverse = 1.0 / bound
        bounds.append(bound)
        uppers.append((level * inverse, (system - level * eye) * inverse))
    lowers = [step_factor(uppers[p]) for p in here]
    uppers = [product(uppers[p], lowers[p]) for p in here]
    for sweep in range(1, ITERS):
        factors = [step_factor(product(lowers[p], uppers[p])) for p in here]
        if sweep < ITERS - 1:
            uppers = [product(uppers[p], factors[p]) for p in here]
        lowers = [product(factors[p], lowers[p]) for p in here]
    for p in here:
        norm = lax.rsqrt(bounds[p])
        root = (lowers[p][0] * norm, lowers[p][1] * norm)
        shift = row_times(row_times(drives[p], root), root)
        corner, both, tail = pack(root[1] + root[0] * eye, vector_rows(shift, half))
        o_ref, row = outs[p % 2], p // 2
        o_ref[row, :half] = corner
        o_ref[row, half:members] = both
        o_ref[row, members:] = tail


def state_kernel(places, mixing, mean_ref, pert_ref, w_ref, o_ref):
    step = pl.program_id(0)
    count, cells, members = o_ref.shape
    ones = jnp.ones((TAIL, members), bf16)
    for t in range(count):
        tile = step * count + t
        total = mixing[tile, 0] * w_ref[places[tile, 0]].astype(f32)
        for j in range(1, 4):
            total = total + mixing[tile, j] * w_ref[places[tile, j]].astype(f32)
        root, shift = unpack(total)
        turned = (root + shift).astype(bf16)
        mean = mean_ref[t]
        hi = mean.astype(bf16).astype(f32)
        mid = (mean - hi).astype(bf16).astype(f32)
        thirds = jnp.concatenate(
            [hi, mid, mean - hi - mid, jnp.zeros((TAIL - 3, cells), f32)], axis=0
        ).astype(bf16)
        moved = lax.dot_general(
            pert_ref[t], turned, (((1,), (1,)), ((), ())), preferred_element_type=f32
        )
        mean = lax.dot_general(
            thirds, ones, (((0,), (0,)), ((), ())), preferred_element_type=f32
        )
        o_ref[t] = (mean + moved).astype(bf16)


def column_of(rows):
    size = lax.axis_size("lon")
    up = [(i, (i + 2) % size) for i in range(size)]
    down = [(i, (i - 2) % size) for i in range(size)]
    cut = rows.shape[0] // 2

    def send(x, pairs):
        return lax.ppermute(x, "lon", pairs)

    def swap(x):
        return lax.ppermute(x, "lon", [(i, i ^ 1) for i in range(size)])

    below = send(rows, up)
    above = send(rows, down)
    far_a = send(below[:cut], up)
    far_b = send(above[cut:], down)
    near = [rows, below, above]
    far = [far_a, far_b]
    return near + [swap(x) for x in near] + far + [swap(x) for x in far]


def place_of(apart, other):
    near = jnp.where(apart == 0, 0, jnp.where(apart == 1, 2, 1)) + 3 * other
    return jnp.where(apart == 2, 6 + other, near)


def turn(stage, k, chips):
    pairs = []
    for lon in range(2 * chips):
        for x in range(SIDE):
            for y in range(SIDE):
                if (lon + stage) % 2 == 0:
                    to = x * SIDE + (y + k) % SIDE
                else:
                    to = (x + k) % SIDE * SIDE + y
                start = lon * SIDE * SIDE
                pairs.append((start + x * SIDE + y, start + to))
    return pairs


def local(
    obs_rows,
    innovations,
    obs_home,
    obs_lists,
    loc_weights,
    state_mean,
    state_perturb,
    interp_ids,
    interp_wts,
):
    lon_count = lax.axis_size("lon")
    lat_count = lax.axis_size("lat")
    lon = lax.axis_index("lon")
    lat = lax.axis_index("lat")
    held, obs_count, members = obs_rows.shape
    half = members // 2
    point_rows, point_cols, list_len = obs_lists.shape
    points = point_rows * point_cols
    ranks = 2 * lon_count
    column_blocks = lon_count * held

    pieces = column_of(obs_rows)
    project = jnp.einsum("lok,lo->lk", obs_rows, innovations, preferred_element_type=f32)
    column_proj = lax.all_to_all(
        jnp.broadcast_to(project, (lon_count, held, members)), "lon", 0, 0, tiled=True
    ).reshape(column_blocks, members)

    ids = obs_lists.reshape(points, list_len)
    live = ids >= 0
    home = jnp.take(obs_home, jnp.maximum(ids, 0))
    column = jnp.where(live, home // held % lat_count, lat_count)
    slot = home // (held * lat_count) * held + home % held
    mask = column[None] == jnp.arange(lat_count, dtype=jnp.int32)[:, None, None]
    rank = jnp.cumsum(mask.astype(jnp.int32), axis=2) - 1
    chosen = mask[..., None] & (rank[..., None] == jnp.arange(ranks, dtype=jnp.int32))
    slots_f = jnp.sum(jnp.where(chosen, slot.astype(f32)[None, :, :, None], 0.0), axis=2)
    wts_f = jnp.sum(
        jnp.where(chosen, loc_weights.reshape(1, points, list_len, 1), 0.0), axis=2
    )
    counts = jnp.sum(mask.astype(f32), axis=2)
    asked = jnp.concatenate(
        [
            slots_f.reshape(lat_count, points * ranks),
            counts,
            wts_f.reshape(lat_count, points * ranks),
        ],
        axis=1,
    )
    asked = lax.all_to_all(asked, "lat", 0, 0, tiled=True)
    cut = points * ranks + points
    wts = asked[:, cut:]
    named = asked[:, : points * ranks].astype(jnp.int32)
    from_lon = named // held
    apart = (from_lon // 2 - lon // 2) % (lon_count // 2)
    other = (from_lon + lon) % 2
    slots = jnp.concatenate(
        [
            place_of(apart, other) * held + named % held,
            asked[:, points * ranks : cut].astype(jnp.int32),
        ],
        axis=1,
    )

    spread = jnp.sum(
        jnp.where(
            named.reshape(lat_count * points, ranks, 1)
            == jnp.arange(column_blocks, dtype=jnp.int32),
            wts.reshape(lat_count * points, ranks, 1),
            0.0,
        ),
        axis=1,
    )
    drive = jnp.dot(spread, column_proj, precision=highest)
    drive_hi = drive.astype(bf16).astype(f32)
    drive_rows = jnp.concatenate(
        [v.reshape(lat_count, points, 2, half) for v in (drive_hi, drive - drive_hi)], axis=2
    )

    smem = pl.BlockSpec(memory_space=pltpu.SMEM)
    vmem = pl.BlockSpec(memory_space=pltpu.VMEM)
    rows = members + TAIL
    x, y = lat // SIDE, lat % SIDE
    others = jnp.arange(SIDE, dtype=jnp.int32)
    y_first = lon % 2 == 0

    def gram(k):
        order = jnp.where(
            y_first,
            (x + others) % SIDE * SIDE + (y + k) % SIDE,
            (x + k) % SIDE * SIDE + (y + others) % SIDE,
        )
        return pl.pallas_call(
            functools.partial(gram_kernel, points, ranks),
            grid=(SIDE,),
            out_shape=jax.ShapeDtypeStruct((SIDE, points, rows, half), bf16),
            in_specs=[smem, smem, smem, vmem]
            + [pl.BlockSpec(memory_space=pl.ANY)] * len(pieces),
            out_specs=pl.BlockSpec((1, points, rows, half), lambda i: (i, 0, 0, 0)),
            scratch_shapes=[
                pltpu.VMEM((points, members, members), f32),
                pltpu.VMEM((column_blocks, obs_count, members), bf16),
                pltpu.SemaphoreType.DMA((len(pieces),)),
            ],
            compiler_params=pltpu.CompilerParams(vmem_limit_bytes=2 * GRANT),
            cost_estimate=pl.CostEstimate(
                flops=2 * 16 * 512 * 256 * 256, bytes_accessed=10 << 20, transcendentals=0
            ),
            name="gram",
        )(order, slots, wts, drive_rows, *pieces)

    chips = lon_count // 2
    axes = ("lon", "lat")
    got = {}
    for k in (3, 1, 2):
        got[k] = lax.ppermute(gram(k), axes, turn(0, k, chips))
    got[0] = gram(0)

    def total(k):
        sums = got[0][k].astype(f32)
        for part in (2, 1, 3):
            sums = sums + got[part][k].astype(f32)
        return sums

    own = total(0)
    seconds = [
        lax.ppermute(total(k).astype(bf16), axes, turn(1, k, chips)) for k in (2, 1, 3)
    ]

    col = jax.ShapeDtypeStruct((point_rows, rows, half), bf16)
    whole = pl.BlockSpec((points, rows, half), lambda i: (0, 0, 0))
    col_a, col_b = pl.pallas_call(
        root_kernel,
        grid=(1,),
        out_shape=(col, col),
        in_specs=[whole] * (1 + len(seconds)),
        out_specs=(pl.BlockSpec((point_rows, rows, half), lambda i: (0, 0, 0)),) * 2,
        compiler_params=pltpu.CompilerParams(vmem_limit_bytes=2 * GRANT),
        cost_estimate=pl.CostEstimate(
            flops=4 * 12 * 2 * 256**3, bytes_accessed=2 << 20, transcendentals=0
        ),
        name="root",
    )(own, *seconds)

    right = lax.ppermute(col_a, "lat", [(i + 1, i) for i in range(lat_count - 1)])
    left = lax.ppermute(col_b, "lat", [(i, i + 1) for i in range(lat_count - 1)])
    cols = [left, col_a, col_b, right]
    top = jnp.stack([c[0] for c in cols])
    bottom = jnp.stack([c[1] for c in cols])
    inside = lax.ppermute(
        jnp.where(y_first, bottom, top), "lon", [(i, i ^ 1) for i in range(lon_count)]
    )
    outside = lax.ppermute(
        jnp.where(y_first, top, bottom),
        "lon",
        [(i, (i ^ 1) + (2 if i % 2 else -2)) for i in range(1, lon_count - 1)],
    )
    held_w = jnp.concatenate([top, bottom, inside, outside], axis=0)

    grid_cols = point_cols * lat_count
    tile_rows, tile_cols, cells = state_mean.shape
    tiles = tile_rows * tile_cols
    target_ids = interp_ids.reshape(tiles, 4)
    local_row = target_ids // grid_cols - lon * point_rows
    local_col = target_ids % grid_cols - lat * point_cols + 1
    block = jnp.where(
        local_row < 0,
        jnp.where(y_first, 3, 2),
        jnp.where(local_row >= point_rows, jnp.where(y_first, 2, 3), local_row),
    )
    places = block * 4 + local_col
    per = 4
    result = pl.pallas_call(
        state_kernel,
        grid=(tiles // per,),
        out_shape=jax.ShapeDtypeStruct((tiles, cells, members), bf16),
        in_specs=[
            smem,
            smem,
            pl.BlockSpec((per, 1, cells), lambda i: (i, 0, 0)),
            pl.BlockSpec((per, cells, members), lambda i: (i, 0, 0)),
            vmem,
        ],
        out_specs=pl.BlockSpec((per, cells, members), lambda i: (i, 0, 0)),
        compiler_params=pltpu.CompilerParams(vmem_limit_bytes=GRANT),
        cost_estimate=pl.CostEstimate(
            flops=2 * 16 * 512 * 256 * 256, bytes_accessed=11 << 20, transcendentals=0
        ),
        name="state",
    )(
        places,
        interp_wts.reshape(tiles, 4),
        state_mean.reshape(tiles, 1, cells),
        state_perturb.reshape(tiles, cells, members),
        held_w,
    )
    return result.reshape(tile_rows, tile_cols, cells, members)


def solution(mesh):
    return jax.shard_map(
        local,
        mesh=mesh,
        in_specs=(
            P(("lon", "lat"), None, None),
            P(("lon", "lat"), None),
            P(),
            P("lon", "lat", None),
            P("lon", "lat", None),
            P("lon", "lat", None),
            P("lon", "lat", None, None),
            P("lon", "lat", None),
            P("lon", "lat", None),
        ),
        out_specs=P("lon", "lat", None, None),
        check_vma=False,
    )
```

time: 165 us -> 132 us (0.80); the launches traced: 163 us -> 132 us
  local copies, waits for them, and re-layouts: 22.9 us -> 5.46 us
  blocking collectives: 16.7 us -> 0 us
  waiting for transfers between devices: 32.7 us -> 42.3 us
  starting transfers between devices: 47.1 us -> 39.3 us
    unnamed x27 -> x22, local copies, waits for them, and re-layouts: 18.1 us -> 0.14 us
    all_gather x1 -> x0, blocking collectives: 16.7 us -> none  [local(): column_proj = lax.all_gather(project, 'lon', tiled=True)]
    ppermute x14 -> x8, starting transfers between devices: 25.4 us -> 11.7 us  [the longest x1 4.68 us: local(): lax.ppermute(jnp.where(y_first, bottom, top), 'lon', [(i, i ^ 1) for i in...]
    pallas_call x4, Pallas kernels: 15.7 us -> 28.4 us  [gram(): pl.pallas_call(functools.partial(gram_kernel, points, ranks), grid=(SIDE,...]
    pallas_call x2 -> x1, Pallas kernels: 12.9 us -> 3.82 us  [local(): pl.pallas_call(root_kernel, grid=(1,), out_shape=(col, col), in_specs=[wh...]
    ppermute x14 -> x8, waiting for transfers between devices: 16.6 us -> 22.1 us  [the longest x3 8.57 us: local(): lax.ppermute(total(k).astype(bf16), axes, turn(1, k, chips))]
    all_to_all x0 -> x1, starting transfers between devices: none -> 4.7 us  [local(): lax.all_to_all(jnp.broadcast_to(project, (lon_count, held, members)), 'lo...]
    all_to_all x1, waiting for transfers between devices: 0.01 us -> 4.43 us  [local(): asked = lax.all_to_all(asked, 'lat', 0, 0, tiled=True)]
  transfers between devices with their start and end apart: 26 -> 21, of which waited for: 7 -> 12; matrix products, arithmetic and copies ran while one was open for 13% -> 7% of each run, Pallas kernels for 15% -> 16%
where the time goes in v3:
time: 132 us
  waiting for transfers between devices  42.3 us (32%)
  starting transfers between devices  39.3 us (30%)
  Pallas kernels  37.7 us (29%)
  other arithmetic  6.11 us (5%)
  local copies, waits for them, and re-layouts  5.46 us (4%)
    pallas_call x4, Pallas kernels, gram(): pl.pallas_call(functools.partial(gram_kernel, points, ranks), grid=(SIDE,...  28.4 us
    ppermute x4, waiting for transfers between devices, send(): return lax.ppermute(x, 'lon', pairs)  9.47 us
    ppermute x3, waiting for transfers between devices, local(): lax.ppermute(total(k).astype(bf16), axes, turn(1, k, chips))  8.57 us
    ppermute x3, waiting for transfers between devices, local(): got[k] = lax.ppermute(gram(k), axes, turn(0, k, chips))  7.63 us
    all_to_all x1, starting transfers between devices, local(): asked = lax.all_to_all(asked, 'lat', 0, 0, tiled=True)  6.61 us
    ppermute x4, starting transfers between devices, send(): return lax.ppermute(x, 'lon', pairs)  6.51 us
    ppermute x1, waiting for transfers between devices, local(): lax.ppermute(jnp.where(y_first, top, bottom), 'lon', [(i, (i ^ 1) + (2 if...  5.86 us
    pallas_call x1, Pallas kernels, local(): pl.pallas_call(state_kernel, grid=(tiles // per,), out_shape=jax.ShapeDty...  5.5 us
  transfers between devices with their start and end apart: 21, of which 12 were waited for; matrix products, arithmetic and copies ran while one was open for 7% of the time, Pallas kernels for 16%

profile of v3, /device:TPU:25, one launch (start us, length us, event | category | flops | bytes accessed | tf_op | source)
XLA Modules:
  0.0 131.8 jit_solution(8997825563384993819)
XLA Ops:
  0.0 1.6 %collective-permute-start = (bf16[16,128,256]{2,1,0:T(8,128)(2,1)}, bf16[16,128,256]{2,1,0:T(8,128)(2,1)S(1)}, u32[]{:S(2)}, u32[]{:S(2)}) collective-permute-start(bf16[16,128,256]{2,1,0:T(8,128)(2,1)} %refs_0_.7), channel_id=1, source_target_pairs={{0,32},{16,48},{32,64},{48,80},{64,96},{80,112},{96,0},{112,16},{1... | collective-permute-start | bytes 3145736 | tf_op jit(solution)/shard_map/ppermute | solution.py:221
  1.6 2.2 %collective-permute-start.1 = (bf16[16,128,256]{2,1,0:T(8,128)(2,1)}, bf16[16,128,256]{2,1,0:T(8,128)(2,1)S(1)}, u32[]{:S(2)}, u32[]{:S(2)}) collective-permute-start(bf16[16,128,256]{2,1,0:T(8,128)(2,1)} %refs_0_.7), channel_id=1, source_target_pairs={{0,96},{16,112},{32,0},{48,16},{64,32},{80,48},{96,64},{112,80},{1... | collective-permute-start | bytes 3145736 | tf_op jit(solution)/shard_map/ppermute | solution.py:221
  10.3 6.6 %all-to-all-start = ((f32[16,1,132]{2,1,0:T(1,128)}), f32[16,1,132]{2,1,0:T(1,128)S(1)}, u32[]{:S(2)}, u32[]{:S(2)}) async-start(f32[16,1,132]{2,1,0:T(1,128)} %all_to_all.11), calls=%async_computation | async-start | bytes 32768 | tf_op jit(solution)/shard_map/all_to_all | solution.py:303
  17.2 4.4 %all-to-all-done = f32[16,1,132]{2,1,0:T(1,128)S(1)} async-done(((f32[16,1,132]{2,1,0:T(1,128)}), f32[16,1,132]{2,1,0:T(1,128)S(1)}, u32[]{:S(2)}, u32[]{:S(2)}) %all-to-all-start) | async-done | bytes 8480 | tf_op jit(solution)/shard_map/all_to_all | solution.py:303
  22.3 4.7 %all-to-all-start.1 = ((f32[8,16,256]{2,1,0:T(8,128)}), f32[8,16,256]{2,1,0:T(8,128)S(1)}, u32[]{:S(2)}, u32[]{:S(2)}) async-start(f32[8,16,256]{2,1,0:T(8,128)} %broadcast_in_dim.75), calls=%async_computation.1 | async-start | bytes 262144 | tf_op jit(solution)/shard_map/all_to_all | solution.py:278
  31.4 1.6 %collective-permute-start.3 = (bf16[16,128,256]{2,1,0:T(8,128)(2,1)S(1)}, bf16[16,128,256]{2,1,0:T(8,128)(2,1)}, u32[]{:S(2)}, u32[]{:S(2)}) collective-permute-start(bf16[16,128,256]{2,1,0:T(8,128)(2,1)S(1)} %collective-permute-done.refs_1_), channel_id=1, source_target_pairs={{0,16},{16,0},{32,48},{48,32},{64,80},{80,64},{96,112},{112,96},{1... | collective-permute-start | bytes 3145736 | tf_op jit(solution)/shard_map/ppermute | solution.py:224
  33.3 9.5 %collective-permute-done.5.refs_6_ = bf16[8,128,256]{2,1,0:T(8,128)(2,1)} collective-permute-done((bf16[8,128,256]{2,1,0:T(8,128)(2,1)}, bf16[8,128,256]{2,1,0:T(8,128)(2,1)}, u32[]{:S(2)}, u32[]{:S(2)}) %collective-permute-start.5) | collective-permute-done | bytes 524320 | tf_op jit(solution)/shard_map/ppermute | solution.py:221
  46.9 7.5 %gram.5 = bf16[4,4,272,128]{3,2,1,0:T(8,128)(2,1)} custom-call(s32[4]{0:T(128)S(1)} %broadcast_select_fusion.4.order, s32[16,68]{1,0:T(8,128)S(1)} %pad_add_fusion.slots, f32[16,64]{1,0:T(8,128)S(1)} %get-tuple-element.32.wts, f32[16,4,4,128]{3,2,1,0:T(4,128)S(1)} %pad_maximum_fusion.2.drive_ref, bf16[16,128,256]{2,1,0:T(8,128)(2,1)S(1)} %copy-done.1, ...), custom_call_target="tpu_custom_call" | custom-call | flops 1073741824 | bytes 10485760 | tf_op jit(solution)/shard_map/gram/pallas_call | solution.py:346
  55.8 7.5 %gram.6 = bf16[4,4,272,128]{3,2,1,0:T(8,128)(2,1)} custom-call(s32[4]{0:T(128)S(1)} %broadcast_select_fusion.3.order, s32[16,68]{1,0:T(8,128)S(1)} %pad_add_fusion.slots, f32[16,64]{1,0:T(8,128)S(1)} %get-tuple-element.32.wts, f32[16,4,4,128]{3,2,1,0:T(4,128)S(1)} %pad_maximum_fusion.2.drive_ref, bf16[16,128,256]{2,1,0:T(8,128)(2,1)S(1)} %copy-done.1, ...), custom_call_target="tpu_custom_call" | custom-call | flops 1073741824 | bytes 10485760 | tf_op jit(solution)/shard_map/gram/pallas_call | solution.py:346
  64.0 7.5 %gram.7 = bf16[4,4,272,128]{3,2,1,0:T(8,128)(2,1)} custom-call(s32[4]{0:T(128)S(1)} %broadcast_select_fusion.2.order, s32[16,68]{1,0:T(8,128)S(1)} %pad_add_fusion.slots, f32[16,64]{1,0:T(8,128)S(1)} %get-tuple-element.32.wts, f32[16,4,4,128]{3,2,1,0:T(4,128)S(1)} %pad_maximum_fusion.2.drive_ref, bf16[16,128,256]{2,1,0:T(8,128)(2,1)S(1)} %copy-done.1, ...), custom_call_target="tpu_custom_call" | custom-call | flops 1073741824 | bytes 10485760 | tf_op jit(solution)/shard_map/gram/pallas_call | solution.py:346
  72.9 5.9 %gram.4 = bf16[4,4,272,128]{3,2,1,0:T(8,128)(2,1)S(1)} custom-call(s32[4]{0:T(128)S(1)} %broadcast_select_fusion.5.order, s32[16,68]{1,0:T(8,128)S(1)} %pad_add_fusion.slots, f32[16,64]{1,0:T(8,128)S(1)} %get-tuple-element.32.wts, f32[16,4,4,128]{3,2,1,0:T(4,128)S(1)} %pad_maximum_fusion.2.drive_ref, bf16[16,128,256]{2,1,0:T(8,128)(2,1)S(1)} %copy-done.1, ...), custom_call_target="tpu_custom_call" | custom-call | flops 1073741824 | bytes 10485760 | tf_op jit(solution)/shard_map/gram/pallas_call | solution.py:346
  78.9 4.0 %collective-permute-done.10 = bf16[4,4,272,128]{3,2,1,0:T(8,128)(2,1)} collective-permute-done((bf16[4,4,272,128]{3,2,1,0:T(8,128)(2,1)}, bf16[4,4,272,128]{3,2,1,0:T(8,128)(2,1)}, u32[]{:S(2)}, u32[]{:S(2)}) %collective-permute-start.10) | collective-permute-done | bytes 1114144 | tf_op jit(solution)/shard_map/ppermute | solution.py:369
  82.8 3.6 %collective-permute-done.11 = bf16[4,4,272,128]{3,2,1,0:T(8,128)(2,1)} collective-permute-done((bf16[4,4,272,128]{3,2,1,0:T(8,128)(2,1)}, bf16[4,4,272,128]{3,2,1,0:T(8,128)(2,1)}, u32[]{:S(2)}, u32[]{:S(2)}) %collective-permute-start.11) | collective-permute-done | bytes 1114144 | tf_op jit(solution)/shard_map/ppermute | solution.py:369
  86.5 2.4 %fusion.3 = (bf16[4,272,128]{2,1,0:T(8,128)(2,1)S(1)}, bf16[4,272,128]{2,1,0:T(8,128)(2,1)S(1)}, bf16[4,272,128]{2,1,0:T(8,128)(2,1)S(1)}, f32[4,272,128]{2,1,0:T(8,128)S(1)}) fusion(bf16[4,4,272,128]{3,2,1,0:T(8,128)(2,1)} %collective-permute-done.11, bf16[4,4,272,128]{3,2,1,0:T(8,128)(2,1)} %collective-permute-done.10, ...), kind=kLoop, calls=%fused_computation.13 | loop fusion | flops 4317184 | bytes 5849088 | tf_op jit(solution)/shard_map/add | solution.py:375
  90.6 5.4 %collective-permute-done.12.refs_1_ = bf16[4,272,128]{2,1,0:T(8,128)(2,1)S(1)} collective-permute-done((bf16[4,272,128]{2,1,0:T(8,128)(2,1)S(1)}, bf16[4,272,128]{2,1,0:T(8,128)(2,1)S(1)}, u32[]{:S(2)}, u32[]{:S(2)}) %collective-permute-start.12) | collective-permute-done | bytes 278560 | tf_op jit(solution)/shard_map/ppermute | solution.py:380
  96.0 1.7 %collective-permute-done.13.refs_2_ = bf16[4,272,128]{2,1,0:T(8,128)(2,1)S(1)} collective-permute-done((bf16[4,272,128]{2,1,0:T(8,128)(2,1)S(1)}, bf16[4,272,128]{2,1,0:T(8,128)(2,1)S(1)}, u32[]{:S(2)}, u32[]{:S(2)}) %collective-permute-start.13) | collective-permute-done | bytes 278560 | tf_op jit(solution)/shard_map/ppermute | solution.py:380
  99.2 3.8 %root.1 = (bf16[2,272,128]{2,1,0:T(8,128)(2,1)S(1)}, bf16[2,272,128]{2,1,0:T(8,128)(2,1)S(1)}) custom-call(f32[4,272,128]{2,1,0:T(8,128)S(1)} %get-tuple-element.14.refs_0_, bf16[4,272,128]{2,1,0:T(8,128)(2,1)S(1)} %collective-permute-done.12.refs_1_, bf16[4,272,128]{2,1,0:T(8,128)(2,1)S(1)} %collective-permute-done.13.refs_2_, ...), custom_call_target="tpu_custom_call" | custom-call | flops 1610612736 | bytes 2097152 | tf_op jit(solution)/shard_map/root/pallas_call | solution.py:385
  103.0 2.5 %collective-permute-start.15 = (bf16[2,272,128]{2,1,0:T(8,128)(2,1)S(1)}, bf16[2,272,128]{2,1,0:T(8,128)(2,1)S(1)}, u32[]{:S(2)}, u32[]{:S(2)}) collective-permute-start(bf16[2,272,128]{2,1,0:T(8,128)(2,1)S(1)} %get-tuple-element.7), channel_id=1, source_target_pairs={{0,1},{1,2},{2,3},{3,4},{4,5},{5,6},{6,7},{7,8},{8,9},{9,10},{10,1... | collective-permute-start | bytes 417800 | tf_op jit(solution)/shard_map/ppermute | solution.py:399
  105.6 2.7 %collective-permute-start.16 = (bf16[2,272,128]{2,1,0:T(8,128)(2,1)S(1)}, bf16[2,272,128]{2,1,0:T(8,128)(2,1)S(1)}, u32[]{:S(2)}, u32[]{:S(2)}) collective-permute-start(bf16[2,272,128]{2,1,0:T(8,128)(2,1)S(1)} %get-tuple-element.8), channel_id=1, source_target_pairs={{1,0},{2,1},{3,2},{4,3},{5,4},{6,5},{7,6},{8,7},{9,8},{10,9},{11,1... | collective-permute-start | bytes 417800 | tf_op jit(solution)/shard_map/ppermute | solution.py:398
  108.9 4.6 %collective-permute-done.16 = bf16[2,272,128]{2,1,0:T(8,128)(2,1)S(1)} collective-permute-done((bf16[2,272,128]{2,1,0:T(8,128)(2,1)S(1)}, bf16[2,272,128]{2,1,0:T(8,128)(2,1)S(1)}, u32[]{:S(2)}, u32[]{:S(2)}) %collective-permute-start.16) | collective-permute-done | bytes 139296 | tf_op jit(solution)/shard_map/ppermute | solution.py:398
  113.7 4.7 %collective-permute-start.17 = (bf16[4,272,128]{2,1,0:T(8,128)(2,1)S(1)}, bf16[4,272,128]{2,1,0:T(8,128)(2,1)S(1)}, u32[]{:S(2)}, u32[]{:S(2)}) collective-permute-start(bf16[4,272,128]{2,1,0:T(8,128)(2,1)S(1)} %get-tuple-element.16), channel_id=1, source_target_pairs={{0,16},{16,0},{32,48},{48,32},{64,80},{80,64},{96,112},{112,96},{1... | collective-permute-start | bytes 835592 | tf_op jit(solution)/shard_map/ppermute | solution.py:403
  118.4 1.9 %collective-permute-start.18 = (bf16[4,272,128]{2,1,0:T(8,128)(2,1)S(1)}, bf16[4,272,128]{2,1,0:T(8,128)(2,1)S(1)}, u32[]{:S(2)}, u32[]{:S(2)}) collective-permute-start(bf16[4,272,128]{2,1,0:T(8,128)(2,1)S(1)} %get-tuple-element.15), channel_id=1, source_target_pairs={{16,32},{32,16},{48,64},{64,48},{80,96},{96,80},{17,33},{33,17},{4... | collective-permute-start | bytes 835592 | tf_op jit(solution)/shard_map/ppermute | solution.py:406
  120.4 5.9 %collective-permute-done.18 = bf16[4,272,128]{2,1,0:T(8,128)(2,1)S(1)} collective-permute-done((bf16[4,272,128]{2,1,0:T(8,128)(2,1)S(1)}, bf16[4,272,128]{2,1,0:T(8,128)(2,1)S(1)}, u32[]{:S(2)}, u32[]{:S(2)}) %collective-permute-start.18) | collective-permute-done | bytes 278560 | tf_op jit(solution)/shard_map/ppermute | solution.py:406
  126.3 5.5 %state.1 = bf16[16,512,256]{2,1,0:T(8,128)(2,1)} custom-call(s32[16,4]{1,0:T(8,128)S(1)} %fusion.9.places, f32[16,4]{1,0:T(8,128)S(1)} %bitcast.25, f32[16,1,512]{2,1,0:T(1,128)S(1)} %reshape.189.mean_ref, bf16[16,512,256]{2,1,0:T(8,128)(2,1)S(1)} %bitcast.24, bf16[16,272,128]{2,1,0:T(8,128)(2,1)S(1)} %constant_dynamic-update-slice_fusion.w_ref), custom_call_target="tpu_custom_call" | custom-call | flops 1073741824 | bytes 11534336 | tf_op jit(solution)/shard_map/state/pallas_call | solution.py:426
  (96 shorter events, 23.5 us)
Async XLA Ops:
  0.0 27.0 %collective-permute-start = (bf16[16,128,256]{2,1,0:T(8,128)(2,1)}, bf16[16,128,256]{2,1,0:T(8,128)(2,1)S(1)}, u32[]{:S(2)}, u32[]{:S(2)}) collective-permute-start(bf16[16,128,256]{2,1,0:T(8,128)(2,1)} %refs_0_.7), channel_id=1, source_target_pairs={{0,32},{16,48},{32,64},{48,80},{64,96},{80,112},{96,0},{112,16},{1... | collective-permute-start | bytes 3145736 | tf_op jit(solution)/shard_map/ppermute | solution.py:221
  1.6 27.6 %collective-permute-start.1 = (bf16[16,128,256]{2,1,0:T(8,128)(2,1)}, bf16[16,128,256]{2,1,0:T(8,128)(2,1)S(1)}, u32[]{:S(2)}, u32[]{:S(2)}) collective-permute-start(bf16[16,128,256]{2,1,0:T(8,128)(2,1)} %refs_0_.7), channel_id=1, source_target_pairs={{0,96},{16,112},{32,0},{48,16},{64,32},{80,48},{96,64},{112,80},{1... | collective-permute-start | bytes 3145736 | tf_op jit(solution)/shard_map/ppermute | solution.py:221
  3.8 41.7 %collective-permute-start.2 = (bf16[16,128,256]{2,1,0:T(8,128)(2,1)}, bf16[16,128,256]{2,1,0:T(8,128)(2,1)}, u32[]{:S(2)}, u32[]{:S(2)}) collective-permute-start(bf16[16,128,256]{2,1,0:T(8,128)(2,1)} %refs_0_.7), channel_id=1, source_target_pairs={{0,16},{16,0},{32,48},{48,32},{64,80},{80,64},{96,112},{112,96},{1... | collective-permute-start | bytes 3145736 | tf_op jit(solution)/shard_map/ppermute | solution.py:224
  10.3 11.4 %all-to-all-start = ((f32[16,1,132]{2,1,0:T(1,128)}), f32[16,1,132]{2,1,0:T(1,128)S(1)}, u32[]{:S(2)}, u32[]{:S(2)}) async-start(f32[16,1,132]{2,1,0:T(1,128)} %all_to_all.11), calls=%async_computation | async-start | bytes 32768 | tf_op jit(solution)/shard_map/all_to_all | solution.py:303
  22.3 22.9 %all-to-all-start.1 = ((f32[8,16,256]{2,1,0:T(8,128)}), f32[8,16,256]{2,1,0:T(8,128)S(1)}, u32[]{:S(2)}, u32[]{:S(2)}) async-start(f32[8,16,256]{2,1,0:T(8,128)} %broadcast_in_dim.75), calls=%async_computation.1 | async-start | bytes 262144 | tf_op jit(solution)/shard_map/all_to_all | solution.py:278
  27.9 14.9 %collective-permute-start.5 = (bf16[8,128,256]{2,1,0:T(8,128)(2,1)}, bf16[8,128,256]{2,1,0:T(8,128)(2,1)}, u32[]{:S(2)}, u32[]{:S(2)}) collective-permute-start(bf16[8,128,256]{2,1,0:T(8,128)(2,1)} %slice.121), channel_id=1, source_target_pairs={{0,32},{16,48},{32,64},{48,80},{64,96},{80,112},{96,0},{112,16},{1... | collective-permute-start | bytes 1572872 | tf_op jit(solution)/shard_map/ppermute | solution.py:221
  30.1 14.2 %collective-permute-start.6 = (bf16[8,128,256]{2,1,0:T(8,128)(2,1)}, bf16[8,128,256]{2,1,0:T(8,128)(2,1)}, u32[]{:S(2)}, u32[]{:S(2)}) collective-permute-start(bf16[8,128,256]{2,1,0:T(8,128)(2,1)} %slice.122), channel_id=1, source_target_pairs={{0,96},{16,112},{32,0},{48,16},{64,32},{80,48},{96,64},{112,80},{1... | collective-permute-start | bytes 1572872 | tf_op jit(solution)/shard_map/ppermute | solution.py:221
  31.4 15.5 %collective-permute-start.3 = (bf16[16,128,256]{2,1,0:T(8,128)(2,1)S(1)}, bf16[16,128,256]{2,1,0:T(8,128)(2,1)}, u32[]{:S(2)}, u32[]{:S(2)}) collective-permute-start(bf16[16,128,256]{2,1,0:T(8,128)(2,1)S(1)} %collective-permute-done.refs_1_), channel_id=1, source_target_pairs={{0,16},{16,0},{32,48},{48,32},{64,80},{80,64},{96,112},{112,96},{1... | collective-permute-start | bytes 3145736 | tf_op jit(solution)/shard_map/ppermute | solution.py:224
  33.0 13.9 %collective-permute-start.4 = (bf16[16,128,256]{2,1,0:T(8,128)(2,1)S(1)}, bf16[16,128,256]{2,1,0:T(8,128)(2,1)}, u32[]{:S(2)}, u32[]{:S(2)}) collective-permute-start(bf16[16,128,256]{2,1,0:T(8,128)(2,1)S(1)} %collective-permute-done.1.refs_2_), channel_id=1, source_target_pairs={{0,16},{16,0},{32,48},{48,32},{64,80},{80,64},{96,112},{112,96},{1... | collective-permute-start | bytes 3145736 | tf_op jit(solution)/shard_map/ppermute | solution.py:224
  42.8 3.3 %collective-permute-start.7 = (bf16[8,128,256]{2,1,0:T(8,128)(2,1)}, bf16[8,128,256]{2,1,0:T(8,128)(2,1)}, u32[]{:S(2)}, u32[]{:S(2)}) collective-permute-start(bf16[8,128,256]{2,1,0:T(8,128)(2,1)} %collective-permute-done.5.refs_6_), channel_id=1, source_target_pairs={{0,16},{16,0},{32,48},{48,32},{64,80},{80,64},{96,112},{112,96},{1... | collective-permute-start | bytes 1572872 | tf_op jit(solution)/shard_map/ppermute | solution.py:224
  44.3 2.6 %collective-permute-start.8 = (bf16[8,128,256]{2,1,0:T(8,128)(2,1)}, bf16[8,128,256]{2,1,0:T(8,128)(2,1)}, u32[]{:S(2)}, u32[]{:S(2)}) collective-permute-start(bf16[8,128,256]{2,1,0:T(8,128)(2,1)} %collective-permute-done.6.refs_7_), channel_id=1, source_target_pairs={{0,16},{16,0},{32,48},{48,32},{64,80},{80,64},{96,112},{112,96},{1... | collective-permute-start | bytes 1572872 | tf_op jit(solution)/shard_map/ppermute | solution.py:224
  54.4 24.5 %collective-permute-start.9 = (bf16[4,4,272,128]{3,2,1,0:T(8,128)(2,1)}, bf16[4,4,272,128]{3,2,1,0:T(8,128)(2,1)}, u32[]{:S(2)}, u32[]{:S(2)}) collective-permute-start(bf16[4,4,272,128]{3,2,1,0:T(8,128)(2,1)} %gram.5), channel_id=1, source_target_pairs={{0,2},{1,3},{2,0},{3,1},{4,6},{5,7},{6,4},{7,5},{8,10},{9,11},{10,... | collective-permute-start | bytes 3342344 | tf_op jit(solution)/shard_map/ppermute | solution.py:369
  63.3 19.5 %collective-permute-start.10 = (bf16[4,4,272,128]{3,2,1,0:T(8,128)(2,1)}, bf16[4,4,272,128]{3,2,1,0:T(8,128)(2,1)}, u32[]{:S(2)}, u32[]{:S(2)}) collective-permute-start(bf16[4,4,272,128]{3,2,1,0:T(8,128)(2,1)} %gram.6), channel_id=1, source_target_pairs={{0,1},{1,2},{2,3},{3,0},{4,5},{5,6},{6,7},{7,4},{8,9},{9,10},{10,1... | collective-permute-start | bytes 3342344 | tf_op jit(solution)/shard_map/ppermute | solution.py:369
  71.5 15.0 %collective-permute-start.11 = (bf16[4,4,272,128]{3,2,1,0:T(8,128)(2,1)}, bf16[4,4,272,128]{3,2,1,0:T(8,128)(2,1)}, u32[]{:S(2)}, u32[]{:S(2)}) collective-permute-start(bf16[4,4,272,128]{3,2,1,0:T(8,128)(2,1)} %gram.7), channel_id=1, source_target_pairs={{0,3},{1,0},{2,1},{3,2},{4,7},{5,4},{6,5},{7,6},{8,11},{9,8},{10,9... | collective-permute-start | bytes 3342344 | tf_op jit(solution)/shard_map/ppermute | solution.py:369
  78.8 11.7 %copy-start.4 = (f32[4,4,512]{2,1,0:T(4,128)S(1)}, f32[4,4,512]{2,1,0:T(4,128)}, u32[]{:S(2)}) copy-start(f32[4,4,512]{2,1,0:T(4,128)} %param.14) | copy-start | bytes 98308
  88.9 7.1 %collective-permute-start.12 = (bf16[4,272,128]{2,1,0:T(8,128)(2,1)S(1)}, bf16[4,272,128]{2,1,0:T(8,128)(2,1)S(1)}, u32[]{:S(2)}, u32[]{:S(2)}) collective-permute-start(bf16[4,272,128]{2,1,0:T(8,128)(2,1)S(1)} %get-tuple-element.13), channel_id=1, source_target_pairs={{0,8},{1,9},{2,10},{3,11},{4,12},{5,13},{6,14},{7,15},{8,0},{9,1},... | collective-permute-start | bytes 835592 | tf_op jit(solution)/shard_map/ppermute | solution.py:380
  89.0 8.7 %collective-permute-start.13 = (bf16[4,272,128]{2,1,0:T(8,128)(2,1)S(1)}, bf16[4,272,128]{2,1,0:T(8,128)(2,1)S(1)}, u32[]{:S(2)}, u32[]{:S(2)}) collective-permute-start(bf16[4,272,128]{2,1,0:T(8,128)(2,1)S(1)} %get-tuple-element.12), channel_id=1, source_target_pairs={{0,4},{1,5},{2,6},{3,7},{4,8},{5,9},{6,10},{7,11},{8,12},{9,13},{1... | collective-permute-start | bytes 835592 | tf_op jit(solution)/shard_map/ppermute | solution.py:380
  90.4 8.8 %collective-permute-start.14 = (bf16[4,272,128]{2,1,0:T(8,128)(2,1)S(1)}, bf16[4,272,128]{2,1,0:T(8,128)(2,1)S(1)}, u32[]{:S(2)}, u32[]{:S(2)}) collective-permute-start(bf16[4,272,128]{2,1,0:T(8,128)(2,1)S(1)} %get-tuple-element.11), channel_id=1, source_target_pairs={{0,12},{1,13},{2,14},{3,15},{4,0},{5,1},{6,2},{7,3},{8,4},{9,5},{1... | collective-permute-start | bytes 835592 | tf_op jit(solution)/shard_map/ppermute | solution.py:380
  103.0 5.8 %collective-permute-start.15 = (bf16[2,272,128]{2,1,0:T(8,128)(2,1)S(1)}, bf16[2,272,128]{2,1,0:T(8,128)(2,1)S(1)}, u32[]{:S(2)}, u32[]{:S(2)}) collective-permute-start(bf16[2,272,128]{2,1,0:T(8,128)(2,1)S(1)} %get-tuple-element.7), channel_id=1, source_target_pairs={{0,1},{1,2},{2,3},{3,4},{4,5},{5,6},{6,7},{7,8},{8,9},{9,10},{10,1... | collective-permute-start | bytes 417800 | tf_op jit(solution)/shard_map/ppermute | solution.py:399
  105.6 7.9 %collective-permute-start.16 = (bf16[2,272,128]{2,1,0:T(8,128)(2,1)S(1)}, bf16[2,272,128]{2,1,0:T(8,128)(2,1)S(1)}, u32[]{:S(2)}, u32[]{:S(2)}) collective-permute-start(bf16[2,272,128]{2,1,0:T(8,128)(2,1)S(1)} %get-tuple-element.8), channel_id=1, source_target_pairs={{1,0},{2,1},{3,2},{4,3},{5,4},{6,5},{7,6},{8,7},{9,8},{10,9},{11,1... | collective-permute-start | bytes 417800 | tf_op jit(solution)/shard_map/ppermute | solution.py:398
  108.8 17.5 %copy-start.2 = (bf16[4,4,512,256]{3,2,1,0:T(8,128)(2,1)S(1)}, bf16[4,4,512,256]{3,2,1,0:T(8,128)(2,1)}, u32[]{:S(2)}) copy-start(bf16[4,4,512,256]{3,2,1,0:T(8,128)(2,1)} %param.15) | copy-start | bytes 12582916
  113.6 12.7 %copy-start.3 = (f32[4,4,4]{2,1,0:T(4,128)S(1)}, f32[4,4,4]{2,1,0:T(4,128)}, u32[]{:S(2)}) copy-start(f32[4,4,4]{2,1,0:T(4,128)} %param.17) | copy-start | bytes 772
  113.7 6.7 %collective-permute-start.17 = (bf16[4,272,128]{2,1,0:T(8,128)(2,1)S(1)}, bf16[4,272,128]{2,1,0:T(8,128)(2,1)S(1)}, u32[]{:S(2)}, u32[]{:S(2)}) collective-permute-start(bf16[4,272,128]{2,1,0:T(8,128)(2,1)S(1)} %get-tuple-element.16), channel_id=1, source_target_pairs={{0,16},{16,0},{32,48},{48,32},{64,80},{80,64},{96,112},{112,96},{1... | collective-permute-start | bytes 835592 | tf_op jit(solution)/shard_map/ppermute | solution.py:403
  118.4 7.9 %collective-permute-start.18 = (bf16[4,272,128]{2,1,0:T(8,128)(2,1)S(1)}, bf16[4,272,128]{2,1,0:T(8,128)(2,1)S(1)}, u32[]{:S(2)}, u32[]{:S(2)}) collective-permute-start(bf16[4,272,128]{2,1,0:T(8,128)(2,1)S(1)} %get-tuple-element.15), channel_id=1, source_target_pairs={{16,32},{32,16},{48,64},{64,48},{80,96},{96,80},{17,33},{33,17},{4... | collective-permute-start | bytes 835592 | tf_op jit(solution)/shard_map/ppermute | solution.py:406
  (5 other events, 36.4 us)

commit v4 on v3

--- a/solution.py
+++ b/solution.py
@@ -11,7 +11,7 @@
 FAST = 4
 TAIL = 16
 SIDE = 4
-GRANT = 12 << 20
+GRANT = 8 << 20
 bf16 = jnp.bfloat16
 f32 = jnp.float32
 highest = lax.Precision.HIGHEST
@@ -87,25 +87,23 @@
     return jnp.concatenate([hi[:, :half], hi[:, half:], lo[:, :half], lo[:, half:]], axis=0)
 
 
-def gram_kernel(points, ranks, order, slots, wts, drive_ref, *refs):
-    pieces = refs[:-4]
-    o_ref, acc_ref, y_ref, sem = refs[-4:]
+def join_kernel(start, *refs):
+    pieces, (y_ref, sem) = refs[:-2], refs[-2:]
+    copies = []
+    at = start
+    for i, piece in enumerate(pieces):
+        copies.append(
+            pltpu.make_async_copy(piece, y_ref.at[pl.ds(at, piece.shape[0])], sem.at[i])
+        )
+        copies[-1].start()
+        at += piece.shape[0]
+    for copy in copies:
+        copy.wait()
+
+
+def gram_kernel(points, ranks, order, slots, wts, drive_ref, y_ref, o_ref, acc_ref):
     dest = order[pl.program_id(0)]
     half = y_ref.shape[2] // 2
-
-    @pl.when(pl.program_id(0) == 0)
-    def _():
-        copies = []
-        at = 0
-        for i, piece in enumerate(pieces):
-            copies.append(
-                pltpu.make_async_copy(piece, y_ref.at[pl.ds(at, piece.shape[0])], sem.at[i])
-            )
-            copies[-1].start()
-            at += piece.shape[0]
-        for copy in copies:
-            copy.wait()
-
     most = jnp.int32(0)
     for p in range(points):
         at = p * ranks
@@ -139,7 +137,7 @@
         o_ref[0, p, 2 * half :] = tail
 
 
-def root_kernel(*refs):
+def root_kernel(odd, *refs):
     parts, outs = refs[:-2], refs[-2:]
     points, rows, half = parts[0].shape
     members = 2 * half
@@ -179,10 +177,14 @@
         root = (lowers[p][0] * norm, lowers[p][1] * norm)
         shift = row_times(row_times(drives[p], root), root)
         corner, both, tail = pack(root[1] + root[0] * eye, vector_rows(shift, half))
-        o_ref, row = outs[p % 2], p // 2
-        o_ref[row, :half] = corner
-        o_ref[row, half:members] = both
-        o_ref[row, members:] = tail
+        row = p // 2
+        for flip in range(2):
+
+            @pl.when(odd[0] == flip)
+            def _(o_ref=outs[(p + 1 + flip) % 2], row=row, corner=corner, both=both, tail=tail):
+                o_ref[row, :half] = corner
+                o_ref[row, half:members] = both
+                o_ref[row, members:] = tail
 
 
 def state_kernel(places, mixing, mean_ref, pert_ref, w_ref, o_ref):
@@ -347,22 +349,28 @@
             functools.partial(gram_kernel, points, ranks),
             grid=(SIDE,),
             out_shape=jax.ShapeDtypeStruct((SIDE, points, rows, half), bf16),
-            in_specs=[smem, smem, smem, vmem]
-            + [pl.BlockSpec(memory_space=pl.ANY)] * len(pieces),
+            in_specs=[smem, smem, smem, vmem, vmem],
             out_specs=pl.BlockSpec((1, points, rows, half), lambda i: (i, 0, 0, 0)),
             scratch_shapes=[
                 pltpu.VMEM((points, members, members), f32),
-                pltpu.VMEM((column_blocks, obs_count, members), bf16),
-                pltpu.SemaphoreType.DMA((len(pieces),)),
             ],
-            compiler_params=pltpu.CompilerParams(vmem_limit_bytes=2 * GRANT),
+            compiler_params=pltpu.CompilerParams(vmem_limit_bytes=GRANT),
             cost_estimate=pl.CostEstimate(
                 flops=2 * 16 * 512 * 256 * 256, bytes_accessed=10 << 20, transcendentals=0
             ),
             name="gram",
-        )(order, slots, wts, drive_rows, *pieces)
+        )(order, slots, wts, drive_rows, column_rows)
 
     chips = lon_count // 2
+    column_rows = pl.pallas_call(
+        functools.partial(join_kernel, 0),
+        out_shape=jax.ShapeDtypeStruct((column_blocks, obs_count, members), bf16),
+        in_specs=[pl.BlockSpec(memory_space=pl.ANY)] * len(pieces),
+        out_specs=pl.BlockSpec(memory_space=pl.ANY),
+        scratch_shapes=[pltpu.SemaphoreType.DMA((len(pieces),))],
+        compiler_params=pltpu.CompilerParams(vmem_limit_bytes=1 << 20),
+        name="join",
+    )(*pieces)
     axes = ("lon", "lat")
     got = {}
     for k in (3, 1, 2):
@@ -382,22 +390,25 @@
 
     col = jax.ShapeDtypeStruct((point_rows, rows, half), bf16)
     whole = pl.BlockSpec((points, rows, half), lambda i: (0, 0, 0))
-    col_a, col_b = pl.pallas_call(
+    odd = lat % 2 == 1
+    near_col, other_col = pl.pallas_call(
         root_kernel,
         grid=(1,),
         out_shape=(col, col),
-        in_specs=[whole] * (1 + len(seconds)),
+        in_specs=[smem] + [whole] * (1 + len(seconds)),
         out_specs=(pl.BlockSpec((point_rows, rows, half), lambda i: (0, 0, 0)),) * 2,
-        compiler_params=pltpu.CompilerParams(vmem_limit_bytes=2 * GRANT),
+        compiler_params=pltpu.CompilerParams(vmem_limit_bytes=16 << 20),
         cost_estimate=pl.CostEstimate(
             flops=4 * 12 * 2 * 256**3, bytes_accessed=2 << 20, transcendentals=0
         ),
         name="root",
-    )(own, *seconds)
-
-    right = lax.ppermute(col_a, "lat", [(i + 1, i) for i in range(lat_count - 1)])
-    left = lax.ppermute(col_b, "lat", [(i, i + 1) for i in range(lat_count - 1)])
-    cols = [left, col_a, col_b, right]
+    )((lat % 2).astype(jnp.int32).reshape(1), own, *seconds)
+
+    near_got = lax.ppermute(near_col, "lat", [(i, i ^ 1) for i in range(lat_count)])
+    other_got = lax.ppermute(
+        other_col, "lat", [(i, (i - 1 ^ 1) + 1) for i in range(1, lat_count - 1)]
+    )
+    cols = [other_got, other_col, near_col, near_got]
     top = jnp.stack([c[0] for c in cols])
     bottom = jnp.stack([c[1] for c in cols])
     inside = lax.ppermute(
@@ -421,7 +432,7 @@
         jnp.where(y_first, 3, 2),
         jnp.where(local_row >= point_rows, jnp.where(y_first, 2, 3), local_row),
     )
-    places = block * 4 + local_col
+    places = block * 4 + jnp.where(odd, 3 - local_col, local_col)
     per = 4
     result = pl.pallas_call(
         state_kernel,
@@ -435,7 +446,7 @@
             vmem,
         ],
         out_specs=pl.BlockSpec((per, cells, members), lambda i: (i, 0, 0)),
-        compiler_params=pltpu.CompilerParams(vmem_limit_bytes=GRANT),
+        compiler_params=pltpu.CompilerParams(vmem_limit_bytes=12 << 20),
         cost_estimate=pl.CostEstimate(
             flops=2 * 16 * 512 * 256 * 256, bytes_accessed=11 << 20, transcendentals=0
         ),

time: 132 us -> 125 us (0.947)
  Pallas kernels: 37.7 us -> 27.8 us
  waiting for transfers between devices: 42.3 us -> 38.5 us
  local copies, waits for them, and re-layouts: 5.46 us -> 8.83 us
  starting transfers between devices: 39.3 us -> 41.5 us
    pallas_call x4, Pallas kernels: 28.4 us -> 15.1 us  [gram(): pl.pallas_call(functools.partial(gram_kernel, points, ranks), grid=(SIDE,...]
    pallas_call x1 -> x2, Pallas kernels: 3.82 us -> 7.27 us  [the longest x1 4.51 us: local(): pl.pallas_call(root_kernel, grid=(1,), out_shape=(col, col), in_specs=[sm...]
    unnamed x22 -> x26, local copies, waits for them, and re-layouts: 0.14 us -> 3.52 us
    ppermute x3, starting transfers between devices: 1.62 us -> 3.48 us  [local(): lax.ppermute(total(k).astype(bf16), axes, turn(1, k, chips))]
    ppermute x3, waiting for transfers between devices: 8.57 us -> 6.72 us  [local(): lax.ppermute(total(k).astype(bf16), axes, turn(1, k, chips))]
    ppermute x3, starting transfers between devices: 3.51 us -> 5.12 us  [local(): got[k] = lax.ppermute(gram(k), axes, turn(0, k, chips))]
    ppermute x2, starting transfers between devices: 5.28 us -> 3.7 us  [the longest x1 3.62 us: local(): lax.ppermute(other_col, 'lat', [(i, (i - 1 ^ 1) + 1) for i in range(1, la...]
    ppermute x1, starting transfers between devices: 1.92 us -> 3.36 us  [local(): lax.ppermute(jnp.where(y_first, top, bottom), 'lon', [(i, (i ^ 1) + (2 if...]
  transfers between devices with their start and end apart: 21 -> 21, of which waited for: 12 -> 10; matrix products, arithmetic and copies ran while one was open for 7% -> 7% of each run, Pallas kernels for 16% -> 10%
where the time goes in v4:
time: 125 us; the launch traced here: 124 us
  starting transfers between devices  41.5 us (33%)
  waiting for transfers between devices  38.5 us (31%)
  Pallas kernels  27.8 us (22%)
  local copies, waits for them, and re-layouts  8.83 us (7%)
  other arithmetic  6.11 us (5%)
    pallas_call x4, Pallas kernels, gram(): pl.pallas_call(functools.partial(gram_kernel, points, ranks), grid=(SIDE,...  15.1 us
    ppermute x4, waiting for transfers between devices, send(): return lax.ppermute(x, 'lon', pairs)  9.48 us
    ppermute x3, waiting for transfers between devices, local(): got[k] = lax.ppermute(gram(k), axes, turn(0, k, chips))  7.95 us
    ppermute x3, waiting for transfers between devices, local(): lax.ppermute(total(k).astype(bf16), axes, turn(1, k, chips))  6.72 us
    all_to_all x1, starting transfers between devices, local(): asked = lax.all_to_all(asked, 'lat', 0, 0, tiled=True)  6.61 us
    ppermute x4, starting transfers between devices, send(): return lax.ppermute(x, 'lon', pairs)  6.51 us
    pallas_call x1, Pallas kernels, local(): pl.pallas_call(state_kernel, grid=(tiles // per,), out_shape=jax.ShapeDty...  5.53 us
    ppermute x3, starting transfers between devices, local(): got[k] = lax.ppermute(gram(k), axes, turn(0, k, chips))  5.12 us
  transfers between devices with their start and end apart: 21, of which 10 were waited for; matrix products, arithmetic and copies ran while one was open for 7% of the time, Pallas kernels for 10%

profile of v4, /device:TPU:25, one launch (start us, length us, event | category | flops | bytes accessed | tf_op | source)
XLA Modules:
  0.0 123.6 jit_solution(5677539383338493130)
XLA Ops:
  1.6 2.2 %collective-permute-start.1 = (bf16[16,128,256]{2,1,0:T(8,128)(2,1)}, bf16[16,128,256]{2,1,0:T(8,128)(2,1)S(1)}, u32[]{:S(2)}, u32[]{:S(2)}) collective-permute-start(bf16[16,128,256]{2,1,0:T(8,128)(2,1)} %refs_0_.1), channel_id=1, source_target_pairs={{0,96},{16,112},{32,0},{48,16},{64,32},{80,48},{96,64},{112,80},{1... | collective-permute-start | bytes 3145736 | tf_op jit(solution)/shard_map/ppermute | solution.py:223
  10.3 6.6 %all-to-all-start = ((f32[16,1,132]{2,1,0:T(1,128)}), f32[16,1,132]{2,1,0:T(1,128)S(1)}, u32[]{:S(2)}, u32[]{:S(2)}) async-start(f32[16,1,132]{2,1,0:T(1,128)} %all_to_all.11), calls=%async_computation | async-start | bytes 32768 | tf_op jit(solution)/shard_map/all_to_all | solution.py:305
  17.2 4.4 %all-to-all-done = f32[16,1,132]{2,1,0:T(1,128)S(1)} async-done(((f32[16,1,132]{2,1,0:T(1,128)}), f32[16,1,132]{2,1,0:T(1,128)S(1)}, u32[]{:S(2)}, u32[]{:S(2)}) %all-to-all-start) | async-done | bytes 8480 | tf_op jit(solution)/shard_map/all_to_all | solution.py:305
  22.3 4.7 %all-to-all-start.1 = ((f32[8,16,256]{2,1,0:T(8,128)}), f32[8,16,256]{2,1,0:T(8,128)S(1)}, u32[]{:S(2)}, u32[]{:S(2)}) async-start(f32[8,16,256]{2,1,0:T(8,128)} %broadcast_in_dim.75), calls=%async_computation.1 | async-start | bytes 262144 | tf_op jit(solution)/shard_map/all_to_all | solution.py:280
  33.3 9.5 %collective-permute-done.5.refs_6_ = bf16[8,128,256]{2,1,0:T(8,128)(2,1)} collective-permute-done((bf16[8,128,256]{2,1,0:T(8,128)(2,1)}, bf16[8,128,256]{2,1,0:T(8,128)(2,1)}, u32[]{:S(2)}, u32[]{:S(2)}) %collective-permute-start.5) | collective-permute-done | bytes 524320 | tf_op jit(solution)/shard_map/ppermute | solution.py:223
  46.9 2.8 %join.1.y_ref = bf16[128,128,256]{2,1,0:T(8,128)(2,1)S(1)} custom-call(bf16[16,128,256]{2,1,0:T(8,128)(2,1)S(1)} %copy-done.4, bf16[16,128,256]{2,1,0:T(8,128)(2,1)S(1)} %collective-permute-done.refs_1_, bf16[16,128,256]{2,1,0:T(8,128)(2,1)S(1)} %collective-permute-done.1.refs_2_, bf16[16,128,256]{2,1,0:T(8,128)(2,1)} %collective-permute-done.2.refs_3_, ...), custom_call_target="tpu_custom_call" | custom-call | tf_op jit(solution)/shard_map/join/pallas_call | solution.py:365
  49.7 3.3 %gram.5 = bf16[4,4,272,128]{3,2,1,0:T(8,128)(2,1)S(1)} custom-call(s32[4]{0:T(128)S(1)} %broadcast_select_fusion.4.order, s32[16,68]{1,0:T(8,128)S(1)} %pad_add_fusion.slots, f32[16,64]{1,0:T(8,128)S(1)} %get-tuple-element.32.wts, f32[16,4,4,128]{3,2,1,0:T(4,128)S(1)} %pad_maximum_fusion.2.drive_ref, bf16[128,128,256]{2,1,0:T(8,128)(2,1)S(1)} %join.1.y_ref), custom_call_target="tpu_custom_call" | custom-call | flops 1073741824 | bytes 10485760 | tf_op jit(solution)/shard_map/gram/pallas_call | solution.py:348
  52.9 2.4 %collective-permute-start.9 = (bf16[4,4,272,128]{3,2,1,0:T(8,128)(2,1)S(1)}, bf16[4,4,272,128]{3,2,1,0:T(8,128)(2,1)}, u32[]{:S(2)}, u32[]{:S(2)}) collective-permute-start(bf16[4,4,272,128]{3,2,1,0:T(8,128)(2,1)S(1)} %gram.5), channel_id=1, source_target_pairs={{0,2},{1,3},{2,0},{3,1},{4,6},{5,7},{6,4},{7,5},{8,10},{9,11},{10,... | collective-permute-start | bytes 3342344 | tf_op jit(solution)/shard_map/ppermute | solution.py:377
  55.3 3.8 %gram.6 = bf16[4,4,272,128]{3,2,1,0:T(8,128)(2,1)S(1)} custom-call(s32[4]{0:T(128)S(1)} %broadcast_select_fusion.3.order, s32[16,68]{1,0:T(8,128)S(1)} %pad_add_fusion.slots, f32[16,64]{1,0:T(8,128)S(1)} %get-tuple-element.32.wts, f32[16,4,4,128]{3,2,1,0:T(4,128)S(1)} %pad_maximum_fusion.2.drive_ref, bf16[128,128,256]{2,1,0:T(8,128)(2,1)S(1)} %join.1.y_ref), custom_call_target="tpu_custom_call" | custom-call | flops 1073741824 | bytes 10485760 | tf_op jit(solution)/shard_map/gram/pallas_call | solution.py:348
  59.2 4.3 %gram.7 = bf16[4,4,272,128]{3,2,1,0:T(8,128)(2,1)} custom-call(s32[4]{0:T(128)S(1)} %broadcast_select_fusion.2.order, s32[16,68]{1,0:T(8,128)S(1)} %pad_add_fusion.slots, f32[16,64]{1,0:T(8,128)S(1)} %get-tuple-element.32.wts, f32[16,4,4,128]{3,2,1,0:T(4,128)S(1)} %pad_maximum_fusion.2.drive_ref, bf16[128,128,256]{2,1,0:T(8,128)(2,1)S(1)} %join.1.y_ref), custom_call_target="tpu_custom_call" | custom-call | flops 1073741824 | bytes 10485760 | tf_op jit(solution)/shard_map/gram/pallas_call | solution.py:348
  63.5 2.6 %collective-permute-start.11 = (bf16[4,4,272,128]{3,2,1,0:T(8,128)(2,1)}, bf16[4,4,272,128]{3,2,1,0:T(8,128)(2,1)}, u32[]{:S(2)}, u32[]{:S(2)}) collective-permute-start(bf16[4,4,272,128]{3,2,1,0:T(8,128)(2,1)} %gram.7), channel_id=1, source_target_pairs={{0,3},{1,0},{2,1},{3,2},{4,7},{5,4},{6,5},{7,6},{8,11},{9,8},{10,9... | collective-permute-start | bytes 3342344 | tf_op jit(solution)/shard_map/ppermute | solution.py:377
  66.2 3.4 %copy-done.2 = bf16[128,128,256]{2,1,0:T(8,128)(2,1)S(1)} copy-done((bf16[128,128,256]{2,1,0:T(8,128)(2,1)S(1)}, bf16[128,128,256]{2,1,0:T(8,128)(2,1)}, u32[]{:S(2)}) %copy-start.2) | copy-done | bytes 8388632
  69.5 3.7 %gram.4 = bf16[4,4,272,128]{3,2,1,0:T(8,128)(2,1)S(1)} custom-call(s32[4]{0:T(128)S(1)} %broadcast_select_fusion.5.order, s32[16,68]{1,0:T(8,128)S(1)} %pad_add_fusion.slots, f32[16,64]{1,0:T(8,128)S(1)} %get-tuple-element.32.wts, f32[16,4,4,128]{3,2,1,0:T(4,128)S(1)} %pad_maximum_fusion.2.drive_ref, bf16[128,128,256]{2,1,0:T(8,128)(2,1)S(1)} %copy-done.2), custom_call_target="tpu_custom_call" | custom-call | flops 1073741824 | bytes 10485760 | tf_op jit(solution)/shard_map/gram/pallas_call | solution.py:348
  73.3 7.9 %collective-permute-done.10 = bf16[4,4,272,128]{3,2,1,0:T(8,128)(2,1)} collective-permute-done((bf16[4,4,272,128]{3,2,1,0:T(8,128)(2,1)S(1)}, bf16[4,4,272,128]{3,2,1,0:T(8,128)(2,1)}, u32[]{:S(2)}, u32[]{:S(2)}) %collective-permute-start.10) | collective-permute-done | bytes 1114144 | tf_op jit(solution)/shard_map/ppermute | solution.py:377
  81.2 2.4 %fusion.3 = (bf16[4,272,128]{2,1,0:T(8,128)(2,1)S(1)}, bf16[4,272,128]{2,1,0:T(8,128)(2,1)S(1)}, bf16[4,272,128]{2,1,0:T(8,128)(2,1)S(1)}, f32[4,272,128]{2,1,0:T(8,128)S(1)}) fusion(bf16[4,4,272,128]{3,2,1,0:T(8,128)(2,1)} %collective-permute-done.11, bf16[4,4,272,128]{3,2,1,0:T(8,128)(2,1)} %collective-permute-done.10, ...), kind=kLoop, calls=%fused_computation.13 | loop fusion | flops 4317184 | bytes 5849088 | tf_op jit(solution)/shard_map/add | solution.py:383
  87.2 3.7 %collective-permute-done.12.refs_1_ = bf16[4,272,128]{2,1,0:T(8,128)(2,1)S(1)} collective-permute-done((bf16[4,272,128]{2,1,0:T(8,128)(2,1)S(1)}, bf16[4,272,128]{2,1,0:T(8,128)(2,1)S(1)}, u32[]{:S(2)}, u32[]{:S(2)}) %collective-permute-start.12) | collective-permute-done | bytes 278560 | tf_op jit(solution)/shard_map/ppermute | solution.py:388
  91.0 2.4 %collective-permute-done.13.refs_2_ = bf16[4,272,128]{2,1,0:T(8,128)(2,1)S(1)} collective-permute-done((bf16[4,272,128]{2,1,0:T(8,128)(2,1)S(1)}, bf16[4,272,128]{2,1,0:T(8,128)(2,1)S(1)}, u32[]{:S(2)}, u32[]{:S(2)}) %collective-permute-start.13) | collective-permute-done | bytes 278560 | tf_op jit(solution)/shard_map/ppermute | solution.py:388
  93.9 4.5 %root.1 = (bf16[2,272,128]{2,1,0:T(8,128)(2,1)S(1)}, bf16[2,272,128]{2,1,0:T(8,128)(2,1)S(1)}) custom-call(s32[1]{0:T(128)} %bitcast.3.odd, f32[4,272,128]{2,1,0:T(8,128)S(1)} %get-tuple-element.14.refs_0_, bf16[4,272,128]{2,1,0:T(8,128)(2,1)S(1)} %collective-permute-done.12.refs_1_, bf16[4,272,128]{2,1,0:T(8,128)(2,1)S(1)} %collective-permute-done.13.refs_2_, ...), custom_call_target="tpu_custom_call" | custom-call | flops 1610612736 | bytes 2097152 | tf_op jit(solution)/shard_map/root/pallas_call | solution.py:394
  98.5 3.6 %collective-permute-start.15 = (bf16[2,272,128]{2,1,0:T(8,128)(2,1)S(1)}, bf16[2,272,128]{2,1,0:T(8,128)(2,1)S(1)}, u32[]{:S(2)}, u32[]{:S(2)}) collective-permute-start(bf16[2,272,128]{2,1,0:T(8,128)(2,1)S(1)} %get-tuple-element.7), channel_id=1, source_target_pairs={{1,2},{2,1},{3,4},{4,3},{5,6},{6,5},{7,8},{8,7},{9,10},{10,9},{11,... | collective-permute-start | bytes 417800 | tf_op jit(solution)/shard_map/ppermute | solution.py:408
  102.2 4.2 %collective-permute-done.15 = bf16[2,272,128]{2,1,0:T(8,128)(2,1)S(1)} collective-permute-done((bf16[2,272,128]{2,1,0:T(8,128)(2,1)S(1)}, bf16[2,272,128]{2,1,0:T(8,128)(2,1)S(1)}, u32[]{:S(2)}, u32[]{:S(2)}) %collective-permute-start.15) | collective-permute-done | bytes 139296 | tf_op jit(solution)/shard_map/ppermute | solution.py:408
  106.6 3.5 %collective-permute-start.17 = (bf16[4,272,128]{2,1,0:T(8,128)(2,1)S(1)}, bf16[4,272,128]{2,1,0:T(8,128)(2,1)S(1)}, u32[]{:S(2)}, u32[]{:S(2)}) collective-permute-start(bf16[4,272,128]{2,1,0:T(8,128)(2,1)S(1)} %get-tuple-element.16), channel_id=1, source_target_pairs={{0,16},{16,0},{32,48},{48,32},{64,80},{80,64},{96,112},{112,96},{1... | collective-permute-start | bytes 835592 | tf_op jit(solution)/shard_map/ppermute | solution.py:414
  110.2 3.4 %collective-permute-start.18 = (bf16[4,272,128]{2,1,0:T(8,128)(2,1)S(1)}, bf16[4,272,128]{2,1,0:T(8,128)(2,1)S(1)}, u32[]{:S(2)}, u32[]{:S(2)}) collective-permute-start(bf16[4,272,128]{2,1,0:T(8,128)(2,1)S(1)} %get-tuple-element.15), channel_id=1, source_target_pairs={{16,32},{32,16},{48,64},{64,48},{80,96},{96,80},{17,33},{33,17},{4... | collective-permute-start | bytes 835592 | tf_op jit(solution)/shard_map/ppermute | solution.py:417
  113.6 4.4 %collective-permute-done.18 = bf16[4,272,128]{2,1,0:T(8,128)(2,1)S(1)} collective-permute-done((bf16[4,272,128]{2,1,0:T(8,128)(2,1)S(1)}, bf16[4,272,128]{2,1,0:T(8,128)(2,1)S(1)}, u32[]{:S(2)}, u32[]{:S(2)}) %collective-permute-start.18) | collective-permute-done | bytes 278560 | tf_op jit(solution)/shard_map/ppermute | solution.py:417
  118.1 5.5 %state.1 = bf16[16,512,256]{2,1,0:T(8,128)(2,1)} custom-call(s32[16,4]{1,0:T(8,128)S(1)} %fusion.9.places, f32[16,4]{1,0:T(8,128)S(1)} %bitcast.26, f32[16,1,512]{2,1,0:T(1,128)S(1)} %reshape.192.mean_ref, bf16[16,512,256]{2,1,0:T(8,128)(2,1)S(1)} %bitcast.25, bf16[16,272,128]{2,1,0:T(8,128)(2,1)S(1)} %constant_dynamic-update-slice_fusion.w_ref), custom_call_target="tpu_custom_call" | custom-call | flops 1073741824 | bytes 11534336 | tf_op jit(solution)/shard_map/state/pallas_call | solution.py:437
  (101 shorter events, 24.0 us)
Async XLA Ops:
  0.0 27.0 %collective-permute-start = (bf16[16,128,256]{2,1,0:T(8,128)(2,1)}, bf16[16,128,256]{2,1,0:T(8,128)(2,1)S(1)}, u32[]{:S(2)}, u32[]{:S(2)}) collective-permute-start(bf16[16,128,256]{2,1,0:T(8,128)(2,1)} %refs_0_.1), channel_id=1, source_target_pairs={{0,32},{16,48},{32,64},{48,80},{64,96},{80,112},{96,0},{112,16},{1... | collective-permute-start | bytes 3145736 | tf_op jit(solution)/shard_map/ppermute | solution.py:223
  1.6 27.6 %collective-permute-start.1 = (bf16[16,128,256]{2,1,0:T(8,128)(2,1)}, bf16[16,128,256]{2,1,0:T(8,128)(2,1)S(1)}, u32[]{:S(2)}, u32[]{:S(2)}) collective-permute-start(bf16[16,128,256]{2,1,0:T(8,128)(2,1)} %refs_0_.1), channel_id=1, source_target_pairs={{0,96},{16,112},{32,0},{48,16},{64,32},{80,48},{96,64},{112,80},{1... | collective-permute-start | bytes 3145736 | tf_op jit(solution)/shard_map/ppermute | solution.py:223
  3.8 41.7 %collective-permute-start.2 = (bf16[16,128,256]{2,1,0:T(8,128)(2,1)}, bf16[16,128,256]{2,1,0:T(8,128)(2,1)}, u32[]{:S(2)}, u32[]{:S(2)}) collective-permute-start(bf16[16,128,256]{2,1,0:T(8,128)(2,1)} %refs_0_.1), channel_id=1, source_target_pairs={{0,16},{16,0},{32,48},{48,32},{64,80},{80,64},{96,112},{112,96},{1... | collective-permute-start | bytes 3145736 | tf_op jit(solution)/shard_map/ppermute | solution.py:226
  10.3 11.4 %all-to-all-start = ((f32[16,1,132]{2,1,0:T(1,128)}), f32[16,1,132]{2,1,0:T(1,128)S(1)}, u32[]{:S(2)}, u32[]{:S(2)}) async-start(f32[16,1,132]{2,1,0:T(1,128)} %all_to_all.11), calls=%async_computation | async-start | bytes 32768 | tf_op jit(solution)/shard_map/all_to_all | solution.py:305
  22.3 22.9 %all-to-all-start.1 = ((f32[8,16,256]{2,1,0:T(8,128)}), f32[8,16,256]{2,1,0:T(8,128)S(1)}, u32[]{:S(2)}, u32[]{:S(2)}) async-start(f32[8,16,256]{2,1,0:T(8,128)} %broadcast_in_dim.75), calls=%async_computation.1 | async-start | bytes 262144 | tf_op jit(solution)/shard_map/all_to_all | solution.py:280
  27.9 14.9 %collective-permute-start.5 = (bf16[8,128,256]{2,1,0:T(8,128)(2,1)}, bf16[8,128,256]{2,1,0:T(8,128)(2,1)}, u32[]{:S(2)}, u32[]{:S(2)}) collective-permute-start(bf16[8,128,256]{2,1,0:T(8,128)(2,1)} %slice.121), channel_id=1, source_target_pairs={{0,32},{16,48},{32,64},{48,80},{64,96},{80,112},{96,0},{112,16},{1... | collective-permute-start | bytes 1572872 | tf_op jit(solution)/shard_map/ppermute | solution.py:223
  30.1 14.2 %collective-permute-start.6 = (bf16[8,128,256]{2,1,0:T(8,128)(2,1)}, bf16[8,128,256]{2,1,0:T(8,128)(2,1)}, u32[]{:S(2)}, u32[]{:S(2)}) collective-permute-start(bf16[8,128,256]{2,1,0:T(8,128)(2,1)} %slice.122), channel_id=1, source_target_pairs={{0,96},{16,112},{32,0},{48,16},{64,32},{80,48},{96,64},{112,80},{1... | collective-permute-start | bytes 1572872 | tf_op jit(solution)/shard_map/ppermute | solution.py:223
  31.4 15.5 %collective-permute-start.3 = (bf16[16,128,256]{2,1,0:T(8,128)(2,1)S(1)}, bf16[16,128,256]{2,1,0:T(8,128)(2,1)}, u32[]{:S(2)}, u32[]{:S(2)}) collective-permute-start(bf16[16,128,256]{2,1,0:T(8,128)(2,1)S(1)} %collective-permute-done.refs_1_), channel_id=1, source_target_pairs={{0,16},{16,0},{32,48},{48,32},{64,80},{80,64},{96,112},{112,96},{1... | collective-permute-start | bytes 3145736 | tf_op jit(solution)/shard_map/ppermute | solution.py:226
  33.0 13.9 %collective-permute-start.4 = (bf16[16,128,256]{2,1,0:T(8,128)(2,1)S(1)}, bf16[16,128,256]{2,1,0:T(8,128)(2,1)}, u32[]{:S(2)}, u32[]{:S(2)}) collective-permute-start(bf16[16,128,256]{2,1,0:T(8,128)(2,1)S(1)} %collective-permute-done.1.refs_2_), channel_id=1, source_target_pairs={{0,16},{16,0},{32,48},{48,32},{64,80},{80,64},{96,112},{112,96},{1... | collective-permute-start | bytes 3145736 | tf_op jit(solution)/shard_map/ppermute | solution.py:226
  42.8 3.3 %collective-permute-start.7 = (bf16[8,128,256]{2,1,0:T(8,128)(2,1)}, bf16[8,128,256]{2,1,0:T(8,128)(2,1)}, u32[]{:S(2)}, u32[]{:S(2)}) collective-permute-start(bf16[8,128,256]{2,1,0:T(8,128)(2,1)} %collective-permute-done.5.refs_6_), channel_id=1, source_target_pairs={{0,16},{16,0},{32,48},{48,32},{64,80},{80,64},{96,112},{112,96},{1... | collective-permute-start | bytes 1572872 | tf_op jit(solution)/shard_map/ppermute | solution.py:226
  44.3 2.6 %collective-permute-start.8 = (bf16[8,128,256]{2,1,0:T(8,128)(2,1)}, bf16[8,128,256]{2,1,0:T(8,128)(2,1)}, u32[]{:S(2)}, u32[]{:S(2)}) collective-permute-start(bf16[8,128,256]{2,1,0:T(8,128)(2,1)} %collective-permute-done.6.refs_7_), channel_id=1, source_target_pairs={{0,16},{16,0},{32,48},{48,32},{64,80},{80,64},{96,112},{112,96},{1... | collective-permute-start | bytes 1572872 | tf_op jit(solution)/shard_map/ppermute | solution.py:226
  52.9 20.3 %collective-permute-start.9 = (bf16[4,4,272,128]{3,2,1,0:T(8,128)(2,1)S(1)}, bf16[4,4,272,128]{3,2,1,0:T(8,128)(2,1)}, u32[]{:S(2)}, u32[]{:S(2)}) collective-permute-start(bf16[4,4,272,128]{3,2,1,0:T(8,128)(2,1)S(1)} %gram.5), channel_id=1, source_target_pairs={{0,2},{1,3},{2,0},{3,1},{4,6},{5,7},{6,4},{7,5},{8,10},{9,11},{10,... | collective-permute-start | bytes 3342344 | tf_op jit(solution)/shard_map/ppermute | solution.py:377
  59.1 22.1 %collective-permute-start.10 = (bf16[4,4,272,128]{3,2,1,0:T(8,128)(2,1)S(1)}, bf16[4,4,272,128]{3,2,1,0:T(8,128)(2,1)}, u32[]{:S(2)}, u32[]{:S(2)}) collective-permute-start(bf16[4,4,272,128]{3,2,1,0:T(8,128)(2,1)S(1)} %gram.6), channel_id=1, source_target_pairs={{0,1},{1,2},{2,3},{3,0},{4,5},{5,6},{6,7},{7,4},{8,9},{9,10},{10,1... | collective-permute-start | bytes 3342344 | tf_op jit(solution)/shard_map/ppermute | solution.py:377
  63.5 17.7 %collective-permute-start.11 = (bf16[4,4,272,128]{3,2,1,0:T(8,128)(2,1)}, bf16[4,4,272,128]{3,2,1,0:T(8,128)(2,1)}, u32[]{:S(2)}, u32[]{:S(2)}) collective-permute-start(bf16[4,4,272,128]{3,2,1,0:T(8,128)(2,1)} %gram.7), channel_id=1, source_target_pairs={{0,3},{1,0},{2,1},{3,2},{4,7},{5,4},{6,5},{7,6},{8,11},{9,8},{10,9... | collective-permute-start | bytes 3342344 | tf_op jit(solution)/shard_map/ppermute | solution.py:377
  73.3 13.9 %copy-start.6 = (f32[4,4,512]{2,1,0:T(4,128)S(1)}, f32[4,4,512]{2,1,0:T(4,128)}, u32[]{:S(2)}) copy-start(f32[4,4,512]{2,1,0:T(4,128)} %param.14) | copy-start | bytes 98308
  83.7 7.3 %collective-permute-start.12 = (bf16[4,272,128]{2,1,0:T(8,128)(2,1)S(1)}, bf16[4,272,128]{2,1,0:T(8,128)(2,1)S(1)}, u32[]{:S(2)}, u32[]{:S(2)}) collective-permute-start(bf16[4,272,128]{2,1,0:T(8,128)(2,1)S(1)} %get-tuple-element.13), channel_id=1, source_target_pairs={{0,8},{1,9},{2,10},{3,11},{4,12},{5,13},{6,14},{7,15},{8,0},{9,1},... | collective-permute-start | bytes 835592 | tf_op jit(solution)/shard_map/ppermute | solution.py:388
  85.7 7.7 %collective-permute-start.13 = (bf16[4,272,128]{2,1,0:T(8,128)(2,1)S(1)}, bf16[4,272,128]{2,1,0:T(8,128)(2,1)S(1)}, u32[]{:S(2)}, u32[]{:S(2)}) collective-permute-start(bf16[4,272,128]{2,1,0:T(8,128)(2,1)S(1)} %get-tuple-element.12), channel_id=1, source_target_pairs={{0,4},{1,5},{2,6},{3,7},{4,8},{5,9},{6,10},{7,11},{8,12},{9,13},{1... | collective-permute-start | bytes 835592 | tf_op jit(solution)/shard_map/ppermute | solution.py:388
  86.3 7.7 %collective-permute-start.14 = (bf16[4,272,128]{2,1,0:T(8,128)(2,1)S(1)}, bf16[4,272,128]{2,1,0:T(8,128)(2,1)S(1)}, u32[]{:S(2)}, u32[]{:S(2)}) collective-permute-start(bf16[4,272,128]{2,1,0:T(8,128)(2,1)S(1)} %get-tuple-element.11), channel_id=1, source_target_pairs={{0,12},{1,13},{2,14},{3,15},{4,0},{5,1},{6,2},{7,3},{8,4},{9,5},{1... | collective-permute-start | bytes 835592 | tf_op jit(solution)/shard_map/ppermute | solution.py:388
  98.5 7.9 %collective-permute-start.15 = (bf16[2,272,128]{2,1,0:T(8,128)(2,1)S(1)}, bf16[2,272,128]{2,1,0:T(8,128)(2,1)S(1)}, u32[]{:S(2)}, u32[]{:S(2)}) collective-permute-start(bf16[2,272,128]{2,1,0:T(8,128)(2,1)S(1)} %get-tuple-element.7), channel_id=1, source_target_pairs={{1,2},{2,1},{3,4},{4,3},{5,6},{6,5},{7,8},{8,7},{9,10},{10,9},{11,... | collective-permute-start | bytes 417800 | tf_op jit(solution)/shard_map/ppermute | solution.py:408
  102.1 4.4 %collective-permute-start.16 = (bf16[2,272,128]{2,1,0:T(8,128)(2,1)S(1)}, bf16[2,272,128]{2,1,0:T(8,128)(2,1)S(1)}, u32[]{:S(2)}, u32[]{:S(2)}) collective-permute-start(bf16[2,272,128]{2,1,0:T(8,128)(2,1)S(1)} %get-tuple-element.8), channel_id=1, source_target_pairs={{0,1},{1,0},{2,3},{3,2},{4,5},{5,4},{6,7},{7,6},{8,9},{9,8},{10,11... | collective-permute-start | bytes 417800 | tf_op jit(solution)/shard_map/ppermute | solution.py:407
  106.4 11.7 %copy-start.3 = (bf16[4,4,512,256]{3,2,1,0:T(8,128)(2,1)S(1)}, bf16[4,4,512,256]{3,2,1,0:T(8,128)(2,1)}, u32[]{:S(2)}) copy-start(bf16[4,4,512,256]{3,2,1,0:T(8,128)(2,1)} %param.15) | copy-start | bytes 12582916
  106.6 11.5 %copy-start.5 = (f32[4,4,4]{2,1,0:T(4,128)S(1)}, f32[4,4,4]{2,1,0:T(4,128)}, u32[]{:S(2)}) copy-start(f32[4,4,4]{2,1,0:T(4,128)} %param.17) | copy-start | bytes 772
  106.6 6.9 %collective-permute-start.17 = (bf16[4,272,128]{2,1,0:T(8,128)(2,1)S(1)}, bf16[4,272,128]{2,1,0:T(8,128)(2,1)S(1)}, u32[]{:S(2)}, u32[]{:S(2)}) collective-permute-start(bf16[4,272,128]{2,1,0:T(8,128)(2,1)S(1)} %get-tuple-element.16), channel_id=1, source_target_pairs={{0,16},{16,0},{32,48},{48,32},{64,80},{80,64},{96,112},{112,96},{1... | collective-permute-start | bytes 835592 | tf_op jit(solution)/shard_map/ppermute | solution.py:414
  110.2 7.9 %collective-permute-start.18 = (bf16[4,272,128]{2,1,0:T(8,128)(2,1)S(1)}, bf16[4,272,128]{2,1,0:T(8,128)(2,1)S(1)}, u32[]{:S(2)}, u32[]{:S(2)}) collective-permute-start(bf16[4,272,128]{2,1,0:T(8,128)(2,1)S(1)} %get-tuple-element.15), channel_id=1, source_target_pairs={{16,32},{32,16},{48,64},{64,48},{80,96},{96,80},{17,33},{33,17},{4... | collective-permute-start | bytes 835592 | tf_op jit(solution)/shard_map/ppermute | solution.py:417
  (7 other events, 51.1 us)

commit v5 on v4

--- a/solution.py
+++ b/solution.py
@@ -49,7 +49,7 @@
     tail = jnp.concatenate(
         [hi, diagonal - hi, vector_rows, jnp.zeros((TAIL - 6, half), f32)], axis=0
     )
-    return matrix[half:, :half].astype(bf16), both.astype(bf16), tail.astype(bf16)
+    return matrix[half:, :half], both, tail
 
 
 def unpack(total):
@@ -101,7 +101,8 @@
         copy.wait()
 
 
-def gram_kernel(points, ranks, order, slots, wts, drive_ref, y_ref, o_ref, acc_ref):
+def gram_kernel(points, ranks, order, slots, wts, drive_ref, y_ref, *refs):
+    added, (o_ref, acc_ref) = refs[:-2], refs[-2:]
     dest = order[pl.program_id(0)]
     half = y_ref.shape[2] // 2
     most = jnp.int32(0)
@@ -131,10 +132,12 @@
                 )
 
     for p in range(points):
-        corner, both, tail = pack(acc_ref[p], drive_ref[dest, p])
-        o_ref[0, p, :half] = corner
-        o_ref[0, p, half : 2 * half] = both
-        o_ref[0, p, 2 * half :] = tail
+        packed = pack(acc_ref[p], drive_ref[dest, p])
+        for i, part in enumerate(packed):
+            at = pl.ds(i * half, part.shape[0])
+            for ref in added:
+                part = part + ref[0, p, at].astype(f32)
+            o_ref[0, p, at] = part.astype(bf16)
 
 
 def root_kernel(odd, *refs):
@@ -176,7 +179,9 @@
         norm = lax.rsqrt(bounds[p])
         root = (lowers[p][0] * norm, lowers[p][1] * norm)
         shift = row_times(row_times(drives[p], root), root)
-        corner, both, tail = pack(root[1] + root[0] * eye, vector_rows(shift, half))
+        corner, both, tail = (
+            v.astype(bf16) for v in pack(root[1] + root[0] * eye, vector_rows(shift, half))
+        )
         row = p // 2
         for flip in range(2):
 
@@ -276,6 +281,7 @@
     column_blocks = lon_count * held
 
     pieces = column_of(obs_rows)
+    innovations, _, _ = lax.optimization_barrier((innovations, pieces[1], pieces[2]))
     project = jnp.einsum("lok,lo->lk", obs_rows, innovations, preferred_element_type=f32)
     column_proj = lax.all_to_all(
         jnp.broadcast_to(project, (lon_count, held, members)), "lon", 0, 0, tiled=True
@@ -336,10 +342,10 @@
     vmem = pl.BlockSpec(memory_space=pltpu.VMEM)
     rows = members + TAIL
     x, y = lat // SIDE, lat % SIDE
-    others = jnp.arange(SIDE, dtype=jnp.int32)
     y_first = lon % 2 == 0
 
-    def gram(k):
+    def gram(k, ways, *added):
+        others = jnp.asarray(ways, jnp.int32)
         order = jnp.where(
             y_first,
             (x + others) % SIDE * SIDE + (y + k) % SIDE,
@@ -347,19 +353,20 @@
         )
         return pl.pallas_call(
             functools.partial(gram_kernel, points, ranks),
-            grid=(SIDE,),
-            out_shape=jax.ShapeDtypeStruct((SIDE, points, rows, half), bf16),
-            in_specs=[smem, smem, smem, vmem, vmem],
+            grid=(len(ways),),
+            out_shape=jax.ShapeDtypeStruct((len(ways), points, rows, half), bf16),
+            in_specs=[smem, smem, smem, vmem, vmem]
+            + [pl.BlockSpec((1, points, rows, half), lambda i: (i, 0, 0, 0))] * len(added),
             out_specs=pl.BlockSpec((1, points, rows, half), lambda i: (i, 0, 0, 0)),
             scratch_shapes=[
                 pltpu.VMEM((points, members, members), f32),
             ],
             compiler_params=pltpu.CompilerParams(vmem_limit_bytes=GRANT),
             cost_estimate=pl.CostEstimate(
-                flops=2 * 16 * 512 * 256 * 256, bytes_accessed=10 << 20, transcendentals=0
+                flops=len(ways) * 8 * 512 * 256 * 256, bytes_accessed=len(ways) << 20, transcendentals=0
             ),
             name="gram",
-        )(order, slots, wts, drive_rows, column_rows)
+        )(order, slots, wts, drive_rows, column_rows, *added)
 
     chips = lon_count // 2
     column_rows = pl.pallas_call(
@@ -372,15 +379,23 @@
         name="join",
     )(*pieces)
     axes = ("lon", "lat")
-    got = {}
-    for k in (3, 1, 2):
-        got[k] = lax.ppermute(gram(k), axes, turn(0, k, chips))
-    got[0] = gram(0)
+    def send(block, k):
+        return lax.ppermute(block, axes, turn(0, k, chips))
+
+    early, late = (0, 1), (2, 3)
+    onward = send(gram(2, early), 1), send(gram(2, late), 3)
+    straight = send(gram(1, late), 1), send(gram(3, early), 3)
+    relayed = (
+        send(gram(1, early, onward[0]), 1),
+        send(gram(3, late, onward[1]), 3),
+    )
+    mine = gram(0, early + late)
 
     def total(k):
-        sums = got[0][k].astype(f32)
-        for part in (2, 1, 3):
-            sums = sums + got[part][k].astype(f32)
+        arrived = (relayed[0], straight[1]) if k in early else (straight[0], relayed[1])
+        sums = mine[k].astype(f32)
+        for part in arrived:
+            sums = sums + part[k % 2].astype(f32)
         return sums
 
     own = total(0)

time: 125 us -> 123 us (0.984)
  waiting for transfers between devices: 38.5 us -> 34.9 us
  Pallas kernels: 27.8 us -> 29.8 us
    ppermute x3 -> x6, waiting for transfers between devices: 7.95 us -> 1.74 us  [send(): return lax.ppermute(block, axes, turn(0, k, chips))]
    add x1 -> x0, other arithmetic: 2.44 us -> none  [total(): sums = sums + got[part][k].astype(f32)]
    pallas_call x4 -> x7, Pallas kernels: 15.1 us -> 17.1 us  [gram(): pl.pallas_call(functools.partial(gram_kernel, points, ranks), grid=(len(w...]
    convert_element_type x0 -> x1, other arithmetic: none -> 1.81 us  [local(): total(k).astype(bf16)]
    ppermute x5, starting transfers between devices: 4.51 us -> 6.21 us  [swap(): return lax.ppermute(x, 'lon', [(i, i ^ 1) for i in range(size)])]
    ppermute x1, starting transfers between devices: 3.5 us -> 5.09 us  [local(): lax.ppermute(jnp.where(y_first, bottom, top), 'lon', [(i, i ^ 1) for i in...]
    ppermute x1, starting transfers between devices: 3.36 us -> 1.92 us  [local(): lax.ppermute(jnp.where(y_first, top, bottom), 'lon', [(i, (i ^ 1) + (2 if...]
    ppermute x1, waiting for transfers between devices: 4.43 us -> 5.86 us  [local(): lax.ppermute(jnp.where(y_first, top, bottom), 'lon', [(i, (i ^ 1) + (2 if...]
  transfers between devices with their start and end apart: 21 -> 24, of which waited for: 10 -> 12; matrix products, arithmetic and copies ran while one was open for 7% -> 7% of each run, Pallas kernels for 10% -> 12%
where the time goes in v5:
time: 123 us; the launch traced here: 121 us
  starting transfers between devices  41.5 us (34%)
  waiting for transfers between devices  34.9 us (28%)
  Pallas kernels  29.8 us (24%)
  local copies, waits for them, and re-layouts  8.85 us (7%)
  other arithmetic  5.51 us (4%)
    pallas_call x7, Pallas kernels, gram(): pl.pallas_call(functools.partial(gram_kernel, points, ranks), grid=(len(w...  17.1 us
    ppermute x4, waiting for transfers between devices, send(): return lax.ppermute(x, 'lon', pairs)  8.53 us
    ppermute x3, waiting for transfers between devices, local(): lax.ppermute(total(k).astype(bf16), axes, turn(1, k, chips))  7.55 us
    all_to_all x1, starting transfers between devices, local(): asked = lax.all_to_all(asked, 'lat', 0, 0, tiled=True)  6.61 us
    ppermute x4, starting transfers between devices, send(): return lax.ppermute(x, 'lon', pairs)  6.51 us
    ppermute x6, starting transfers between devices, send(): return lax.ppermute(block, axes, turn(0, k, chips))  6.24 us
    ppermute x5, starting transfers between devices, swap(): return lax.ppermute(x, 'lon', [(i, i ^ 1) for i in range(size)])  6.21 us
    ppermute x1, waiting for transfers between devices, local(): lax.ppermute(jnp.where(y_first, top, bottom), 'lon', [(i, (i ^ 1) + (2 if...  5.86 us
  transfers between devices with their start and end apart: 24, of which 12 were waited for; matrix products, arithmetic and copies ran while one was open for 7% of the time, Pallas kernels for 12%

profile of v5, /device:TPU:25, one launch (start us, length us, event | category | flops | bytes accessed | tf_op | source)
XLA Modules:
  0.0 121.5 jit_solution(16428924208339023993)
XLA Ops:
  1.6 2.2 %collective-permute-start.1 = (bf16[16,128,256]{2,1,0:T(8,128)(2,1)}, bf16[16,128,256]{2,1,0:T(8,128)(2,1)S(1)}, u32[]{:S(2)}, u32[]{:S(2)}) collective-permute-start(bf16[16,128,256]{2,1,0:T(8,128)(2,1)} %refs_0_.1), channel_id=1, source_target_pairs={{0,96},{16,112},{32,0},{48,16},{64,32},{80,48},{96,64},{112,80},{1... | collective-permute-start | bytes 3145736 | tf_op jit(solution)/shard_map/ppermute | solution.py:228
  10.3 6.6 %all-to-all-start = ((f32[16,1,132]{2,1,0:T(1,128)}), f32[16,1,132]{2,1,0:T(1,128)S(1)}, u32[]{:S(2)}, u32[]{:S(2)}) async-start(f32[16,1,132]{2,1,0:T(1,128)} %all_to_all.11), calls=%async_computation | async-start | bytes 32768 | tf_op jit(solution)/shard_map/all_to_all | solution.py:311
  16.9 4.7 %all-to-all-done = f32[16,1,132]{2,1,0:T(1,128)S(1)} async-done(((f32[16,1,132]{2,1,0:T(1,128)}), f32[16,1,132]{2,1,0:T(1,128)S(1)}, u32[]{:S(2)}, u32[]{:S(2)}) %all-to-all-start) | async-done | bytes 8480 | tf_op jit(solution)/shard_map/all_to_all | solution.py:311
  21.7 5.1 %collective-permute-done.refs_1_ = bf16[16,128,256]{2,1,0:T(8,128)(2,1)S(1)} collective-permute-done((bf16[16,128,256]{2,1,0:T(8,128)(2,1)}, bf16[16,128,256]{2,1,0:T(8,128)(2,1)S(1)}, u32[]{:S(2)}, u32[]{:S(2)}) %collective-permute-start) | collective-permute-done | bytes 1048608 | tf_op jit(solution)/shard_map/ppermute | solution.py:228
  28.5 2.7 %collective-permute-start.6 = (bf16[8,128,256]{2,1,0:T(8,128)(2,1)}, bf16[8,128,256]{2,1,0:T(8,128)(2,1)}, u32[]{:S(2)}, u32[]{:S(2)}) collective-permute-start(bf16[8,128,256]{2,1,0:T(8,128)(2,1)} %slice.106), channel_id=1, source_target_pairs={{0,96},{16,112},{32,0},{48,16},{64,32},{80,48},{96,64},{112,80},{1... | collective-permute-start | bytes 1572872 | tf_op jit(solution)/shard_map/ppermute | solution.py:228
  34.3 3.7 %all-to-all-start.1 = ((f32[8,16,256]{2,1,0:T(8,128)}), f32[8,16,256]{2,1,0:T(8,128)S(1)}, u32[]{:S(2)}, u32[]{:S(2)}) async-start(f32[8,16,256]{2,1,0:T(8,128)} %broadcast_in_dim.75), calls=%async_computation.1 | async-start | bytes 262144 | tf_op jit(solution)/shard_map/all_to_all | solution.py:286
  38.0 3.4 %collective-permute-done.5.refs_6_ = bf16[8,128,256]{2,1,0:T(8,128)(2,1)} collective-permute-done((bf16[8,128,256]{2,1,0:T(8,128)(2,1)}, bf16[8,128,256]{2,1,0:T(8,128)(2,1)}, u32[]{:S(2)}, u32[]{:S(2)}) %collective-permute-start.5) | collective-permute-done | bytes 524320 | tf_op jit(solution)/shard_map/ppermute | solution.py:228
  41.4 2.8 %collective-permute-start.7 = (bf16[8,128,256]{2,1,0:T(8,128)(2,1)}, bf16[8,128,256]{2,1,0:T(8,128)(2,1)}, u32[]{:S(2)}, u32[]{:S(2)}) collective-permute-start(bf16[8,128,256]{2,1,0:T(8,128)(2,1)} %collective-permute-done.5.refs_6_), channel_id=1, source_target_pairs={{0,16},{16,0},{32,48},{48,32},{64,80},{80,64},{96,112},{112,96},{1... | collective-permute-start | bytes 1572872 | tf_op jit(solution)/shard_map/ppermute | solution.py:231
  46.8 2.8 %join.1.y_ref = bf16[128,128,256]{2,1,0:T(8,128)(2,1)S(1)} custom-call(bf16[16,128,256]{2,1,0:T(8,128)(2,1)S(1)} %copy-done.4, bf16[16,128,256]{2,1,0:T(8,128)(2,1)S(1)} %collective-permute-done.refs_1_, bf16[16,128,256]{2,1,0:T(8,128)(2,1)S(1)} %collective-permute-done.1.refs_2_, bf16[16,128,256]{2,1,0:T(8,128)(2,1)} %collective-permute-done.2.refs_3_, ...), custom_call_target="tpu_custom_call" | custom-call | tf_op jit(solution)/shard_map/join/pallas_call | solution.py:372
  49.6 2.3 %gram.8 = bf16[2,4,272,128]{3,2,1,0:T(8,128)(2,1)S(1)} custom-call(s32[2]{0:T(128)S(1)} %broadcast_select_fusion.6.order, s32[16,68]{1,0:T(8,128)S(1)} %pad_add_fusion.slots, f32[16,64]{1,0:T(8,128)S(1)} %get-tuple-element.39.wts, f32[16,4,4,128]{3,2,1,0:T(4,128)S(1)} %pad_maximum_fusion.2.drive_ref, bf16[128,128,256]{2,1,0:T(8,128)(2,1)S(1)} %join.1.y_ref), custom_call_target="tpu_custom_call" | custom-call | flops 536870912 | bytes 2097152 | tf_op jit(solution)/shard_map/gram/pallas_call | solution.py:354
  52.9 2.7 %gram.12 = bf16[2,4,272,128]{3,2,1,0:T(8,128)(2,1)S(1)} custom-call(s32[2]{0:T(128)S(1)} %get-tuple-element.46.order, s32[16,68]{1,0:T(8,128)S(1)} %pad_add_fusion.slots, f32[16,64]{1,0:T(8,128)S(1)} %get-tuple-element.39.wts, f32[16,4,4,128]{3,2,1,0:T(4,128)S(1)} %pad_maximum_fusion.2.drive_ref, bf16[128,128,256]{2,1,0:T(8,128)(2,1)S(1)} %join.1.y_ref), custom_call_target="tpu_custom_call" | custom-call | flops 536870912 | bytes 2097152 | tf_op jit(solution)/shard_map/gram/pallas_call | solution.py:354
  62.5 2.1 %gram.9 = bf16[2,4,272,128]{3,2,1,0:T(8,128)(2,1)S(1)} custom-call(s32[2]{0:T(128)S(1)} %broadcast_select_fusion.7.order, s32[16,68]{1,0:T(8,128)S(1)} %pad_add_fusion.slots, f32[16,64]{1,0:T(8,128)S(1)} %get-tuple-element.39.wts, f32[16,4,4,128]{3,2,1,0:T(4,128)S(1)} %pad_maximum_fusion.2.drive_ref, bf16[128,128,256]{2,1,0:T(8,128)(2,1)S(1)} %join.1.y_ref, ...), custom_call_target="tpu_custom_call" | custom-call | flops 536870912 | bytes 2097152 | tf_op jit(solution)/shard_map/gram/pallas_call | solution.py:354
  64.6 2.1 %collective-permute-start.10 = (bf16[2,4,272,128]{3,2,1,0:T(8,128)(2,1)S(1)}, bf16[2,4,272,128]{3,2,1,0:T(8,128)(2,1)S(1)}, u32[]{:S(2)}, u32[]{:S(2)}) collective-permute-start(bf16[2,4,272,128]{3,2,1,0:T(8,128)(2,1)S(1)} %gram.9), channel_id=1, source_target_pairs={{0,1},{1,2},{2,3},{3,0},{4,5},{5,6},{6,7},{7,4},{8,9},{9,10},{10,1... | collective-permute-start | bytes 1671176 | tf_op jit(solution)/shard_map/ppermute | solution.py:383
  66.7 2.6 %gram.13 = bf16[2,4,272,128]{3,2,1,0:T(8,128)(2,1)S(1)} custom-call(s32[2]{0:T(128)S(1)} %get-tuple-element.47.order, s32[16,68]{1,0:T(8,128)S(1)} %pad_add_fusion.slots, f32[16,64]{1,0:T(8,128)S(1)} %get-tuple-element.39.wts, f32[16,4,4,128]{3,2,1,0:T(4,128)S(1)} %pad_maximum_fusion.2.drive_ref, bf16[128,128,256]{2,1,0:T(8,128)(2,1)S(1)} %join.1.y_ref, ...), custom_call_target="tpu_custom_call" | custom-call | flops 536870912 | bytes 2097152 | tf_op jit(solution)/shard_map/gram/pallas_call | solution.py:354
  69.8 3.4 %copy-done.2 = bf16[128,128,256]{2,1,0:T(8,128)(2,1)S(1)} copy-done((bf16[128,128,256]{2,1,0:T(8,128)(2,1)S(1)}, bf16[128,128,256]{2,1,0:T(8,128)(2,1)}, u32[]{:S(2)}) %copy-start.2) | copy-done | bytes 8388632
  73.1 3.2 %gram.7 = bf16[4,4,272,128]{3,2,1,0:T(8,128)(2,1)S(1)} custom-call(s32[4]{0:T(128)S(1)} %broadcast_select_fusion.8.order, s32[16,68]{1,0:T(8,128)S(1)} %pad_add_fusion.slots, f32[16,64]{1,0:T(8,128)S(1)} %get-tuple-element.39.wts, f32[16,4,4,128]{3,2,1,0:T(4,128)S(1)} %pad_maximum_fusion.2.drive_ref, bf16[128,128,256]{2,1,0:T(8,128)(2,1)S(1)} %copy-done.2), custom_call_target="tpu_custom_call" | custom-call | flops 1073741824 | bytes 4194304 | tf_op jit(solution)/shard_map/gram/pallas_call | solution.py:354
  82.7 4.6 %collective-permute-done.15.refs_1_ = bf16[4,272,128]{2,1,0:T(8,128)(2,1)S(1)} collective-permute-done((bf16[4,272,128]{2,1,0:T(8,128)(2,1)S(1)}, bf16[4,272,128]{2,1,0:T(8,128)(2,1)S(1)}, u32[]{:S(2)}, u32[]{:S(2)}) %collective-permute-start.15) | collective-permute-done | bytes 278560 | tf_op jit(solution)/shard_map/ppermute | solution.py:403
  87.5 2.7 %collective-permute-done.17.refs_3_ = bf16[4,272,128]{2,1,0:T(8,128)(2,1)S(1)} collective-permute-done((bf16[4,272,128]{2,1,0:T(8,128)(2,1)S(1)}, bf16[4,272,128]{2,1,0:T(8,128)(2,1)S(1)}, u32[]{:S(2)}, u32[]{:S(2)}) %collective-permute-start.17) | collective-permute-done | bytes 278560 | tf_op jit(solution)/shard_map/ppermute | solution.py:403
  90.2 4.5 %root.1 = (bf16[2,272,128]{2,1,0:T(8,128)(2,1)S(1)}, bf16[2,272,128]{2,1,0:T(8,128)(2,1)S(1)}) custom-call(s32[1]{0:T(128)} %bitcast.3.odd, f32[4,272,128]{2,1,0:T(8,128)S(1)} %get-tuple-element.20.refs_0_, bf16[4,272,128]{2,1,0:T(8,128)(2,1)S(1)} %collective-permute-done.15.refs_1_, bf16[4,272,128]{2,1,0:T(8,128)(2,1)S(1)} %collective-permute-done.16.refs_2_, ...), custom_call_target="tpu_custom_call" | custom-call | flops 1610612736 | bytes 2097152 | tf_op jit(solution)/shard_map/root/pallas_call | solution.py:409
  94.7 2.5 %collective-permute-start.18 = (bf16[2,272,128]{2,1,0:T(8,128)(2,1)S(1)}, bf16[2,272,128]{2,1,0:T(8,128)(2,1)S(1)}, u32[]{:S(2)}, u32[]{:S(2)}) collective-permute-start(bf16[2,272,128]{2,1,0:T(8,128)(2,1)S(1)} %get-tuple-element.9), channel_id=1, source_target_pairs={{1,2},{2,1},{3,4},{4,3},{5,6},{6,5},{7,8},{8,7},{9,10},{10,9},{11,... | collective-permute-start | bytes 417800 | tf_op jit(solution)/shard_map/ppermute | solution.py:423
  97.4 5.3 %collective-permute-done.18 = bf16[2,272,128]{2,1,0:T(8,128)(2,1)S(1)} collective-permute-done((bf16[2,272,128]{2,1,0:T(8,128)(2,1)S(1)}, bf16[2,272,128]{2,1,0:T(8,128)(2,1)S(1)}, u32[]{:S(2)}, u32[]{:S(2)}) %collective-permute-start.18) | collective-permute-done | bytes 139296 | tf_op jit(solution)/shard_map/ppermute | solution.py:423
  102.9 5.1 %collective-permute-start.20 = (bf16[4,272,128]{2,1,0:T(8,128)(2,1)S(1)}, bf16[4,272,128]{2,1,0:T(8,128)(2,1)S(1)}, u32[]{:S(2)}, u32[]{:S(2)}) collective-permute-start(bf16[4,272,128]{2,1,0:T(8,128)(2,1)S(1)} %get-tuple-element.23), channel_id=1, source_target_pairs={{0,16},{16,0},{32,48},{48,32},{64,80},{80,64},{96,112},{112,96},{1... | collective-permute-start | bytes 835592 | tf_op jit(solution)/shard_map/ppermute | solution.py:429
  110.0 5.9 %collective-permute-done.21 = bf16[4,272,128]{2,1,0:T(8,128)(2,1)S(1)} collective-permute-done((bf16[4,272,128]{2,1,0:T(8,128)(2,1)S(1)}, bf16[4,272,128]{2,1,0:T(8,128)(2,1)S(1)}, u32[]{:S(2)}, u32[]{:S(2)}) %collective-permute-start.21) | collective-permute-done | bytes 278560 | tf_op jit(solution)/shard_map/ppermute | solution.py:432
  116.0 5.5 %state.1 = bf16[16,512,256]{2,1,0:T(8,128)(2,1)} custom-call(s32[16,4]{1,0:T(8,128)S(1)} %fusion.9.places, f32[16,4]{1,0:T(8,128)S(1)} %bitcast.26, f32[16,1,512]{2,1,0:T(1,128)S(1)} %reshape.184.mean_ref, bf16[16,512,256]{2,1,0:T(8,128)(2,1)S(1)} %bitcast.25, bf16[16,272,128]{2,1,0:T(8,128)(2,1)S(1)} %constant_dynamic-update-slice_fusion.w_ref), custom_call_target="tpu_custom_call" | custom-call | flops 1073741824 | bytes 11534336 | tf_op jit(solution)/shard_map/state/pallas_call | solution.py:452
  (114 shorter events, 32.7 us)
Async XLA Ops:
  0.0 26.9 %collective-permute-start = (bf16[16,128,256]{2,1,0:T(8,128)(2,1)}, bf16[16,128,256]{2,1,0:T(8,128)(2,1)S(1)}, u32[]{:S(2)}, u32[]{:S(2)}) collective-permute-start(bf16[16,128,256]{2,1,0:T(8,128)(2,1)} %refs_0_.1), channel_id=1, source_target_pairs={{0,32},{16,48},{32,64},{48,80},{64,96},{80,112},{96,0},{112,16},{1... | collective-permute-start | bytes 3145736 | tf_op jit(solution)/shard_map/ppermute | solution.py:228
  1.6 26.1 %collective-permute-start.1 = (bf16[16,128,256]{2,1,0:T(8,128)(2,1)}, bf16[16,128,256]{2,1,0:T(8,128)(2,1)S(1)}, u32[]{:S(2)}, u32[]{:S(2)}) collective-permute-start(bf16[16,128,256]{2,1,0:T(8,128)(2,1)} %refs_0_.1), channel_id=1, source_target_pairs={{0,96},{16,112},{32,0},{48,16},{64,32},{80,48},{96,64},{112,80},{1... | collective-permute-start | bytes 3145736 | tf_op jit(solution)/shard_map/ppermute | solution.py:228
  3.8 41.7 %collective-permute-start.2 = (bf16[16,128,256]{2,1,0:T(8,128)(2,1)}, bf16[16,128,256]{2,1,0:T(8,128)(2,1)}, u32[]{:S(2)}, u32[]{:S(2)}) collective-permute-start(bf16[16,128,256]{2,1,0:T(8,128)(2,1)} %refs_0_.1), channel_id=1, source_target_pairs={{0,16},{16,0},{32,48},{48,32},{64,80},{80,64},{96,112},{112,96},{1... | collective-permute-start | bytes 3145736 | tf_op jit(solution)/shard_map/ppermute | solution.py:231
  10.3 11.4 %all-to-all-start = ((f32[16,1,132]{2,1,0:T(1,128)}), f32[16,1,132]{2,1,0:T(1,128)S(1)}, u32[]{:S(2)}, u32[]{:S(2)}) async-start(f32[16,1,132]{2,1,0:T(1,128)} %all_to_all.11), calls=%async_computation | async-start | bytes 32768 | tf_op jit(solution)/shard_map/all_to_all | solution.py:311
  27.7 13.7 %collective-permute-start.5 = (bf16[8,128,256]{2,1,0:T(8,128)(2,1)}, bf16[8,128,256]{2,1,0:T(8,128)(2,1)}, u32[]{:S(2)}, u32[]{:S(2)}) collective-permute-start(bf16[8,128,256]{2,1,0:T(8,128)(2,1)} %slice.105), channel_id=1, source_target_pairs={{0,32},{16,48},{32,64},{48,80},{64,96},{80,112},{96,0},{112,16},{1... | collective-permute-start | bytes 1572872 | tf_op jit(solution)/shard_map/ppermute | solution.py:228
  28.5 15.6 %collective-permute-start.6 = (bf16[8,128,256]{2,1,0:T(8,128)(2,1)}, bf16[8,128,256]{2,1,0:T(8,128)(2,1)}, u32[]{:S(2)}, u32[]{:S(2)}) collective-permute-start(bf16[8,128,256]{2,1,0:T(8,128)(2,1)} %slice.106), channel_id=1, source_target_pairs={{0,96},{16,112},{32,0},{48,16},{64,32},{80,48},{96,64},{112,80},{1... | collective-permute-start | bytes 1572872 | tf_op jit(solution)/shard_map/ppermute | solution.py:228
  31.4 15.4 %collective-permute-start.3 = (bf16[16,128,256]{2,1,0:T(8,128)(2,1)S(1)}, bf16[16,128,256]{2,1,0:T(8,128)(2,1)}, u32[]{:S(2)}, u32[]{:S(2)}) collective-permute-start(bf16[16,128,256]{2,1,0:T(8,128)(2,1)S(1)} %collective-permute-done.refs_1_), channel_id=1, source_target_pairs={{0,16},{16,0},{32,48},{48,32},{64,80},{80,64},{96,112},{112,96},{1... | collective-permute-start | bytes 3145736 | tf_op jit(solution)/shard_map/ppermute | solution.py:231
  33.2 13.6 %collective-permute-start.4 = (bf16[16,128,256]{2,1,0:T(8,128)(2,1)S(1)}, bf16[16,128,256]{2,1,0:T(8,128)(2,1)}, u32[]{:S(2)}, u32[]{:S(2)}) collective-permute-start(bf16[16,128,256]{2,1,0:T(8,128)(2,1)S(1)} %collective-permute-done.1.refs_2_), channel_id=1, source_target_pairs={{0,16},{16,0},{32,48},{48,32},{64,80},{80,64},{96,112},{112,96},{1... | collective-permute-start | bytes 3145736 | tf_op jit(solution)/shard_map/ppermute | solution.py:231
  34.3 10.9 %all-to-all-start.1 = ((f32[8,16,256]{2,1,0:T(8,128)}), f32[8,16,256]{2,1,0:T(8,128)S(1)}, u32[]{:S(2)}, u32[]{:S(2)}) async-start(f32[8,16,256]{2,1,0:T(8,128)} %broadcast_in_dim.75), calls=%async_computation.1 | async-start | bytes 262144 | tf_op jit(solution)/shard_map/all_to_all | solution.py:286
  41.4 4.6 %collective-permute-start.7 = (bf16[8,128,256]{2,1,0:T(8,128)(2,1)}, bf16[8,128,256]{2,1,0:T(8,128)(2,1)}, u32[]{:S(2)}, u32[]{:S(2)}) collective-permute-start(bf16[8,128,256]{2,1,0:T(8,128)(2,1)} %collective-permute-done.5.refs_6_), channel_id=1, source_target_pairs={{0,16},{16,0},{32,48},{48,32},{64,80},{80,64},{96,112},{112,96},{1... | collective-permute-start | bytes 1572872 | tf_op jit(solution)/shard_map/ppermute | solution.py:231
  44.2 2.6 %collective-permute-start.8 = (bf16[8,128,256]{2,1,0:T(8,128)(2,1)}, bf16[8,128,256]{2,1,0:T(8,128)(2,1)}, u32[]{:S(2)}, u32[]{:S(2)}) collective-permute-start(bf16[8,128,256]{2,1,0:T(8,128)(2,1)} %collective-permute-done.6.refs_7_), channel_id=1, source_target_pairs={{0,16},{16,0},{32,48},{48,32},{64,80},{80,64},{96,112},{112,96},{1... | collective-permute-start | bytes 1572872 | tf_op jit(solution)/shard_map/ppermute | solution.py:231
  51.9 10.6 %collective-permute-start.9 = (bf16[2,4,272,128]{3,2,1,0:T(8,128)(2,1)S(1)}, bf16[2,4,272,128]{3,2,1,0:T(8,128)(2,1)S(1)}, u32[]{:S(2)}, u32[]{:S(2)}) collective-permute-start(bf16[2,4,272,128]{3,2,1,0:T(8,128)(2,1)S(1)} %gram.8), channel_id=1, source_target_pairs={{0,1},{1,2},{2,3},{3,0},{4,5},{5,6},{6,7},{7,4},{8,9},{9,10},{10,1... | collective-permute-start | bytes 1671176 | tf_op jit(solution)/shard_map/ppermute | solution.py:383
  55.7 11.0 %collective-permute-start.13 = (bf16[2,4,272,128]{3,2,1,0:T(8,128)(2,1)S(1)}, bf16[2,4,272,128]{3,2,1,0:T(8,128)(2,1)S(1)}, u32[]{:S(2)}, u32[]{:S(2)}) collective-permute-start(bf16[2,4,272,128]{3,2,1,0:T(8,128)(2,1)S(1)} %gram.12), channel_id=1, source_target_pairs={{0,3},{1,0},{2,1},{3,2},{4,7},{5,4},{6,5},{7,6},{8,11},{9,8},{10,9... | collective-permute-start | bytes 1671176 | tf_op jit(solution)/shard_map/ppermute | solution.py:383
  58.8 17.5 %collective-permute-start.11 = (bf16[2,4,272,128]{3,2,1,0:T(8,128)(2,1)S(1)}, bf16[2,4,272,128]{3,2,1,0:T(8,128)(2,1)}, u32[]{:S(2)}, u32[]{:S(2)}) collective-permute-start(bf16[2,4,272,128]{3,2,1,0:T(8,128)(2,1)S(1)} %gram.10), channel_id=1, source_target_pairs={{0,3},{1,0},{2,1},{3,2},{4,7},{5,4},{6,5},{7,6},{8,11},{9,8},{10,9... | collective-permute-start | bytes 1671176 | tf_op jit(solution)/shard_map/ppermute | solution.py:383
  62.0 14.4 %collective-permute-start.12 = (bf16[2,4,272,128]{3,2,1,0:T(8,128)(2,1)S(1)}, bf16[2,4,272,128]{3,2,1,0:T(8,128)(2,1)}, u32[]{:S(2)}, u32[]{:S(2)}) collective-permute-start(bf16[2,4,272,128]{3,2,1,0:T(8,128)(2,1)S(1)} %gram.11), channel_id=1, source_target_pairs={{0,1},{1,2},{2,3},{3,0},{4,5},{5,6},{6,7},{7,4},{8,9},{9,10},{10,1... | collective-permute-start | bytes 1671176 | tf_op jit(solution)/shard_map/ppermute | solution.py:383
  64.6 13.4 %collective-permute-start.10 = (bf16[2,4,272,128]{3,2,1,0:T(8,128)(2,1)S(1)}, bf16[2,4,272,128]{3,2,1,0:T(8,128)(2,1)S(1)}, u32[]{:S(2)}, u32[]{:S(2)}) collective-permute-start(bf16[2,4,272,128]{3,2,1,0:T(8,128)(2,1)S(1)} %gram.9), channel_id=1, source_target_pairs={{0,1},{1,2},{2,3},{3,0},{4,5},{5,6},{6,7},{7,4},{8,9},{9,10},{10,1... | collective-permute-start | bytes 1671176 | tf_op jit(solution)/shard_map/ppermute | solution.py:383
  69.3 8.9 %collective-permute-start.14 = (bf16[2,4,272,128]{3,2,1,0:T(8,128)(2,1)S(1)}, bf16[2,4,272,128]{3,2,1,0:T(8,128)(2,1)}, u32[]{:S(2)}, u32[]{:S(2)}) collective-permute-start(bf16[2,4,272,128]{3,2,1,0:T(8,128)(2,1)S(1)} %gram.13), channel_id=1, source_target_pairs={{0,3},{1,0},{2,1},{3,2},{4,7},{5,4},{6,5},{7,6},{8,11},{9,8},{10,9... | collective-permute-start | bytes 1671176 | tf_op jit(solution)/shard_map/ppermute | solution.py:383
  79.9 7.3 %collective-permute-start.15 = (bf16[4,272,128]{2,1,0:T(8,128)(2,1)S(1)}, bf16[4,272,128]{2,1,0:T(8,128)(2,1)S(1)}, u32[]{:S(2)}, u32[]{:S(2)}) collective-permute-start(bf16[4,272,128]{2,1,0:T(8,128)(2,1)S(1)} %get-tuple-element.17), channel_id=1, source_target_pairs={{0,8},{1,9},{2,10},{3,11},{4,12},{5,13},{6,14},{7,15},{8,0},{9,1},... | collective-permute-start | bytes 835592 | tf_op jit(solution)/shard_map/ppermute | solution.py:403
  80.7 6.8 %collective-permute-start.16 = (bf16[4,272,128]{2,1,0:T(8,128)(2,1)S(1)}, bf16[4,272,128]{2,1,0:T(8,128)(2,1)S(1)}, u32[]{:S(2)}, u32[]{:S(2)}) collective-permute-start(bf16[4,272,128]{2,1,0:T(8,128)(2,1)S(1)} %get-tuple-element.21), channel_id=1, source_target_pairs={{0,4},{1,5},{2,6},{3,7},{4,8},{5,9},{6,10},{7,11},{8,12},{9,13},{1... | collective-permute-start | bytes 835592 | tf_op jit(solution)/shard_map/ppermute | solution.py:403
  82.6 7.6 %collective-permute-start.17 = (bf16[4,272,128]{2,1,0:T(8,128)(2,1)S(1)}, bf16[4,272,128]{2,1,0:T(8,128)(2,1)S(1)}, u32[]{:S(2)}, u32[]{:S(2)}) collective-permute-start(bf16[4,272,128]{2,1,0:T(8,128)(2,1)S(1)} %get-tuple-element.16), channel_id=1, source_target_pairs={{0,12},{1,13},{2,14},{3,15},{4,0},{5,1},{6,2},{7,3},{8,4},{9,5},{1... | collective-permute-start | bytes 835592 | tf_op jit(solution)/shard_map/ppermute | solution.py:403
  94.7 7.9 %collective-permute-start.18 = (bf16[2,272,128]{2,1,0:T(8,128)(2,1)S(1)}, bf16[2,272,128]{2,1,0:T(8,128)(2,1)S(1)}, u32[]{:S(2)}, u32[]{:S(2)}) collective-permute-start(bf16[2,272,128]{2,1,0:T(8,128)(2,1)S(1)} %get-tuple-element.9), channel_id=1, source_target_pairs={{1,2},{2,1},{3,4},{4,3},{5,6},{6,5},{7,8},{8,7},{9,10},{10,9},{11,... | collective-permute-start | bytes 417800 | tf_op jit(solution)/shard_map/ppermute | solution.py:423
  97.3 5.5 %collective-permute-start.19 = (bf16[2,272,128]{2,1,0:T(8,128)(2,1)S(1)}, bf16[2,272,128]{2,1,0:T(8,128)(2,1)S(1)}, u32[]{:S(2)}, u32[]{:S(2)}) collective-permute-start(bf16[2,272,128]{2,1,0:T(8,128)(2,1)S(1)} %get-tuple-element.10), channel_id=1, source_target_pairs={{0,1},{1,0},{2,3},{3,2},{4,5},{5,4},{6,7},{7,6},{8,9},{9,8},{10,11... | collective-permute-start | bytes 417800 | tf_op jit(solution)/shard_map/ppermute | solution.py:422
  102.9 7.1 %collective-permute-start.20 = (bf16[4,272,128]{2,1,0:T(8,128)(2,1)S(1)}, bf16[4,272,128]{2,1,0:T(8,128)(2,1)S(1)}, u32[]{:S(2)}, u32[]{:S(2)}) collective-permute-start(bf16[4,272,128]{2,1,0:T(8,128)(2,1)S(1)} %get-tuple-element.23), channel_id=1, source_target_pairs={{0,16},{16,0},{32,48},{48,32},{64,80},{80,64},{96,112},{112,96},{1... | collective-permute-start | bytes 835592 | tf_op jit(solution)/shard_map/ppermute | solution.py:429
  108.0 7.9 %collective-permute-start.21 = (bf16[4,272,128]{2,1,0:T(8,128)(2,1)S(1)}, bf16[4,272,128]{2,1,0:T(8,128)(2,1)S(1)}, u32[]{:S(2)}, u32[]{:S(2)}) collective-permute-start(bf16[4,272,128]{2,1,0:T(8,128)(2,1)S(1)} %get-tuple-element.22), channel_id=1, source_target_pairs={{16,32},{32,16},{48,64},{64,48},{80,96},{96,80},{17,33},{33,17},{4... | collective-permute-start | bytes 835592 | tf_op jit(solution)/shard_map/ppermute | solution.py:432
  (11 other events, 102.8 us)

commit v6 on v5

--- a/solution.py
+++ b/solution.py
@@ -101,43 +101,54 @@
         copy.wait()
 
 
-def gram_kernel(points, ranks, order, slots, wts, drive_ref, y_ref, *refs):
-    added, (o_ref, acc_ref) = refs[:-2], refs[-2:]
-    dest = order[pl.program_id(0)]
+def gram_kernel(points, ranks, call, outs, slots, wts, drive_ref, y_ref, *refs):
+    added, outs, acc_ref = refs[: -outs - 1], refs[-outs - 1 : -1], refs[-1]
     half = y_ref.shape[2] // 2
+    targets = [(o, way) for o in range(len(outs)) for way in range(outs[o].shape[0])]
+    dests = [slots[wts.shape[0] + call, i] for i in range(len(targets))]
     most = jnp.int32(0)
-    for p in range(points):
-        at = p * ranks
-        ys = [y_ref[slots[dest, at + k]] for k in range(FAST)]
-        yw = [(ys[k].astype(f32) * wts[dest, at + k]).astype(bf16) for k in range(FAST)]
-        acc_ref[p] = lax.dot_general(
-            jnp.concatenate(yw, axis=0),
-            jnp.concatenate(ys, axis=0),
-            (((0,), (0,)), ((), ())),
-            preferred_element_type=f32,
-        )
-        most = jnp.maximum(most, slots[dest, points * ranks + p])
+    for (o, way), dest in zip(targets, dests):
+        o_ref = outs[o]
+        for p in range(points):
+            at = p * ranks
+            ys = [y_ref[slots[dest, at + k]] for k in range(FAST)]
+            yw = [(ys[k].astype(f32) * wts[dest, at + k]).astype(bf16) for k in range(FAST)]
+            gram = lax.dot_general(
+                jnp.concatenate(yw, axis=0),
+                jnp.concatenate(ys, axis=0),
+                (((0,), (0,)), ((), ())),
+                preferred_element_type=f32,
+            )
+            for i, part in enumerate(pack(gram, drive_ref[dest, p])):
+                at = pl.ds(i * half, part.shape[0])
+                if added:
+                    part = part + added[o][way, p, at].astype(f32)
+                o_ref[way, p, at] = part.astype(bf16)
+            most = jnp.maximum(most, slots[dest, points * ranks + p])
 
     @pl.when(most > FAST)
     def _():
-        for p in range(points):
-            at = p * ranks
-
-            @pl.loop(FAST, jnp.maximum(slots[dest, points * ranks + p], FAST))
-            def _(k):
-                y = y_ref[slots[dest, at + k]]
-                w = (y.astype(f32) * wts[dest, at + k]).astype(bf16)
-                acc_ref[p] += lax.dot_general(
-                    w, y, (((0,), (0,)), ((), ())), preferred_element_type=f32
-                )
-
-    for p in range(points):
-        packed = pack(acc_ref[p], drive_ref[dest, p])
-        for i, part in enumerate(packed):
-            at = pl.ds(i * half, part.shape[0])
-            for ref in added:
-                part = part + ref[0, p, at].astype(f32)
-            o_ref[0, p, at] = part.astype(bf16)
+        for (o, way), dest in zip(targets, dests):
+            o_ref = outs[o]
+            for p in range(points):
+                count = slots[dest, points * ranks + p]
+
+                @pl.when(count > FAST)
+                def _(o_ref=o_ref, dest=dest, way=way, p=p, count=count):
+                    acc_ref[...] = jnp.zeros_like(acc_ref)
+
+                    @pl.loop(FAST, count)
+                    def _(k):
+                        y = y_ref[slots[dest, p * ranks + k]]
+                        w = (y.astype(f32) * wts[dest, p * ranks + k]).astype(bf16)
+                        acc_ref[...] += lax.dot_general(
+                            w, y, (((0,), (0,)), ((), ())), preferred_element_type=f32
+                        )
+
+                    rest = pack(acc_ref[...], jnp.zeros((4, half), f32))
+                    for i, part in enumerate(rest):
+                        at = pl.ds(i * half, part.shape[0])
+                        o_ref[way, p, at] = (o_ref[way, p, at].astype(f32) + part).astype(bf16)
 
 
 def root_kernel(odd, *refs):
@@ -344,29 +355,39 @@
     x, y = lat // SIDE, lat % SIDE
     y_first = lon % 2 == 0
 
-    def gram(k, ways, *added):
-        others = jnp.asarray(ways, jnp.int32)
-        order = jnp.where(
-            y_first,
-            (x + others) % SIDE * SIDE + (y + k) % SIDE,
-            (x + k) % SIDE * SIDE + (y + others) % SIDE,
-        )
+    early, late = (0, 1), (2, 3)
+    calls = (
+        ((2, early), (2, late)),
+        ((1, late), (3, early)),
+        ((1, early), (3, late)),
+        ((0, early + late),),
+    )
+    orders = []
+    for results in calls:
+        first = jnp.asarray([k for k, ways in results for _ in ways], jnp.int32)
+        then = jnp.asarray([way for _, ways in results for way in ways], jnp.int32)
+        along_x, along_y = jnp.where(y_first, then, first), jnp.where(y_first, first, then)
+        orders.append((x + along_x) % SIDE * SIDE + (y + along_y) % SIDE)
+    orders = jnp.pad(jnp.stack(orders), ((0, 0), (0, slots.shape[1] - SIDE)))
+    slots = jnp.concatenate([slots, orders], axis=0)
+
+    def gram(call, *added):
+        results = calls[call]
         return pl.pallas_call(
-            functools.partial(gram_kernel, points, ranks),
-            grid=(len(ways),),
-            out_shape=jax.ShapeDtypeStruct((len(ways), points, rows, half), bf16),
-            in_specs=[smem, smem, smem, vmem, vmem]
-            + [pl.BlockSpec((1, points, rows, half), lambda i: (i, 0, 0, 0))] * len(added),
-            out_specs=pl.BlockSpec((1, points, rows, half), lambda i: (i, 0, 0, 0)),
-            scratch_shapes=[
-                pltpu.VMEM((points, members, members), f32),
+            functools.partial(gram_kernel, points, ranks, call, len(results)),
+            out_shape=[
+                jax.ShapeDtypeStruct((len(ways), points, rows, half), bf16)
+                for _, ways in results
             ],
+            in_specs=[smem, smem, vmem, vmem] + [vmem] * len(added),
+            out_specs=[vmem] * len(results),
+            scratch_shapes=[pltpu.VMEM((members, members), f32)],
             compiler_params=pltpu.CompilerParams(vmem_limit_bytes=GRANT),
             cost_estimate=pl.CostEstimate(
-                flops=len(ways) * 8 * 512 * 256 * 256, bytes_accessed=len(ways) << 20, transcendentals=0
+                flops=2 * 16 * 512 * 256 * 256, bytes_accessed=4 << 20, transcendentals=0
             ),
             name="gram",
-        )(order, slots, wts, drive_rows, column_rows, *added)
+        )(slots, wts, drive_rows, column_rows, *added)
 
     chips = lon_count // 2
     column_rows = pl.pallas_call(
@@ -382,14 +403,13 @@
     def send(block, k):
         return lax.ppermute(block, axes, turn(0, k, chips))
 
-    early, late = (0, 1), (2, 3)
-    onward = send(gram(2, early), 1), send(gram(2, late), 3)
-    straight = send(gram(1, late), 1), send(gram(3, early), 3)
-    relayed = (
-        send(gram(1, early, onward[0]), 1),
-        send(gram(3, late, onward[1]), 3),
-    )
-    mine = gram(0, early + late)
+    def both_ways(results):
+        return [send(results[0], 1), send(results[1], 3)]
+
+    onward = both_ways(gram(0))
+    straight = both_ways(gram(1))
+    relayed = both_ways(gram(2, *onward))
+    (mine,) = gram(3)
 
     def total(k):
         arrived = (relayed[0], straight[1]) if k in early else (straight[0], relayed[1])
@@ -426,15 +446,15 @@
     cols = [other_got, other_col, near_col, near_got]
     top = jnp.stack([c[0] for c in cols])
     bottom = jnp.stack([c[1] for c in cols])
-    inside = lax.ppermute(
-        jnp.where(y_first, bottom, top), "lon", [(i, i ^ 1) for i in range(lon_count)]
-    )
     outside = lax.ppermute(
         jnp.where(y_first, top, bottom),
         "lon",
         [(i, (i ^ 1) + (2 if i % 2 else -2)) for i in range(1, lon_count - 1)],
     )
-    held_w = jnp.concatenate([top, bottom, inside, outside], axis=0)
+    inside = lax.ppermute(
+        jnp.where(y_first, bottom, top), "lon", [(i, i ^ 1) for i in range(lon_count)]
+    )
+    held_w = jnp.concatenate([top, bottom, outside, inside], axis=0)
 
     grid_cols = point_cols * lat_count
     tile_rows, tile_cols, cells = state_mean.shape
@@ -444,8 +464,8 @@
     local_col = target_ids % grid_cols - lat * point_cols + 1
     block = jnp.where(
         local_row < 0,
-        jnp.where(y_first, 3, 2),
-        jnp.where(local_row >= point_rows, jnp.where(y_first, 2, 3), local_row),
+        jnp.where(y_first, 2, 3),
+        jnp.where(local_row >= point_rows, jnp.where(y_first, 3, 2), local_row),
     )
     places = block * 4 + jnp.where(odd, 3 - local_col, local_col)
     per = 4

time: 123 us -> 121 us (0.984)
  Pallas kernels: 29.8 us -> 25.2 us
  waiting for transfers between devices: 34.9 us -> 38.3 us
  local copies, waits for them, and re-layouts: 8.85 us -> 5.48 us
  starting transfers between devices: 41.5 us -> 44.1 us
    ppermute x6, waiting for transfers between devices: 1.74 us -> 7.87 us  [send(): return lax.ppermute(block, axes, turn(0, k, chips))]
    ppermute x1, starting transfers between devices: 1.92 us -> 7.22 us  [local(): lax.ppermute(jnp.where(y_first, top, bottom), 'lon', [(i, (i ^ 1) + (2 if...]
    ppermute x1, starting transfers between devices: 5.09 us -> 0.09 us  [local(): lax.ppermute(jnp.where(y_first, bottom, top), 'lon', [(i, i ^ 1) for i in...]
    pallas_call x7 -> x4, Pallas kernels: 17.1 us -> 12.4 us  [gram(): pl.pallas_call(functools.partial(gram_kernel, points, ranks, call, len(re...]
    unnamed x28 -> x26, local copies, waits for them, and re-layouts: 3.52 us -> 0.15 us
    ppermute x1, waiting for transfers between devices: 5.86 us -> 4.05 us  [local(): lax.ppermute(jnp.where(y_first, top, bottom), 'lon', [(i, (i ^ 1) + (2 if...]
    ppermute x6, starting transfers between devices: 6.24 us -> 7.55 us  [send(): return lax.ppermute(block, axes, turn(0, k, chips))]
  transfers between devices with their start and end apart: 24 -> 24, of which waited for: 12 -> 13; matrix products, arithmetic and copies ran while one was open for 7% -> 7% of each run, Pallas kernels for 12% -> 8%
where the time goes in v6:
time: 121 us; the launch traced here: 119 us
  starting transfers between devices  44.1 us (36%)
  waiting for transfers between devices  38.3 us (32%)
  Pallas kernels  25.2 us (21%)
  local copies, waits for them, and re-layouts  5.48 us (5%)
  other arithmetic  4.81 us (4%)
    pallas_call x4, Pallas kernels, gram(): pl.pallas_call(functools.partial(gram_kernel, points, ranks, call, len(re...  12.4 us
    ppermute x4, waiting for transfers between devices, send(): return lax.ppermute(x, 'lon', pairs)  8.52 us
    ppermute x6, waiting for transfers between devices, send(): return lax.ppermute(block, axes, turn(0, k, chips))  7.87 us
    ppermute x6, starting transfers between devices, send(): return lax.ppermute(block, axes, turn(0, k, chips))  7.55 us
    ppermute x1, starting transfers between devices, local(): lax.ppermute(jnp.where(y_first, top, bottom), 'lon', [(i, (i ^ 1) + (2 if...  7.22 us
    ppermute x3, waiting for transfers between devices, local(): lax.ppermute(total(k).astype(bf16), axes, turn(1, k, chips))  7.17 us
    all_to_all x1, starting transfers between devices, local(): asked = lax.all_to_all(asked, 'lat', 0, 0, tiled=True)  6.61 us
    ppermute x4, starting transfers between devices, send(): return lax.ppermute(x, 'lon', pairs)  6.51 us
  transfers between devices with their start and end apart: 24, of which 13 were waited for; matrix products, arithmetic and copies ran while one was open for 7% of the time, Pallas kernels for 8%

profile of v6, /device:TPU:25, one launch (start us, length us, event | category | flops | bytes accessed | tf_op | source)
XLA Modules:
  0.0 118.8 jit_solution(13529255062186610889)
XLA Ops:
  1.6 2.2 %collective-permute-start.1 = (bf16[16,128,256]{2,1,0:T(8,128)(2,1)}, bf16[16,128,256]{2,1,0:T(8,128)(2,1)S(1)}, u32[]{:S(2)}, u32[]{:S(2)}) collective-permute-start(bf16[16,128,256]{2,1,0:T(8,128)(2,1)} %refs_0_.1), channel_id=1, source_target_pairs={{0,96},{16,112},{32,0},{48,16},{64,32},{80,48},{96,64},{112,80},{1... | collective-permute-start | bytes 3145736 | tf_op jit(solution)/shard_map/ppermute | solution.py:239
  10.3 6.6 %all-to-all-start = ((f32[16,1,132]{2,1,0:T(1,128)}), f32[16,1,132]{2,1,0:T(1,128)S(1)}, u32[]{:S(2)}, u32[]{:S(2)}) async-start(f32[16,1,132]{2,1,0:T(1,128)} %all_to_all.11), calls=%async_computation | async-start | bytes 32768 | tf_op jit(solution)/shard_map/all_to_all | solution.py:322
  17.0 4.7 %all-to-all-done = f32[16,1,132]{2,1,0:T(1,128)S(1)} async-done(((f32[16,1,132]{2,1,0:T(1,128)}), f32[16,1,132]{2,1,0:T(1,128)S(1)}, u32[]{:S(2)}, u32[]{:S(2)}) %all-to-all-start) | async-done | bytes 8480 | tf_op jit(solution)/shard_map/all_to_all | solution.py:322
  21.7 5.1 %collective-permute-done.refs_1_ = bf16[16,128,256]{2,1,0:T(8,128)(2,1)S(1)} collective-permute-done((bf16[16,128,256]{2,1,0:T(8,128)(2,1)}, bf16[16,128,256]{2,1,0:T(8,128)(2,1)S(1)}, u32[]{:S(2)}, u32[]{:S(2)}) %collective-permute-start) | collective-permute-done | bytes 1048608 | tf_op jit(solution)/shard_map/ppermute | solution.py:239
  28.5 2.7 %collective-permute-start.6 = (bf16[8,128,256]{2,1,0:T(8,128)(2,1)}, bf16[8,128,256]{2,1,0:T(8,128)(2,1)}, u32[]{:S(2)}, u32[]{:S(2)}) collective-permute-start(bf16[8,128,256]{2,1,0:T(8,128)(2,1)} %slice.106), channel_id=1, source_target_pairs={{0,96},{16,112},{32,0},{48,16},{64,32},{80,48},{96,64},{112,80},{1... | collective-permute-start | bytes 1572872 | tf_op jit(solution)/shard_map/ppermute | solution.py:239
  34.3 3.7 %all-to-all-start.1 = ((f32[8,16,256]{2,1,0:T(8,128)}), f32[8,16,256]{2,1,0:T(8,128)S(1)}, u32[]{:S(2)}, u32[]{:S(2)}) async-start(f32[8,16,256]{2,1,0:T(8,128)} %broadcast_in_dim.75), calls=%async_computation.1 | async-start | bytes 262144 | tf_op jit(solution)/shard_map/all_to_all | solution.py:297
  38.0 3.4 %collective-permute-done.5.refs_6_ = bf16[8,128,256]{2,1,0:T(8,128)(2,1)} collective-permute-done((bf16[8,128,256]{2,1,0:T(8,128)(2,1)}, bf16[8,128,256]{2,1,0:T(8,128)(2,1)}, u32[]{:S(2)}, u32[]{:S(2)}) %collective-permute-start.5) | collective-permute-done | bytes 524320 | tf_op jit(solution)/shard_map/ppermute | solution.py:239
  41.4 2.8 %collective-permute-start.7 = (bf16[8,128,256]{2,1,0:T(8,128)(2,1)}, bf16[8,128,256]{2,1,0:T(8,128)(2,1)}, u32[]{:S(2)}, u32[]{:S(2)}) collective-permute-start(bf16[8,128,256]{2,1,0:T(8,128)(2,1)} %collective-permute-done.5.refs_6_), channel_id=1, source_target_pairs={{0,16},{16,0},{32,48},{48,32},{64,80},{80,64},{96,112},{112,96},{1... | collective-permute-start | bytes 1572872 | tf_op jit(solution)/shard_map/ppermute | solution.py:242
  46.8 2.8 %join.1.y_ref = bf16[128,128,256]{2,1,0:T(8,128)(2,1)S(1)} custom-call(bf16[16,128,256]{2,1,0:T(8,128)(2,1)S(1)} %copy-done.2, bf16[16,128,256]{2,1,0:T(8,128)(2,1)S(1)} %collective-permute-done.refs_1_, bf16[16,128,256]{2,1,0:T(8,128)(2,1)S(1)} %collective-permute-done.1.refs_2_, bf16[16,128,256]{2,1,0:T(8,128)(2,1)} %collective-permute-done.2.refs_3_, ...), custom_call_target="tpu_custom_call" | custom-call | tf_op jit(solution)/shard_map/join/pallas_call | solution.py:393
  49.6 3.0 %gram.5 = (bf16[2,4,272,128]{3,2,1,0:T(8,128)(2,1)S(1)}, bf16[2,4,272,128]{3,2,1,0:T(8,128)(2,1)S(1)}) custom-call(s32[20,68]{1,0:T(8,128)S(1)} %pad_add_fusion.slots, f32[16,64]{1,0:T(8,128)S(1)} %get-tuple-element.48.wts, f32[16,4,4,128]{3,2,1,0:T(4,128)S(1)} %pad_maximum_fusion.2.drive_ref, bf16[128,128,256]{2,1,0:T(8,128)(2,1)S(1)} %join.1.y_ref), custom_call_target="tpu_custom_call" | custom-call | flops 1073741824 | bytes 4194304 | tf_op jit(solution)/shard_map/gram/pallas_call | solution.py:376
  52.6 2.3 %collective-permute-start.10 = (bf16[2,4,272,128]{3,2,1,0:T(8,128)(2,1)S(1)}, bf16[2,4,272,128]{3,2,1,0:T(8,128)(2,1)S(1)}, u32[]{:S(2)}, u32[]{:S(2)}) collective-permute-start(bf16[2,4,272,128]{3,2,1,0:T(8,128)(2,1)S(1)} %get-tuple-element.16), channel_id=1, source_target_pairs={{0,3},{1,0},{2,1},{3,2},{4,7},{5,4},{6,5},{7,6},{8,11},{9,8},{10,9... | collective-permute-start | bytes 1671176 | tf_op jit(solution)/shard_map/ppermute | solution.py:404
  54.9 3.7 %gram.7 = (bf16[2,4,272,128]{3,2,1,0:T(8,128)(2,1)S(1)}, bf16[2,4,272,128]{3,2,1,0:T(8,128)(2,1)S(1)}) custom-call(s32[20,68]{1,0:T(8,128)S(1)} %pad_add_fusion.slots, f32[16,64]{1,0:T(8,128)S(1)} %get-tuple-element.48.wts, f32[16,4,4,128]{3,2,1,0:T(4,128)S(1)} %pad_maximum_fusion.2.drive_ref, bf16[128,128,256]{2,1,0:T(8,128)(2,1)S(1)} %join.1.y_ref), custom_call_target="tpu_custom_call" | custom-call | flops 1073741824 | bytes 4194304 | tf_op jit(solution)/shard_map/gram/pallas_call | solution.py:376
  58.6 2.5 %collective-permute-start.12 = (bf16[2,4,272,128]{3,2,1,0:T(8,128)(2,1)S(1)}, bf16[2,4,272,128]{3,2,1,0:T(8,128)(2,1)S(1)}, u32[]{:S(2)}, u32[]{:S(2)}) collective-permute-start(bf16[2,4,272,128]{3,2,1,0:T(8,128)(2,1)S(1)} %get-tuple-element.18), channel_id=1, source_target_pairs={{0,3},{1,0},{2,1},{3,2},{4,7},{5,4},{6,5},{7,6},{8,11},{9,8},{10,9... | collective-permute-start | bytes 1671176 | tf_op jit(solution)/shard_map/ppermute | solution.py:404
  61.4 3.4 %collective-permute-done.9.refs_0_ = bf16[2,4,272,128]{3,2,1,0:T(8,128)(2,1)S(1)} collective-permute-done((bf16[2,4,272,128]{3,2,1,0:T(8,128)(2,1)S(1)}, bf16[2,4,272,128]{3,2,1,0:T(8,128)(2,1)S(1)}, u32[]{:S(2)}, u32[]{:S(2)}) %collective-permute-start.9) | collective-permute-done | bytes 557088 | tf_op jit(solution)/shard_map/ppermute | solution.py:404
  64.8 2.7 %gram.6 = (bf16[2,4,272,128]{3,2,1,0:T(8,128)(2,1)S(1)}, bf16[2,4,272,128]{3,2,1,0:T(8,128)(2,1)S(1)}) custom-call(s32[20,68]{1,0:T(8,128)S(1)} %pad_add_fusion.slots, f32[16,64]{1,0:T(8,128)S(1)} %get-tuple-element.48.wts, f32[16,4,4,128]{3,2,1,0:T(4,128)S(1)} %pad_maximum_fusion.2.drive_ref, bf16[128,128,256]{2,1,0:T(8,128)(2,1)S(1)} %join.1.y_ref, ...), custom_call_target="tpu_custom_call" | custom-call | flops 1073741824 | bytes 4194304 | tf_op jit(solution)/shard_map/gram/pallas_call | solution.py:376
  67.6 2.7 %collective-permute-start.14 = (bf16[2,4,272,128]{3,2,1,0:T(8,128)(2,1)S(1)}, bf16[2,4,272,128]{3,2,1,0:T(8,128)(2,1)S(1)}, u32[]{:S(2)}, u32[]{:S(2)}) collective-permute-start(bf16[2,4,272,128]{3,2,1,0:T(8,128)(2,1)S(1)} %get-tuple-element.20), channel_id=1, source_target_pairs={{0,3},{1,0},{2,1},{3,2},{4,7},{5,4},{6,5},{7,6},{8,11},{9,8},{10,9... | collective-permute-start | bytes 1671176 | tf_op jit(solution)/shard_map/ppermute | solution.py:404
  70.3 3.0 %gram.4 = bf16[4,4,272,128]{3,2,1,0:T(8,128)(2,1)S(1)} custom-call(s32[20,68]{1,0:T(8,128)S(1)} %pad_add_fusion.slots, f32[16,64]{1,0:T(8,128)S(1)} %get-tuple-element.48.wts, f32[16,4,4,128]{3,2,1,0:T(4,128)S(1)} %pad_maximum_fusion.2.drive_ref, bf16[128,128,256]{2,1,0:T(8,128)(2,1)S(1)} %join.1.y_ref), custom_call_target="tpu_custom_call" | custom-call | flops 1073741824 | bytes 4194304 | tf_op jit(solution)/shard_map/gram/pallas_call | solution.py:376
  73.3 4.2 %collective-permute-done.11 = bf16[2,4,272,128]{3,2,1,0:T(8,128)(2,1)S(1)} collective-permute-done((bf16[2,4,272,128]{3,2,1,0:T(8,128)(2,1)S(1)}, bf16[2,4,272,128]{3,2,1,0:T(8,128)(2,1)S(1)}, u32[]{:S(2)}, u32[]{:S(2)}) %collective-permute-start.11) | collective-permute-done | bytes 557088 | tf_op jit(solution)/shard_map/ppermute | solution.py:404
  81.9 3.9 %collective-permute-done.15.refs_1_ = bf16[4,272,128]{2,1,0:T(8,128)(2,1)S(1)} collective-permute-done((bf16[4,272,128]{2,1,0:T(8,128)(2,1)}, bf16[4,272,128]{2,1,0:T(8,128)(2,1)S(1)}, u32[]{:S(2)}, u32[]{:S(2)}) %collective-permute-start.15) | collective-permute-done | bytes 278560 | tf_op jit(solution)/shard_map/ppermute | solution.py:423
  89.0 4.5 %root.1 = (bf16[2,272,128]{2,1,0:T(8,128)(2,1)S(1)}, bf16[2,272,128]{2,1,0:T(8,128)(2,1)S(1)}) custom-call(s32[1]{0:T(128)} %bitcast.3.odd, f32[4,272,128]{2,1,0:T(8,128)S(1)} %get-tuple-element.29.refs_0_, bf16[4,272,128]{2,1,0:T(8,128)(2,1)S(1)} %collective-permute-done.15.refs_1_, bf16[4,272,128]{2,1,0:T(8,128)(2,1)S(1)} %collective-permute-done.16.refs_2_, ...), custom_call_target="tpu_custom_call" | custom-call | flops 1610612736 | bytes 2097152 | tf_op jit(solution)/shard_map/root/pallas_call | solution.py:429
  96.7 4.8 %collective-permute-done.18 = bf16[2,272,128]{2,1,0:T(8,128)(2,1)S(1)} collective-permute-done((bf16[2,272,128]{2,1,0:T(8,128)(2,1)S(1)}, bf16[2,272,128]{2,1,0:T(8,128)(2,1)S(1)}, u32[]{:S(2)}, u32[]{:S(2)}) %collective-permute-start.18) | collective-permute-done | bytes 139296 | tf_op jit(solution)/shard_map/ppermute | solution.py:443
  101.7 7.2 %collective-permute-start.20 = (bf16[4,272,128]{2,1,0:T(8,128)(2,1)S(1)}, bf16[4,272,128]{2,1,0:T(8,128)(2,1)S(1)}, u32[]{:S(2)}, u32[]{:S(2)}) collective-permute-start(bf16[4,272,128]{2,1,0:T(8,128)(2,1)S(1)} %get-tuple-element.32), channel_id=1, source_target_pairs={{16,32},{32,16},{48,64},{64,48},{80,96},{96,80},{17,33},{33,17},{4... | collective-permute-start | bytes 835592 | tf_op jit(solution)/shard_map/ppermute | solution.py:449
  109.1 4.0 %collective-permute-done.20 = bf16[4,272,128]{2,1,0:T(8,128)(2,1)S(1)} collective-permute-done((bf16[4,272,128]{2,1,0:T(8,128)(2,1)S(1)}, bf16[4,272,128]{2,1,0:T(8,128)(2,1)S(1)}, u32[]{:S(2)}, u32[]{:S(2)}) %collective-permute-start.20) | collective-permute-done | bytes 278560 | tf_op jit(solution)/shard_map/ppermute | solution.py:449
  113.3 5.5 %state.1 = bf16[16,512,256]{2,1,0:T(8,128)(2,1)} custom-call(s32[16,4]{1,0:T(8,128)S(1)} %fusion.9.places, f32[16,4]{1,0:T(8,128)S(1)} %bitcast.34, f32[16,1,512]{2,1,0:T(1,128)S(1)} %reshape.184.mean_ref, bf16[16,512,256]{2,1,0:T(8,128)(2,1)S(1)} %bitcast.33, bf16[16,272,128]{2,1,0:T(8,128)(2,1)S(1)} %constant_dynamic-update-slice_fusion.w_ref), custom_call_target="tpu_custom_call" | custom-call | flops 1073741824 | bytes 11534336 | tf_op jit(solution)/shard_map/state/pallas_call | solution.py:472
  (106 shorter events, 27.0 us)
Async XLA Ops:
  0.0 26.9 %collective-permute-start = (bf16[16,128,256]{2,1,0:T(8,128)(2,1)}, bf16[16,128,256]{2,1,0:T(8,128)(2,1)S(1)}, u32[]{:S(2)}, u32[]{:S(2)}) collective-permute-start(bf16[16,128,256]{2,1,0:T(8,128)(2,1)} %refs_0_.1), channel_id=1, source_target_pairs={{0,32},{16,48},{32,64},{48,80},{64,96},{80,112},{96,0},{112,16},{1... | collective-permute-start | bytes 3145736 | tf_op jit(solution)/shard_map/ppermute | solution.py:239
  1.6 26.1 %collective-permute-start.1 = (bf16[16,128,256]{2,1,0:T(8,128)(2,1)}, bf16[16,128,256]{2,1,0:T(8,128)(2,1)S(1)}, u32[]{:S(2)}, u32[]{:S(2)}) collective-permute-start(bf16[16,128,256]{2,1,0:T(8,128)(2,1)} %refs_0_.1), channel_id=1, source_target_pairs={{0,96},{16,112},{32,0},{48,16},{64,32},{80,48},{96,64},{112,80},{1... | collective-permute-start | bytes 3145736 | tf_op jit(solution)/shard_map/ppermute | solution.py:239
  3.8 41.7 %collective-permute-start.2 = (bf16[16,128,256]{2,1,0:T(8,128)(2,1)}, bf16[16,128,256]{2,1,0:T(8,128)(2,1)}, u32[]{:S(2)}, u32[]{:S(2)}) collective-permute-start(bf16[16,128,256]{2,1,0:T(8,128)(2,1)} %refs_0_.1), channel_id=1, source_target_pairs={{0,16},{16,0},{32,48},{48,32},{64,80},{80,64},{96,112},{112,96},{1... | collective-permute-start | bytes 3145736 | tf_op jit(solution)/shard_map/ppermute | solution.py:242
  10.3 11.4 %all-to-all-start = ((f32[16,1,132]{2,1,0:T(1,128)}), f32[16,1,132]{2,1,0:T(1,128)S(1)}, u32[]{:S(2)}, u32[]{:S(2)}) async-start(f32[16,1,132]{2,1,0:T(1,128)} %all_to_all.11), calls=%async_computation | async-start | bytes 32768 | tf_op jit(solution)/shard_map/all_to_all | solution.py:322
  27.7 13.7 %collective-permute-start.5 = (bf16[8,128,256]{2,1,0:T(8,128)(2,1)}, bf16[8,128,256]{2,1,0:T(8,128)(2,1)}, u32[]{:S(2)}, u32[]{:S(2)}) collective-permute-start(bf16[8,128,256]{2,1,0:T(8,128)(2,1)} %slice.105), channel_id=1, source_target_pairs={{0,32},{16,48},{32,64},{48,80},{64,96},{80,112},{96,0},{112,16},{1... | collective-permute-start | bytes 1572872 | tf_op jit(solution)/shard_map/ppermute | solution.py:239
  28.5 15.6 %collective-permute-start.6 = (bf16[8,128,256]{2,1,0:T(8,128)(2,1)}, bf16[8,128,256]{2,1,0:T(8,128)(2,1)}, u32[]{:S(2)}, u32[]{:S(2)}) collective-permute-start(bf16[8,128,256]{2,1,0:T(8,128)(2,1)} %slice.106), channel_id=1, source_target_pairs={{0,96},{16,112},{32,0},{48,16},{64,32},{80,48},{96,64},{112,80},{1... | collective-permute-start | bytes 1572872 | tf_op jit(solution)/shard_map/ppermute | solution.py:239
  31.4 15.4 %collective-permute-start.3 = (bf16[16,128,256]{2,1,0:T(8,128)(2,1)S(1)}, bf16[16,128,256]{2,1,0:T(8,128)(2,1)}, u32[]{:S(2)}, u32[]{:S(2)}) collective-permute-start(bf16[16,128,256]{2,1,0:T(8,128)(2,1)S(1)} %collective-permute-done.refs_1_), channel_id=1, source_target_pairs={{0,16},{16,0},{32,48},{48,32},{64,80},{80,64},{96,112},{112,96},{1... | collective-permute-start | bytes 3145736 | tf_op jit(solution)/shard_map/ppermute | solution.py:242
  33.2 13.6 %collective-permute-start.4 = (bf16[16,128,256]{2,1,0:T(8,128)(2,1)S(1)}, bf16[16,128,256]{2,1,0:T(8,128)(2,1)}, u32[]{:S(2)}, u32[]{:S(2)}) collective-permute-start(bf16[16,128,256]{2,1,0:T(8,128)(2,1)S(1)} %collective-permute-done.1.refs_2_), channel_id=1, source_target_pairs={{0,16},{16,0},{32,48},{48,32},{64,80},{80,64},{96,112},{112,96},{1... | collective-permute-start | bytes 3145736 | tf_op jit(solution)/shard_map/ppermute | solution.py:242
  34.3 10.9 %all-to-all-start.1 = ((f32[8,16,256]{2,1,0:T(8,128)}), f32[8,16,256]{2,1,0:T(8,128)S(1)}, u32[]{:S(2)}, u32[]{:S(2)}) async-start(f32[8,16,256]{2,1,0:T(8,128)} %broadcast_in_dim.75), calls=%async_computation.1 | async-start | bytes 262144 | tf_op jit(solution)/shard_map/all_to_all | solution.py:297
  41.4 4.6 %collective-permute-start.7 = (bf16[8,128,256]{2,1,0:T(8,128)(2,1)}, bf16[8,128,256]{2,1,0:T(8,128)(2,1)}, u32[]{:S(2)}, u32[]{:S(2)}) collective-permute-start(bf16[8,128,256]{2,1,0:T(8,128)(2,1)} %collective-permute-done.5.refs_6_), channel_id=1, source_target_pairs={{0,16},{16,0},{32,48},{48,32},{64,80},{80,64},{96,112},{112,96},{1... | collective-permute-start | bytes 1572872 | tf_op jit(solution)/shard_map/ppermute | solution.py:242
  44.2 2.6 %collective-permute-start.8 = (bf16[8,128,256]{2,1,0:T(8,128)(2,1)}, bf16[8,128,256]{2,1,0:T(8,128)(2,1)}, u32[]{:S(2)}, u32[]{:S(2)}) collective-permute-start(bf16[8,128,256]{2,1,0:T(8,128)(2,1)} %collective-permute-done.6.refs_7_), channel_id=1, source_target_pairs={{0,16},{16,0},{32,48},{48,32},{64,80},{80,64},{96,112},{112,96},{1... | collective-permute-start | bytes 1572872 | tf_op jit(solution)/shard_map/ppermute | solution.py:242
  52.6 8.8 %collective-permute-start.10 = (bf16[2,4,272,128]{3,2,1,0:T(8,128)(2,1)S(1)}, bf16[2,4,272,128]{3,2,1,0:T(8,128)(2,1)S(1)}, u32[]{:S(2)}, u32[]{:S(2)}) collective-permute-start(bf16[2,4,272,128]{3,2,1,0:T(8,128)(2,1)S(1)} %get-tuple-element.16), channel_id=1, source_target_pairs={{0,3},{1,0},{2,1},{3,2},{4,7},{5,4},{6,5},{7,6},{8,11},{9,8},{10,9... | collective-permute-start | bytes 1671176 | tf_op jit(solution)/shard_map/ppermute | solution.py:404
  54.9 9.9 %collective-permute-start.9 = (bf16[2,4,272,128]{3,2,1,0:T(8,128)(2,1)S(1)}, bf16[2,4,272,128]{3,2,1,0:T(8,128)(2,1)S(1)}, u32[]{:S(2)}, u32[]{:S(2)}) collective-permute-start(bf16[2,4,272,128]{3,2,1,0:T(8,128)(2,1)S(1)} %get-tuple-element.15), channel_id=1, source_target_pairs={{0,1},{1,2},{2,3},{3,0},{4,5},{5,6},{6,7},{7,4},{8,9},{9,10},{10,1... | collective-permute-start | bytes 1671176 | tf_op jit(solution)/shard_map/ppermute | solution.py:404
  58.6 14.7 %collective-permute-start.12 = (bf16[2,4,272,128]{3,2,1,0:T(8,128)(2,1)S(1)}, bf16[2,4,272,128]{3,2,1,0:T(8,128)(2,1)S(1)}, u32[]{:S(2)}, u32[]{:S(2)}) collective-permute-start(bf16[2,4,272,128]{3,2,1,0:T(8,128)(2,1)S(1)} %get-tuple-element.18), channel_id=1, source_target_pairs={{0,3},{1,0},{2,1},{3,2},{4,7},{5,4},{6,5},{7,6},{8,11},{9,8},{10,9... | collective-permute-start | bytes 1671176 | tf_op jit(solution)/shard_map/ppermute | solution.py:404
  61.1 12.2 %collective-permute-start.13 = (bf16[2,4,272,128]{3,2,1,0:T(8,128)(2,1)S(1)}, bf16[2,4,272,128]{3,2,1,0:T(8,128)(2,1)S(1)}, u32[]{:S(2)}, u32[]{:S(2)}) collective-permute-start(bf16[2,4,272,128]{3,2,1,0:T(8,128)(2,1)S(1)} %get-tuple-element.19), channel_id=1, source_target_pairs={{0,1},{1,2},{2,3},{3,0},{4,5},{5,6},{6,7},{7,4},{8,9},{9,10},{10,1... | collective-permute-start | bytes 1671176 | tf_op jit(solution)/shard_map/ppermute | solution.py:404
  67.5 10.0 %collective-permute-start.11 = (bf16[2,4,272,128]{3,2,1,0:T(8,128)(2,1)S(1)}, bf16[2,4,272,128]{3,2,1,0:T(8,128)(2,1)S(1)}, u32[]{:S(2)}, u32[]{:S(2)}) collective-permute-start(bf16[2,4,272,128]{3,2,1,0:T(8,128)(2,1)S(1)} %get-tuple-element.17), channel_id=1, source_target_pairs={{0,1},{1,2},{2,3},{3,0},{4,5},{5,6},{6,7},{7,4},{8,9},{9,10},{10,1... | collective-permute-start | bytes 1671176 | tf_op jit(solution)/shard_map/ppermute | solution.py:404
  67.6 9.9 %collective-permute-start.14 = (bf16[2,4,272,128]{3,2,1,0:T(8,128)(2,1)S(1)}, bf16[2,4,272,128]{3,2,1,0:T(8,128)(2,1)S(1)}, u32[]{:S(2)}, u32[]{:S(2)}) collective-permute-start(bf16[2,4,272,128]{3,2,1,0:T(8,128)(2,1)S(1)} %get-tuple-element.20), channel_id=1, source_target_pairs={{0,3},{1,0},{2,1},{3,2},{4,7},{5,4},{6,5},{7,6},{8,11},{9,8},{10,9... | collective-permute-start | bytes 1671176 | tf_op jit(solution)/shard_map/ppermute | solution.py:404
  78.6 7.1 %collective-permute-start.15 = (bf16[4,272,128]{2,1,0:T(8,128)(2,1)}, bf16[4,272,128]{2,1,0:T(8,128)(2,1)S(1)}, u32[]{:S(2)}, u32[]{:S(2)}) collective-permute-start(bf16[4,272,128]{2,1,0:T(8,128)(2,1)} %get-tuple-element.26), channel_id=1, source_target_pairs={{0,8},{1,9},{2,10},{3,11},{4,12},{5,13},{6,14},{7,15},{8,0},{9,1},... | collective-permute-start | bytes 835592 | tf_op jit(solution)/shard_map/ppermute | solution.py:423
  79.9 7.6 %collective-permute-start.16 = (bf16[4,272,128]{2,1,0:T(8,128)(2,1)S(1)}, bf16[4,272,128]{2,1,0:T(8,128)(2,1)S(1)}, u32[]{:S(2)}, u32[]{:S(2)}) collective-permute-start(bf16[4,272,128]{2,1,0:T(8,128)(2,1)S(1)} %get-tuple-element.30), channel_id=1, source_target_pairs={{0,4},{1,5},{2,6},{3,7},{4,8},{5,9},{6,10},{7,11},{8,12},{9,13},{1... | collective-permute-start | bytes 835592 | tf_op jit(solution)/shard_map/ppermute | solution.py:423
  81.8 7.2 %collective-permute-start.17 = (bf16[4,272,128]{2,1,0:T(8,128)(2,1)S(1)}, bf16[4,272,128]{2,1,0:T(8,128)(2,1)S(1)}, u32[]{:S(2)}, u32[]{:S(2)}) collective-permute-start(bf16[4,272,128]{2,1,0:T(8,128)(2,1)S(1)} %get-tuple-element.25), channel_id=1, source_target_pairs={{0,12},{1,13},{2,14},{3,15},{4,0},{5,1},{6,2},{7,3},{8,4},{9,5},{1... | collective-permute-start | bytes 835592 | tf_op jit(solution)/shard_map/ppermute | solution.py:423
  93.6 7.9 %collective-permute-start.18 = (bf16[2,272,128]{2,1,0:T(8,128)(2,1)S(1)}, bf16[2,272,128]{2,1,0:T(8,128)(2,1)S(1)}, u32[]{:S(2)}, u32[]{:S(2)}) collective-permute-start(bf16[2,272,128]{2,1,0:T(8,128)(2,1)S(1)} %get-tuple-element.21), channel_id=1, source_target_pairs={{1,2},{2,1},{3,4},{4,3},{5,6},{6,5},{7,8},{8,7},{9,10},{10,9},{11,... | collective-permute-start | bytes 417800 | tf_op jit(solution)/shard_map/ppermute | solution.py:443
  95.5 6.0 %collective-permute-start.19 = (bf16[2,272,128]{2,1,0:T(8,128)(2,1)S(1)}, bf16[2,272,128]{2,1,0:T(8,128)(2,1)S(1)}, u32[]{:S(2)}, u32[]{:S(2)}) collective-permute-start(bf16[2,272,128]{2,1,0:T(8,128)(2,1)S(1)} %get-tuple-element.22), channel_id=1, source_target_pairs={{0,1},{1,0},{2,3},{3,2},{4,5},{5,4},{6,7},{7,6},{8,9},{9,8},{10,11... | collective-permute-start | bytes 417800 | tf_op jit(solution)/shard_map/ppermute | solution.py:442
  101.7 11.4 %collective-permute-start.20 = (bf16[4,272,128]{2,1,0:T(8,128)(2,1)S(1)}, bf16[4,272,128]{2,1,0:T(8,128)(2,1)S(1)}, u32[]{:S(2)}, u32[]{:S(2)}) collective-permute-start(bf16[4,272,128]{2,1,0:T(8,128)(2,1)S(1)} %get-tuple-element.32), channel_id=1, source_target_pairs={{16,32},{32,16},{48,64},{64,48},{80,96},{96,80},{17,33},{33,17},{4... | collective-permute-start | bytes 835592 | tf_op jit(solution)/shard_map/ppermute | solution.py:449
  109.0 4.2 %collective-permute-start.21 = (bf16[4,272,128]{2,1,0:T(8,128)(2,1)S(1)}, bf16[4,272,128]{2,1,0:T(8,128)(2,1)S(1)}, u32[]{:S(2)}, u32[]{:S(2)}) collective-permute-start(bf16[4,272,128]{2,1,0:T(8,128)(2,1)S(1)} %get-tuple-element.31), channel_id=1, source_target_pairs={{0,16},{16,0},{32,48},{48,32},{64,80},{80,64},{96,112},{112,96},{1... | collective-permute-start | bytes 835592 | tf_op jit(solution)/shard_map/ppermute | solution.py:454
  (10 other events, 91.6 us)

commit v7 on v6

--- a/solution.py
+++ b/solution.py
@@ -163,9 +163,10 @@
     scale = 1.0 / (members - 1)
     drives, bounds, uppers, lowers = [], [], [], []
     for p in here:
-        total = parts[0][p].astype(f32)
+        at = p // 2 * 2 + (1 - odd[0] if p % 2 == 0 else odd[0])
+        total = parts[0][at].astype(f32)
         for part in parts[1:]:
-            total = total + part[p].astype(f32)
+            total = total + part[at].astype(f32)
         cov, drive = unpack(total)
         drives.append(drive * scale)
         system = eye + cov * scale
@@ -193,14 +194,10 @@
         corner, both, tail = (
             v.astype(bf16) for v in pack(root[1] + root[0] * eye, vector_rows(shift, half))
         )
-        row = p // 2
-        for flip in range(2):
-
-            @pl.when(odd[0] == flip)
-            def _(o_ref=outs[(p + 1 + flip) % 2], row=row, corner=corner, both=both, tail=tail):
-                o_ref[row, :half] = corner
-                o_ref[row, half:members] = both
-                o_ref[row, members:] = tail
+        o_ref, row = outs[p % 2], p // 2
+        o_ref[row, :half] = corner
+        o_ref[row, half:members] = both
+        o_ref[row, members:] = tail
 
 
 def state_kernel(places, mixing, mean_ref, pert_ref, w_ref, o_ref):
@@ -468,7 +465,7 @@
         jnp.where(local_row >= point_rows, jnp.where(y_first, 3, 2), local_row),
     )
     places = block * 4 + jnp.where(odd, 3 - local_col, local_col)
-    per = 4
+    per = 8
     result = pl.pallas_call(
         state_kernel,
         grid=(tiles // per,),
@@ -481,7 +478,7 @@
             vmem,
         ],
         out_specs=pl.BlockSpec((per, cells, members), lambda i: (i, 0, 0)),
-        compiler_params=pltpu.CompilerParams(vmem_limit_bytes=12 << 20),
+        compiler_params=pltpu.CompilerParams(vmem_limit_bytes=20 << 20),
         cost_estimate=pl.CostEstimate(
             flops=2 * 16 * 512 * 256 * 256, bytes_accessed=11 << 20, transcendentals=0
         ),

time: 121 us -> 123 us (1.017)
  the two profiles are of different devices: /device:TPU:25 before, /device:TPU:69 now
where the time goes in v7:
time: 123 us
  starting transfers between devices  54.6 us (44%)
  waiting for transfers between devices  32.9 us (27%)
  Pallas kernels  24.1 us (20%)
  local copies, waits for them, and re-layouts  5.48 us (4%)
  other arithmetic  4.81 us (4%)
    ppermute x1, starting transfers between devices, local(): lax.ppermute(jnp.where(y_first, top, bottom), 'lon', [(i, (i ^ 1) + (2 if...  15.3 us
    pallas_call x4, Pallas kernels, gram(): pl.pallas_call(functools.partial(gram_kernel, points, ranks, call, len(re...  12.3 us
    ppermute x5, starting transfers between devices, swap(): return lax.ppermute(x, 'lon', [(i, i ^ 1) for i in range(size)])  8.83 us
    ppermute x6, waiting for transfers between devices, send(): return lax.ppermute(block, axes, turn(0, k, chips))  8.77 us
    all_to_all x1, starting transfers between devices, local(): asked = lax.all_to_all(asked, 'lat', 0, 0, tiled=True)  6.89 us
    all_to_all x1, starting transfers between devices, local(): lax.all_to_all(jnp.broadcast_to(project, (lon_count, held, members)), 'lo...  6.5 us
    ppermute x6, starting transfers between devices, send(): return lax.ppermute(block, axes, turn(0, k, chips))  6.11 us
    ppermute x3, waiting for transfers between devices, local(): lax.ppermute(total(k).astype(bf16), axes, turn(1, k, chips))  5.27 us
  transfers between devices with their start and end apart: 24, of which 11 were waited for; matrix products, arithmetic and copies ran while one was open for 7% of the time, Pallas kernels for 8%

profile of v7, /device:TPU:69, one launch (start us, length us, event | category | flops | bytes accessed | tf_op | source)
XLA Modules:
  0.0 122.8 jit_solution(5858019483500873105)
XLA Ops:
  8.2 6.9 %all-to-all-start = ((f32[16,1,132]{2,1,0:T(1,128)}), f32[16,1,132]{2,1,0:T(1,128)S(1)}, u32[]{:S(2)}, u32[]{:S(2)}) async-start(f32[16,1,132]{2,1,0:T(1,128)} %all_to_all.11), calls=%async_computation | async-start | bytes 32768 | tf_op jit(solution)/shard_map/all_to_all | solution.py:319
  15.2 4.7 %all-to-all-done = f32[16,1,132]{2,1,0:T(1,128)S(1)} async-done(((f32[16,1,132]{2,1,0:T(1,128)}), f32[16,1,132]{2,1,0:T(1,128)S(1)}, u32[]{:S(2)}, u32[]{:S(2)}) %all-to-all-start) | async-done | bytes 8480 | tf_op jit(solution)/shard_map/all_to_all | solution.py:319
  19.9 4.3 %collective-permute-done.refs_1_ = bf16[16,128,256]{2,1,0:T(8,128)(2,1)S(1)} collective-permute-done((bf16[16,128,256]{2,1,0:T(8,128)(2,1)}, bf16[16,128,256]{2,1,0:T(8,128)(2,1)S(1)}, u32[]{:S(2)}, u32[]{:S(2)}) %collective-permute-start) | collective-permute-done | bytes 1048608 | tf_op jit(solution)/shard_map/ppermute | solution.py:236
  30.8 6.5 %all-to-all-start.1 = ((f32[8,16,256]{2,1,0:T(8,128)}), f32[8,16,256]{2,1,0:T(8,128)S(1)}, u32[]{:S(2)}, u32[]{:S(2)}) async-start(f32[8,16,256]{2,1,0:T(8,128)} %broadcast_in_dim.75), calls=%async_computation.1 | async-start | bytes 262144 | tf_op jit(solution)/shard_map/all_to_all | solution.py:294
  37.3 2.8 %collective-permute-start.7 = (bf16[8,128,256]{2,1,0:T(8,128)(2,1)}, bf16[8,128,256]{2,1,0:T(8,128)(2,1)}, u32[]{:S(2)}, u32[]{:S(2)}) collective-permute-start(bf16[8,128,256]{2,1,0:T(8,128)(2,1)} %collective-permute-done.5.refs_6_), channel_id=1, source_target_pairs={{0,16},{16,0},{32,48},{48,32},{64,80},{80,64},{96,112},{112,96},{1... | collective-permute-start | bytes 1572872 | tf_op jit(solution)/shard_map/ppermute | solution.py:239
  40.1 2.6 %collective-permute-start.8 = (bf16[8,128,256]{2,1,0:T(8,128)(2,1)}, bf16[8,128,256]{2,1,0:T(8,128)(2,1)}, u32[]{:S(2)}, u32[]{:S(2)}) collective-permute-start(bf16[8,128,256]{2,1,0:T(8,128)(2,1)} %collective-permute-done.6.refs_7_), channel_id=1, source_target_pairs={{0,16},{16,0},{32,48},{48,32},{64,80},{80,64},{96,112},{112,96},{1... | collective-permute-start | bytes 1572872 | tf_op jit(solution)/shard_map/ppermute | solution.py:239
  44.6 2.8 %join.1.y_ref = bf16[128,128,256]{2,1,0:T(8,128)(2,1)S(1)} custom-call(bf16[16,128,256]{2,1,0:T(8,128)(2,1)S(1)} %copy-done.2, bf16[16,128,256]{2,1,0:T(8,128)(2,1)S(1)} %collective-permute-done.refs_1_, bf16[16,128,256]{2,1,0:T(8,128)(2,1)S(1)} %collective-permute-done.1.refs_2_, bf16[16,128,256]{2,1,0:T(8,128)(2,1)} %collective-permute-done.2.refs_3_, ...), custom_call_target="tpu_custom_call" | custom-call | tf_op jit(solution)/shard_map/join/pallas_call | solution.py:390
  47.4 2.8 %gram.5 = (bf16[2,4,272,128]{3,2,1,0:T(8,128)(2,1)S(1)}, bf16[2,4,272,128]{3,2,1,0:T(8,128)(2,1)S(1)}) custom-call(s32[20,68]{1,0:T(8,128)S(1)} %pad_add_fusion.slots, f32[16,64]{1,0:T(8,128)S(1)} %get-tuple-element.48.wts, f32[16,4,4,128]{3,2,1,0:T(4,128)S(1)} %pad_maximum_fusion.2.drive_ref, bf16[128,128,256]{2,1,0:T(8,128)(2,1)S(1)} %join.1.y_ref), custom_call_target="tpu_custom_call" | custom-call | flops 1073741824 | bytes 4194304 | tf_op jit(solution)/shard_map/gram/pallas_call | solution.py:373
  51.7 3.0 %gram.7 = (bf16[2,4,272,128]{3,2,1,0:T(8,128)(2,1)S(1)}, bf16[2,4,272,128]{3,2,1,0:T(8,128)(2,1)S(1)}) custom-call(s32[20,68]{1,0:T(8,128)S(1)} %pad_add_fusion.slots, f32[16,64]{1,0:T(8,128)S(1)} %get-tuple-element.48.wts, f32[16,4,4,128]{3,2,1,0:T(4,128)S(1)} %pad_maximum_fusion.2.drive_ref, bf16[128,128,256]{2,1,0:T(8,128)(2,1)S(1)} %join.1.y_ref), custom_call_target="tpu_custom_call" | custom-call | flops 1073741824 | bytes 4194304 | tf_op jit(solution)/shard_map/gram/pallas_call | solution.py:373
  54.8 2.6 %collective-permute-start.13 = (bf16[2,4,272,128]{3,2,1,0:T(8,128)(2,1)S(1)}, bf16[2,4,272,128]{3,2,1,0:T(8,128)(2,1)S(1)}, u32[]{:S(2)}, u32[]{:S(2)}) collective-permute-start(bf16[2,4,272,128]{3,2,1,0:T(8,128)(2,1)S(1)} %get-tuple-element.19), channel_id=1, source_target_pairs={{0,1},{1,2},{2,3},{3,0},{4,5},{5,6},{6,7},{7,4},{8,9},{9,10},{10,1... | collective-permute-start | bytes 1671176 | tf_op jit(solution)/shard_map/ppermute | solution.py:401
  59.4 3.1 %gram.6 = (bf16[2,4,272,128]{3,2,1,0:T(8,128)(2,1)S(1)}, bf16[2,4,272,128]{3,2,1,0:T(8,128)(2,1)S(1)}) custom-call(s32[20,68]{1,0:T(8,128)S(1)} %pad_add_fusion.slots, f32[16,64]{1,0:T(8,128)S(1)} %get-tuple-element.48.wts, f32[16,4,4,128]{3,2,1,0:T(4,128)S(1)} %pad_maximum_fusion.2.drive_ref, bf16[128,128,256]{2,1,0:T(8,128)(2,1)S(1)} %join.1.y_ref, ...), custom_call_target="tpu_custom_call" | custom-call | flops 1073741824 | bytes 4194304 | tf_op jit(solution)/shard_map/gram/pallas_call | solution.py:373
  64.3 3.4 %gram.4 = bf16[4,4,272,128]{3,2,1,0:T(8,128)(2,1)S(1)} custom-call(s32[20,68]{1,0:T(8,128)S(1)} %pad_add_fusion.slots, f32[16,64]{1,0:T(8,128)S(1)} %get-tuple-element.48.wts, f32[16,4,4,128]{3,2,1,0:T(4,128)S(1)} %pad_maximum_fusion.2.drive_ref, bf16[128,128,256]{2,1,0:T(8,128)(2,1)S(1)} %join.1.y_ref), custom_call_target="tpu_custom_call" | custom-call | flops 1073741824 | bytes 4194304 | tf_op jit(solution)/shard_map/gram/pallas_call | solution.py:373
  67.8 3.5 %collective-permute-done.11 = bf16[2,4,272,128]{3,2,1,0:T(8,128)(2,1)S(1)} collective-permute-done((bf16[2,4,272,128]{3,2,1,0:T(8,128)(2,1)S(1)}, bf16[2,4,272,128]{3,2,1,0:T(8,128)(2,1)S(1)}, u32[]{:S(2)}, u32[]{:S(2)}) %collective-permute-start.11) | collective-permute-done | bytes 557088 | tf_op jit(solution)/shard_map/ppermute | solution.py:401
  71.3 3.3 %collective-permute-done.14 = bf16[2,4,272,128]{3,2,1,0:T(8,128)(2,1)S(1)} collective-permute-done((bf16[2,4,272,128]{3,2,1,0:T(8,128)(2,1)S(1)}, bf16[2,4,272,128]{3,2,1,0:T(8,128)(2,1)S(1)}, u32[]{:S(2)}, u32[]{:S(2)}) %collective-permute-start.14) | collective-permute-done | bytes 557088 | tf_op jit(solution)/shard_map/ppermute | solution.py:401
  75.8 2.2 %collective-permute-start.15 = (bf16[4,272,128]{2,1,0:T(8,128)(2,1)}, bf16[4,272,128]{2,1,0:T(8,128)(2,1)S(1)}, u32[]{:S(2)}, u32[]{:S(2)}) collective-permute-start(bf16[4,272,128]{2,1,0:T(8,128)(2,1)} %get-tuple-element.26), channel_id=1, source_target_pairs={{0,8},{1,9},{2,10},{3,11},{4,12},{5,13},{6,14},{7,15},{8,0},{9,1},... | collective-permute-start | bytes 835592 | tf_op jit(solution)/shard_map/ppermute | solution.py:420
  78.2 2.5 %collective-permute-start.17 = (bf16[4,272,128]{2,1,0:T(8,128)(2,1)S(1)}, bf16[4,272,128]{2,1,0:T(8,128)(2,1)S(1)}, u32[]{:S(2)}, u32[]{:S(2)}) collective-permute-start(bf16[4,272,128]{2,1,0:T(8,128)(2,1)S(1)} %get-tuple-element.25), channel_id=1, source_target_pairs={{0,12},{1,13},{2,14},{3,15},{4,0},{5,1},{6,2},{7,3},{8,4},{9,5},{1... | collective-permute-start | bytes 835592 | tf_op jit(solution)/shard_map/ppermute | solution.py:420
  80.7 2.3 %collective-permute-done.15.refs_1_ = bf16[4,272,128]{2,1,0:T(8,128)(2,1)S(1)} collective-permute-done((bf16[4,272,128]{2,1,0:T(8,128)(2,1)}, bf16[4,272,128]{2,1,0:T(8,128)(2,1)S(1)}, u32[]{:S(2)}, u32[]{:S(2)}) %collective-permute-start.15) | collective-permute-done | bytes 278560 | tf_op jit(solution)/shard_map/ppermute | solution.py:420
  83.0 3.0 %collective-permute-done.16.refs_2_ = bf16[4,272,128]{2,1,0:T(8,128)(2,1)S(1)} collective-permute-done((bf16[4,272,128]{2,1,0:T(8,128)(2,1)S(1)}, bf16[4,272,128]{2,1,0:T(8,128)(2,1)S(1)}, u32[]{:S(2)}, u32[]{:S(2)}) %collective-permute-start.16) | collective-permute-done | bytes 278560 | tf_op jit(solution)/shard_map/ppermute | solution.py:420
  86.0 3.9 %root.1 = (bf16[2,272,128]{2,1,0:T(8,128)(2,1)S(1)}, bf16[2,272,128]{2,1,0:T(8,128)(2,1)S(1)}) custom-call(s32[1]{0:T(128)} %bitcast.3.odd, f32[4,272,128]{2,1,0:T(8,128)S(1)} %get-tuple-element.29.refs_0_, bf16[4,272,128]{2,1,0:T(8,128)(2,1)S(1)} %collective-permute-done.15.refs_1_, bf16[4,272,128]{2,1,0:T(8,128)(2,1)S(1)} %collective-permute-done.16.refs_2_, ...), custom_call_target="tpu_custom_call" | custom-call | flops 1610612736 | bytes 2097152 | tf_op jit(solution)/shard_map/root/pallas_call | solution.py:426
  89.9 2.9 %collective-permute-start.18 = (bf16[2,272,128]{2,1,0:T(8,128)(2,1)S(1)}, bf16[2,272,128]{2,1,0:T(8,128)(2,1)S(1)}, u32[]{:S(2)}, u32[]{:S(2)}) collective-permute-start(bf16[2,272,128]{2,1,0:T(8,128)(2,1)S(1)} %get-tuple-element.21), channel_id=1, source_target_pairs={{1,2},{2,1},{3,4},{4,3},{5,6},{6,5},{7,8},{8,7},{9,10},{10,9},{11,... | collective-permute-start | bytes 417800 | tf_op jit(solution)/shard_map/ppermute | solution.py:440
  93.0 4.8 %collective-permute-done.18 = bf16[2,272,128]{2,1,0:T(8,128)(2,1)S(1)} collective-permute-done((bf16[2,272,128]{2,1,0:T(8,128)(2,1)S(1)}, bf16[2,272,128]{2,1,0:T(8,128)(2,1)S(1)}, u32[]{:S(2)}, u32[]{:S(2)}) %collective-permute-start.18) | collective-permute-done | bytes 139296 | tf_op jit(solution)/shard_map/ppermute | solution.py:440
  98.1 15.3 %collective-permute-start.20 = (bf16[4,272,128]{2,1,0:T(8,128)(2,1)S(1)}, bf16[4,272,128]{2,1,0:T(8,128)(2,1)S(1)}, u32[]{:S(2)}, u32[]{:S(2)}) collective-permute-start(bf16[4,272,128]{2,1,0:T(8,128)(2,1)S(1)} %get-tuple-element.32), channel_id=1, source_target_pairs={{16,32},{32,16},{48,64},{64,48},{80,96},{96,80},{17,33},{33,17},{4... | collective-permute-start | bytes 835592 | tf_op jit(solution)/shard_map/ppermute | solution.py:446
  113.5 4.0 %collective-permute-done.20 = bf16[4,272,128]{2,1,0:T(8,128)(2,1)S(1)} collective-permute-done((bf16[4,272,128]{2,1,0:T(8,128)(2,1)S(1)}, bf16[4,272,128]{2,1,0:T(8,128)(2,1)S(1)}, u32[]{:S(2)}, u32[]{:S(2)}) %collective-permute-start.20) | collective-permute-done | bytes 278560 | tf_op jit(solution)/shard_map/ppermute | solution.py:446
  117.7 5.1 %state.1 = bf16[16,512,256]{2,1,0:T(8,128)(2,1)} custom-call(s32[16,4]{1,0:T(8,128)S(1)} %fusion.9.places, f32[16,4]{1,0:T(8,128)S(1)} %bitcast.34, f32[16,1,512]{2,1,0:T(1,128)S(1)} %reshape.184.mean_ref, bf16[16,512,256]{2,1,0:T(8,128)(2,1)S(1)} %bitcast.33, bf16[16,272,128]{2,1,0:T(8,128)(2,1)S(1)} %constant_dynamic-update-slice_fusion.w_ref), custom_call_target="tpu_custom_call" | custom-call | flops 1073741824 | bytes 11534336 | tf_op jit(solution)/shard_map/state/pallas_call | solution.py:469
  (106 shorter events, 24.1 us)
Async XLA Ops:
  0.0 24.2 %collective-permute-start = (bf16[16,128,256]{2,1,0:T(8,128)(2,1)}, bf16[16,128,256]{2,1,0:T(8,128)(2,1)S(1)}, u32[]{:S(2)}, u32[]{:S(2)}) collective-permute-start(bf16[16,128,256]{2,1,0:T(8,128)(2,1)} %refs_0_.1), channel_id=1, source_target_pairs={{0,32},{16,48},{32,64},{48,80},{64,96},{80,112},{96,0},{112,16},{1... | collective-permute-start | bytes 3145736 | tf_op jit(solution)/shard_map/ppermute | solution.py:236
  1.3 25.1 %collective-permute-start.1 = (bf16[16,128,256]{2,1,0:T(8,128)(2,1)}, bf16[16,128,256]{2,1,0:T(8,128)(2,1)S(1)}, u32[]{:S(2)}, u32[]{:S(2)}) collective-permute-start(bf16[16,128,256]{2,1,0:T(8,128)(2,1)} %refs_0_.1), channel_id=1, source_target_pairs={{0,96},{16,112},{32,0},{48,16},{64,32},{80,48},{96,64},{112,80},{1... | collective-permute-start | bytes 3145736 | tf_op jit(solution)/shard_map/ppermute | solution.py:236
  1.5 42.0 %collective-permute-start.2 = (bf16[16,128,256]{2,1,0:T(8,128)(2,1)}, bf16[16,128,256]{2,1,0:T(8,128)(2,1)}, u32[]{:S(2)}, u32[]{:S(2)}) collective-permute-start(bf16[16,128,256]{2,1,0:T(8,128)(2,1)} %refs_0_.1), channel_id=1, source_target_pairs={{0,16},{16,0},{32,48},{48,32},{64,80},{80,64},{96,112},{112,96},{1... | collective-permute-start | bytes 3145736 | tf_op jit(solution)/shard_map/ppermute | solution.py:239
  8.2 11.7 %all-to-all-start = ((f32[16,1,132]{2,1,0:T(1,128)}), f32[16,1,132]{2,1,0:T(1,128)S(1)}, u32[]{:S(2)}, u32[]{:S(2)}) async-start(f32[16,1,132]{2,1,0:T(1,128)} %all_to_all.11), calls=%async_computation | async-start | bytes 32768 | tf_op jit(solution)/shard_map/all_to_all | solution.py:319
  25.1 12.2 %collective-permute-start.5 = (bf16[8,128,256]{2,1,0:T(8,128)(2,1)}, bf16[8,128,256]{2,1,0:T(8,128)(2,1)}, u32[]{:S(2)}, u32[]{:S(2)}) collective-permute-start(bf16[8,128,256]{2,1,0:T(8,128)(2,1)} %slice.105), channel_id=1, source_target_pairs={{0,32},{16,48},{32,64},{48,80},{64,96},{80,112},{96,0},{112,16},{1... | collective-permute-start | bytes 1572872 | tf_op jit(solution)/shard_map/ppermute | solution.py:236
  27.3 12.8 %collective-permute-start.6 = (bf16[8,128,256]{2,1,0:T(8,128)(2,1)}, bf16[8,128,256]{2,1,0:T(8,128)(2,1)}, u32[]{:S(2)}, u32[]{:S(2)}) collective-permute-start(bf16[8,128,256]{2,1,0:T(8,128)(2,1)} %slice.106), channel_id=1, source_target_pairs={{0,96},{16,112},{32,0},{48,16},{64,32},{80,48},{96,64},{112,80},{1... | collective-permute-start | bytes 1572872 | tf_op jit(solution)/shard_map/ppermute | solution.py:236
  27.6 17.0 %collective-permute-start.3 = (bf16[16,128,256]{2,1,0:T(8,128)(2,1)S(1)}, bf16[16,128,256]{2,1,0:T(8,128)(2,1)}, u32[]{:S(2)}, u32[]{:S(2)}) collective-permute-start(bf16[16,128,256]{2,1,0:T(8,128)(2,1)S(1)} %collective-permute-done.refs_1_), channel_id=1, source_target_pairs={{0,16},{16,0},{32,48},{48,32},{64,80},{80,64},{96,112},{112,96},{1... | collective-permute-start | bytes 3145736 | tf_op jit(solution)/shard_map/ppermute | solution.py:239
  29.7 14.8 %collective-permute-start.4 = (bf16[16,128,256]{2,1,0:T(8,128)(2,1)S(1)}, bf16[16,128,256]{2,1,0:T(8,128)(2,1)}, u32[]{:S(2)}, u32[]{:S(2)}) collective-permute-start(bf16[16,128,256]{2,1,0:T(8,128)(2,1)S(1)} %collective-permute-done.1.refs_2_), channel_id=1, source_target_pairs={{0,16},{16,0},{32,48},{48,32},{64,80},{80,64},{96,112},{112,96},{1... | collective-permute-start | bytes 3145736 | tf_op jit(solution)/shard_map/ppermute | solution.py:239
  30.8 12.3 %all-to-all-start.1 = ((f32[8,16,256]{2,1,0:T(8,128)}), f32[8,16,256]{2,1,0:T(8,128)S(1)}, u32[]{:S(2)}, u32[]{:S(2)}) async-start(f32[8,16,256]{2,1,0:T(8,128)} %broadcast_in_dim.75), calls=%async_computation.1 | async-start | bytes 262144 | tf_op jit(solution)/shard_map/all_to_all | solution.py:294
  37.3 6.2 %collective-permute-start.7 = (bf16[8,128,256]{2,1,0:T(8,128)(2,1)}, bf16[8,128,256]{2,1,0:T(8,128)(2,1)}, u32[]{:S(2)}, u32[]{:S(2)}) collective-permute-start(bf16[8,128,256]{2,1,0:T(8,128)(2,1)} %collective-permute-done.5.refs_6_), channel_id=1, source_target_pairs={{0,16},{16,0},{32,48},{48,32},{64,80},{80,64},{96,112},{112,96},{1... | collective-permute-start | bytes 1572872 | tf_op jit(solution)/shard_map/ppermute | solution.py:239
  40.1 4.5 %collective-permute-start.8 = (bf16[8,128,256]{2,1,0:T(8,128)(2,1)}, bf16[8,128,256]{2,1,0:T(8,128)(2,1)}, u32[]{:S(2)}, u32[]{:S(2)}) collective-permute-start(bf16[8,128,256]{2,1,0:T(8,128)(2,1)} %collective-permute-done.6.refs_7_), channel_id=1, source_target_pairs={{0,16},{16,0},{32,48},{48,32},{64,80},{80,64},{96,112},{112,96},{1... | collective-permute-start | bytes 1572872 | tf_op jit(solution)/shard_map/ppermute | solution.py:239
  50.1 8.7 %collective-permute-start.10 = (bf16[2,4,272,128]{3,2,1,0:T(8,128)(2,1)S(1)}, bf16[2,4,272,128]{3,2,1,0:T(8,128)(2,1)S(1)}, u32[]{:S(2)}, u32[]{:S(2)}) collective-permute-start(bf16[2,4,272,128]{3,2,1,0:T(8,128)(2,1)S(1)} %get-tuple-element.16), channel_id=1, source_target_pairs={{0,3},{1,0},{2,1},{3,2},{4,7},{5,4},{6,5},{7,6},{8,11},{9,8},{10,9... | collective-permute-start | bytes 1671176 | tf_op jit(solution)/shard_map/ppermute | solution.py:401
  50.7 8.7 %collective-permute-start.9 = (bf16[2,4,272,128]{3,2,1,0:T(8,128)(2,1)S(1)}, bf16[2,4,272,128]{3,2,1,0:T(8,128)(2,1)S(1)}, u32[]{:S(2)}, u32[]{:S(2)}) collective-permute-start(bf16[2,4,272,128]{3,2,1,0:T(8,128)(2,1)S(1)} %get-tuple-element.15), channel_id=1, source_target_pairs={{0,1},{1,2},{2,3},{3,0},{4,5},{5,6},{6,7},{7,4},{8,9},{9,10},{10,1... | collective-permute-start | bytes 1671176 | tf_op jit(solution)/shard_map/ppermute | solution.py:401
  54.7 13.1 %collective-permute-start.12 = (bf16[2,4,272,128]{3,2,1,0:T(8,128)(2,1)S(1)}, bf16[2,4,272,128]{3,2,1,0:T(8,128)(2,1)S(1)}, u32[]{:S(2)}, u32[]{:S(2)}) collective-permute-start(bf16[2,4,272,128]{3,2,1,0:T(8,128)(2,1)S(1)} %get-tuple-element.18), channel_id=1, source_target_pairs={{0,3},{1,0},{2,1},{3,2},{4,7},{5,4},{6,5},{7,6},{8,11},{9,8},{10,9... | collective-permute-start | bytes 1671176 | tf_op jit(solution)/shard_map/ppermute | solution.py:401
  54.8 13.0 %collective-permute-start.13 = (bf16[2,4,272,128]{3,2,1,0:T(8,128)(2,1)S(1)}, bf16[2,4,272,128]{3,2,1,0:T(8,128)(2,1)S(1)}, u32[]{:S(2)}, u32[]{:S(2)}) collective-permute-start(bf16[2,4,272,128]{3,2,1,0:T(8,128)(2,1)S(1)} %get-tuple-element.19), channel_id=1, source_target_pairs={{0,1},{1,2},{2,3},{3,0},{4,5},{5,6},{6,7},{7,4},{8,9},{9,10},{10,1... | collective-permute-start | bytes 1671176 | tf_op jit(solution)/shard_map/ppermute | solution.py:401
  62.5 8.8 %collective-permute-start.11 = (bf16[2,4,272,128]{3,2,1,0:T(8,128)(2,1)S(1)}, bf16[2,4,272,128]{3,2,1,0:T(8,128)(2,1)S(1)}, u32[]{:S(2)}, u32[]{:S(2)}) collective-permute-start(bf16[2,4,272,128]{3,2,1,0:T(8,128)(2,1)S(1)} %get-tuple-element.17), channel_id=1, source_target_pairs={{0,1},{1,2},{2,3},{3,0},{4,5},{5,6},{6,7},{7,4},{8,9},{9,10},{10,1... | collective-permute-start | bytes 1671176 | tf_op jit(solution)/shard_map/ppermute | solution.py:401
  64.3 10.3 %collective-permute-start.14 = (bf16[2,4,272,128]{3,2,1,0:T(8,128)(2,1)S(1)}, bf16[2,4,272,128]{3,2,1,0:T(8,128)(2,1)S(1)}, u32[]{:S(2)}, u32[]{:S(2)}) collective-permute-start(bf16[2,4,272,128]{3,2,1,0:T(8,128)(2,1)S(1)} %get-tuple-element.20), channel_id=1, source_target_pairs={{0,3},{1,0},{2,1},{3,2},{4,7},{5,4},{6,5},{7,6},{8,11},{9,8},{10,9... | collective-permute-start | bytes 1671176 | tf_op jit(solution)/shard_map/ppermute | solution.py:401
  75.8 7.2 %collective-permute-start.15 = (bf16[4,272,128]{2,1,0:T(8,128)(2,1)}, bf16[4,272,128]{2,1,0:T(8,128)(2,1)S(1)}, u32[]{:S(2)}, u32[]{:S(2)}) collective-permute-start(bf16[4,272,128]{2,1,0:T(8,128)(2,1)} %get-tuple-element.26), channel_id=1, source_target_pairs={{0,8},{1,9},{2,10},{3,11},{4,12},{5,13},{6,14},{7,15},{8,0},{9,1},... | collective-permute-start | bytes 835592 | tf_op jit(solution)/shard_map/ppermute | solution.py:420
  78.0 8.0 %collective-permute-start.16 = (bf16[4,272,128]{2,1,0:T(8,128)(2,1)S(1)}, bf16[4,272,128]{2,1,0:T(8,128)(2,1)S(1)}, u32[]{:S(2)}, u32[]{:S(2)}) collective-permute-start(bf16[4,272,128]{2,1,0:T(8,128)(2,1)S(1)} %get-tuple-element.30), channel_id=1, source_target_pairs={{0,4},{1,5},{2,6},{3,7},{4,8},{5,9},{6,10},{7,11},{8,12},{9,13},{1... | collective-permute-start | bytes 835592 | tf_op jit(solution)/shard_map/ppermute | solution.py:420
  78.2 7.8 %collective-permute-start.17 = (bf16[4,272,128]{2,1,0:T(8,128)(2,1)S(1)}, bf16[4,272,128]{2,1,0:T(8,128)(2,1)S(1)}, u32[]{:S(2)}, u32[]{:S(2)}) collective-permute-start(bf16[4,272,128]{2,1,0:T(8,128)(2,1)S(1)} %get-tuple-element.25), channel_id=1, source_target_pairs={{0,12},{1,13},{2,14},{3,15},{4,0},{5,1},{6,2},{7,3},{8,4},{9,5},{1... | collective-permute-start | bytes 835592 | tf_op jit(solution)/shard_map/ppermute | solution.py:420
  89.9 7.9 %collective-permute-start.18 = (bf16[2,272,128]{2,1,0:T(8,128)(2,1)S(1)}, bf16[2,272,128]{2,1,0:T(8,128)(2,1)S(1)}, u32[]{:S(2)}, u32[]{:S(2)}) collective-permute-start(bf16[2,272,128]{2,1,0:T(8,128)(2,1)S(1)} %get-tuple-element.21), channel_id=1, source_target_pairs={{1,2},{2,1},{3,4},{4,3},{5,6},{6,5},{7,8},{8,7},{9,10},{10,9},{11,... | collective-permute-start | bytes 417800 | tf_op jit(solution)/shard_map/ppermute | solution.py:440
  92.9 5.0 %collective-permute-start.19 = (bf16[2,272,128]{2,1,0:T(8,128)(2,1)S(1)}, bf16[2,272,128]{2,1,0:T(8,128)(2,1)S(1)}, u32[]{:S(2)}, u32[]{:S(2)}) collective-permute-start(bf16[2,272,128]{2,1,0:T(8,128)(2,1)S(1)} %get-tuple-element.22), channel_id=1, source_target_pairs={{0,1},{1,0},{2,3},{3,2},{4,5},{5,4},{6,7},{7,6},{8,9},{9,8},{10,11... | collective-permute-start | bytes 417800 | tf_op jit(solution)/shard_map/ppermute | solution.py:439
  98.1 19.5 %collective-permute-start.20 = (bf16[4,272,128]{2,1,0:T(8,128)(2,1)S(1)}, bf16[4,272,128]{2,1,0:T(8,128)(2,1)S(1)}, u32[]{:S(2)}, u32[]{:S(2)}) collective-permute-start(bf16[4,272,128]{2,1,0:T(8,128)(2,1)S(1)} %get-tuple-element.32), channel_id=1, source_target_pairs={{16,32},{32,16},{48,64},{64,48},{80,96},{96,80},{17,33},{33,17},{4... | collective-permute-start | bytes 835592 | tf_op jit(solution)/shard_map/ppermute | solution.py:446
  113.4 4.2 %collective-permute-start.21 = (bf16[4,272,128]{2,1,0:T(8,128)(2,1)S(1)}, bf16[4,272,128]{2,1,0:T(8,128)(2,1)S(1)}, u32[]{:S(2)}, u32[]{:S(2)}) collective-permute-start(bf16[4,272,128]{2,1,0:T(8,128)(2,1)S(1)} %get-tuple-element.31), channel_id=1, source_target_pairs={{0,16},{16,0},{32,48},{48,32},{64,80},{80,64},{96,112},{112,96},{1... | collective-permute-start | bytes 835592 | tf_op jit(solution)/shard_map/ppermute | solution.py:451
  (10 other events, 107.6 us)
